TPU v7x, 32 devices: a whole 2x2x4 slice. The times are simulated.
32 devices in a mesh: grp: 2 (over y), row: 4 (over z), ch: 4 (over x, core).
Axes of the slice: x: 2, y: 2, z: 4, core: 2. Of those that a mesh axis runs over, the one named last changes fastest.
Arguments:
- pair: bfloat16 [112, 56, 128], P(('grp', 'row')), parts along dimension 0, may hold values from -6 to 6
- chain_ids: int32 [112], P('grp'), parts along dimension 0, may hold values from 0 to 5, never falling along the last dimension, each value on 1 to 18 neighbouring positions
- mask: int32 [112, 56], P(('grp', 'row')), parts along dimension 0, may hold values 0 or 1
- pair_embed: float32 [2, 128], replicated, may hold values from -6 to 6
- in_gain: float32 [2, 128], replicated, may hold values from 0.5 to 1.5
- in_bias: float32 [2, 128], replicated, may hold values from -3 to 3
- proj_weight: bfloat16 [2, 4, 128, 128], P(None, None, None, 'ch'), may hold values from -0.5 to 0.5
- gate_weight: bfloat16 [2, 128, 128], replicated, may hold values from -0.5 to 0.5
- out_gain: float32 [2, 128], replicated, may hold values from 0.5 to 1.5
- out_bias: float32 [2, 128], replicated, may hold values from -3 to 3
- out_weight: bfloat16 [2, 128, 128], replicated, may hold values from -0.5 to 0.5
Outputs:
- pair_out: bfloat16 [112, 56, 128], P(('grp', 'row')), parts along dimension 0
There are 2 independent parts, one for each index of `grp`. A program takes and returns all parts, laid end to end along the dimension named above; an argument that names none is the same for every part. Nothing has to cross between parts.
Inputs may be any that keep to these rules, and one draw needn't show every extreme that they name: `chain_ids`: chain numbers never fall along the residues; each chain has 1 to 18 residues.
All inputs are finite; a program needn't handle non-finite values. No bound on the sum of `mask` on one device may be relied on, other than what follows from the above.
Results may differ from a plain program's by a relative error of at most 0.008.
Values may be sent and summed in bfloat16 or wider, within the bound.
No kernel may reach another device: no remote copies, remote signals or barrier semaphores. Data moves between devices by JAX's collectives and lax.ppermute only.
A program may use at most 128 MiB of HBM per device.

v0:
```python
import jax
import jax.numpy as jnp
from jax import lax
from jax.sharding import PartitionSpec as P

EPS = 1e-05


def layer_norm(values, gain, bias):
    mean = jnp.mean(values, axis=-1, keepdims=True)
    centered = values - mean
    var = jnp.mean(centered * centered, axis=-1, keepdims=True)
    return centered * lax.rsqrt(var + EPS) * gain + bias


def gated(normed, weights, maskf, form):
    proj = jnp.einsum(form, normed, weights, preferred_element_type=jnp.float32)
    return (jax.nn.sigmoid(proj[0]) * proj[1] * maskf).astype(jnp.bfloat16)


def outgoing(normed, weights, maskf):
    left = gated(normed, weights[0:2], maskf, "rnc,qch->qhrn")
    right = gated(normed, weights[2:4], maskf, "rnc,qch->qhrn")
    return jnp.einsum(
        "hik,hjk->hij",
        left,
        lax.all_gather(right, "row", axis=1, tiled=True),
        preferred_element_type=jnp.float32,
    ).astype(jnp.bfloat16)


def incoming(normed, weights, maskf):
    right = gated(normed, weights[2:4], maskf, "rnc,qch->qhrn")
    left = gated(normed, weights[0:2], maskf, "rnc,qch->qhrn")
    summed = jnp.transpose(
        lax.psum_scatter(
            jnp.einsum("hki,hkj->ihj", left, right, preferred_element_type=jnp.float32),
            "row",
            scatter_dimension=0,
            tiled=True,
        ),
        (1, 0, 2),
    )
    return summed.astype(jnp.bfloat16)


def finish(mixed, layer, out_gain, out_bias, out_weight):
    hid_full = out_weight.shape[1]
    whole = lax.all_gather(mixed, "ch", axis=0, tiled=True)
    values = whole.astype(jnp.float32)
    mean = jnp.sum(values, axis=0) / hid_full
    meansq = jnp.sum(values * values, axis=0) / hid_full
    gain = out_gain[layer]
    bias = out_bias[layer]
    weight = out_weight[layer]
    scale = lax.rsqrt(meansq - mean * mean + EPS)
    hidden = ((values - mean) * scale * gain[:, None, None] + bias[:, None, None]).astype(
        jnp.bfloat16
    )
    update = jnp.einsum("hrn,hc->rnc", hidden, weight, preferred_element_type=jnp.float32)
    return update


def per_device(
    pair,
    chain_ids,
    mask,
    pair_embed,
    in_gain,
    in_bias,
    proj_weight,
    gate_weight,
    out_gain,
    out_bias,
    out_weight,
):
    rows = pair.shape[0]
    start_row = lax.axis_index("row") * rows
    own_chain = lax.dynamic_slice_in_dim(chain_ids, start_row, rows, 0)
    same = (own_chain[:, None] == chain_ids[None, :])[:, :, None]
    current = pair.astype(jnp.float32) + jnp.where(same, pair_embed[1], pair_embed[0])
    maskf = mask.astype(jnp.float32)
    result = pair
    for layer in range(2):
        normed = layer_norm(current, in_gain[layer], in_bias[layer]).astype(jnp.bfloat16)
        weights = proj_weight[layer]
        if layer == 0:
            mixed = outgoing(normed, weights, maskf)
        else:
            mixed = incoming(normed, weights, maskf)
        update = finish(mixed, layer, out_gain, out_bias, out_weight)
        gate = jax.nn.sigmoid(
            jnp.dot(normed, gate_weight[layer], preferred_element_type=jnp.float32)
        )
        result = lax.optimization_barrier((current + gate * update).astype(jnp.bfloat16))
        current = result.astype(jnp.float32)
    return result


def solution(mesh):
    placed = (
        P(("grp", "row"), None, None),
        P("grp"),
        P(("grp", "row"), None),
        P(),
        P(),
        P(),
        P(None, None, None, "ch"),
        P(),
        P(),
        P(),
        P(),
    )
    return jax.shard_map(
        per_device,
        mesh=mesh,
        in_specs=placed,
        out_specs=P(("grp", "row"), None, None),
        check_vma=False,
    )
```

profile of v0, /device:TPU:0, one launch (start us, length us, event | category | flops | bytes accessed | tf_op | source)
XLA Modules:
  0.0 85.7 jit_solution(2961048530940178231)
XLA Ops:
  6.5 0.8 dynamic_slice.3
  7.3 0.7 broadcast_compare_fusion
  8.0 0.8 slice_bitcast_fusion.10
  8.8 1.3 %fusion.35 = f32[14,56]{1,0:T(8,128)S(1)} fusion(bf16[14,56,128]{2,1,0:T(8,128)(2,1)} %param.11, f32[128]{0:T(128)S(1)} %get-tuple-element.26, f32[128]{0:T(128)S(1)} %get-tuple-element.25, pred[14,56]{1,0:T(8,128)(4,1)S(1)} %broadcast_compare_fusion), kind=kLoop, calls=%fused_computation.54 | loop fusion | flops 400624 | bytes 205648 | tf_op jit(solution)/shard_map/reduce_sum | solution.py:10
  10.1 0.4 multiply_reduce_fusion
  10.5 0.6 copy-done.4
  11.2 0.6 convolution_bitcast_fusion.3
  11.8 0.6 convolution_bitcast_fusion.4
  12.6 16.8 %all_gather.9 = bf16[32,56,56]{2,0,1:T(8,128)(2,1)S(1)} all-gather(bf16[32,14,56]{2,0,1:T(8,128)(2,1)S(1)} %get-tuple-element.16), channel_id=1, replica_groups=mesh['grp'=2,'row'=4,'ch'=4] {'row'}, dimensions={1}, use_global_device_ids=true | all-gather | bytes 250880 | tf_op jit(solution)/shard_map/all_gather | solution.py:27
  29.4 0.4 convolution_convert_fusion
  29.8 6.8 %all_gather.10 = bf16[128,14,56]{2,0,1:T(8,128)(2,1)S(1)} all-gather(bf16[32,14,56]{2,0,1:T(8,128)(2,1)S(1)} %copy.70), channel_id=1, replica_groups=mesh['grp'=2,'row'=4,'ch'=4] {'ch'}, dimensions={0}, use_global_device_ids=true | all-gather | bytes 250880 | tf_op jit(solution)/shard_map/all_gather | solution.py:49
  36.9 0.6 copy-done.6
  37.5 0.4 fusion.18
  37.9 0.4 copy-done.8
  38.4 0.8 fusion.9
  39.7 0.5 convolution_bitcast_fusion.1
  40.2 0.5 convolution_bitcast_fusion.2
  40.8 0.5 convolution_bitcast_fusion
  41.2 1.6 %copy.76 = f32[56,32,56]{2,1,0:T(8,128)} copy(f32[56,32,56]{0,2,1:T(8,128)S(1)} %convolution_bitcast_fusion) | data formatting | bytes 802816 | tf_op jit(solution)/shard_map/hki,hkj->ihj/transpose | solution.py:37
  42.9 0.4 fusion.2
  43.3 26.1 %reduce-scatter.2.cloned.1.call-done = f32[14,32,56]{2,1,0:T(8,128)} async-done(((f32[56,32,56]{2,1,0:T(8,128)}), f32[14,32,56]{2,1,0:T(8,128)}) %reduce-scatter.2.cloned.1.call-update) | async-done | bytes 100368 | tf_op jit(solution)/shard_map/reduce_scatter | solution.py:36
  69.5 1.0 %convert_bitcast_fusion = bf16[32,14,56]{2,0,1:T(8,128)(2,1)S(1)} fusion(f32[14,32,56]{2,1,0:T(8,128)} %reduce-scatter.2.cloned.1.call-done), kind=kLoop, calls=%fused_computation.100 | loop fusion | flops 25088 | bytes 150528 | tf_op jit(solution)/shard_map/convert_element_type | solution.py:44
  70.4 6.8 %all_gather.11 = bf16[128,14,56]{2,0,1:T(8,128)(2,1)S(1)} all-gather(bf16[32,14,56]{2,0,1:T(8,128)(2,1)S(1)} %convert_bitcast_fusion), channel_id=1, replica_groups=mesh['grp'=2,'row'=4,'ch'=4] {'ch'}, dimensions={0}, use_global_device_ids=true | all-gather | bytes 250880 | tf_op jit(solution)/shard_map/all_gather | solution.py:49
  77.7 1.1 %fusion.10 = bf16[14,56,128]{2,1,0:T(8,128)(2,1)} fusion(f32[14,56,128]{2,1,0:T(8,128)S(1)} %fusion.2, bf16[14,56,128]{2,1,0:T(8,128)(2,1)S(1)} %fusion.9, bf16[128,14,56]{0,2,1:T(8,128)(2,1)S(1)} %copy.77, f32[128]{0:T(128)S(1)} %get-tuple-element.19, f32[128]{0:T(128)S(1)} %get-tuple-element.30, f32[14,56]{1,0:T(8,128)S(1)} %get-tuple-element.10, ...), kind=kOutput, calls=%fused_computation.21 | convolution fusion | flops 26693632 | bytes 1053696 | tf_op jit(solution)/shard_map/hrn,hc->rnc/dot_general | solution.py:60
  (34 shorter events, 1.8 us)
Async XLA Ops:
  6.5 3.5 %copy-start = (bf16[14,56,128]{2,1,0:T(8,128)(2,1)S(1)}, bf16[14,56,128]{2,1,0:T(8,128)(2,1)}, u32[]{:S(2)}) copy-start(bf16[14,56,128]{2,1,0:T(8,128)(2,1)} %param.11) | copy-start | bytes 602116
  6.5 62.9 %reduce-scatter.2.cloned.1.call-start = ((), (), s32[]{:S(2)}) async-start(), calls=%async_computation.1 | async-start | bytes 1146880 | tf_op jit(solution)/shard_map/reduce_scatter | solution.py:36
  10.1 1.1 %copy-start.1 = (bf16[2,4,128,32]{2,3,1,0:T(8,128)(2,1)S(1)}, bf16[2,4,128,32]{2,3,1,0:T(8,128)(2,1)}, u32[]{:S(2)}) copy-start(bf16[2,4,128,32]{2,3,1,0:T(8,128)(2,1)} %param.17) | copy-start | bytes 196612
  10.5 0.7 copy-start.4
  10.5 0.7 copy-start.5
  11.8 0.7 copy-start.3
  36.6 0.9 %copy-start.2 = (bf16[2,128,128]{2,1,0:T(8,128)(2,1)S(1)}, bf16[2,128,128]{2,1,0:T(8,128)(2,1)}, u32[]{:S(2)}) copy-start(bf16[2,128,128]{2,1,0:T(8,128)(2,1)} %param.21) | copy-start | bytes 196612
  36.8 0.7 copy-start.6
  36.8 0.7 copy-start.7
  37.5 0.8 copy-start.8
Sparse Core Ops, SparseCore 0:
  43.0 26.4 reduce-scatter.1
where the time goes:
time: 86.1 us; the launch traced here: 85.7 us
  blocking collectives  30.4 us (35%)
  waiting for transfers between devices  26.2 us (30%)
  between operations  13.6 us (16%)
  matrix products  5.57 us (6%)
  local copies, waits for them, and re-layouts  5.31 us (6%)
  other arithmetic  4.68 us (5%)
    reduce_scatter x1, waiting for transfers between devices, incoming(): lax.psum_scatter(jnp.einsum('hki,hkj->ihj', left, right, preferred_elemen...  26.1 us
    all_gather x1, blocking collectives, outgoing(): lax.all_gather(right, 'row', axis=1, tiled=True)  16.8 us
    all_gather x2, blocking collectives, finish(): whole = lax.all_gather(mixed, 'ch', axis=0, tiled=True)  13.6 us
    dot_general x4, matrix products, gated(): proj = jnp.einsum(form, normed, weights, preferred_element_type=jnp.float32)  2.07 us
    unnamed x18, local copies, waits for them, and re-layouts  1.92 us
  transfers between devices with their start and end apart: 1, of which 1 were waited for; matrix products, arithmetic and copies ran while one was open for 0% of the time, Pallas kernels for 0%

commit v1 on v0

--- a/solution.py
+++ b/solution.py
@@ -1,9 +1,270 @@
+import functools
+
 import jax
 import jax.numpy as jnp
 from jax import lax
+from jax.experimental import pallas as pl
+from jax.experimental.pallas import tpu as pltpu
 from jax.sharding import PartitionSpec as P
 
 EPS = 1e-05
+F32 = jnp.float32
+BF16 = jnp.bfloat16
+MASK_ROWS = 16
+
+
+def nt_dot(a, b):
+    return lax.dot_general(a, b, (((1,), (1,)), ((), ())), preferred_element_type=F32)
+
+
+def nn_dot(a, b):
+    return lax.dot_general(a, b, (((1,), (0,)), ((), ())), preferred_element_type=F32)
+
+
+def half_sigmoid(half):
+    return 0.5 * jnp.tanh(half) + 0.5
+
+
+def normalize(values, gain, bias):
+    mean = jnp.mean(values, axis=-1, keepdims=True)
+    centered = values - mean
+    var = jnp.mean(centered * centered, axis=-1, keepdims=True)
+    return (centered * lax.rsqrt(var + EPS) * gain + bias).astype(BF16)
+
+
+def pieces(rows, most):
+    out, first = [], 0
+    while first < rows:
+        count = min(most, rows - first)
+        out.append((first, count))
+        first += count
+    return out
+
+
+def pack_kernel(n, rows, half, pair, mask, weights, packed, halved):
+    core = lax.rem(lax.axis_index("ch"), 2)
+    block = rows * n
+    chan = pair.shape[1]
+    masks = jnp.concatenate([mask[...].astype(F32), jnp.zeros((rows, chan - n), F32)], axis=1)
+    masks = jnp.concatenate([masks, jnp.zeros((MASK_ROWS - rows, chan), F32)], axis=0).astype(BF16)
+    size = weights.shape[0]
+    packed[0:block, :] = pair[...]
+    packed[block : block + size, :] = weights[...]
+    packed[block + size : block + size + MASK_ROWS, :] = masks
+    start = pl.multiple_of(core * (rows - half) * n, 16)
+    halved[0 : half * n, :] = pair[pl.ds(start, half * n), :]
+    halved[half * n : half * n + MASK_ROWS, :] = masks
+
+
+def whole_kernel(
+    n,
+    rows,
+    half,
+    packed_o, packed_a, packed_e, half_b, half_f, w_e,
+    chain_s, chain_v, embed, in_gain, in_bias, gate_w, out_gain, out_bias, out_w,
+    result,
+    z_ref, zn_ref, zm_ref, mask_ref, left_ref, right_ref, x_ref, w_ref,
+):
+    r = lax.axis_index("row")
+    c = lax.axis_index("ch")
+    core = lax.rem(c, 2)
+    block = rows * n
+    chan = packed_o.shape[1]
+    size = w_e.shape[0]
+    hid = size // 8
+    masks_at = block + size
+
+    def put_weights(ref, at, position):
+        for u in range(2):
+            for q in range(4):
+                first = at + (u * 4 + q) * hid
+                w_ref[u, q, position] = ref[first : first + hid, :] * jnp.asarray(0.5, BF16)
+
+    put_weights(packed_o, block, c)
+    put_weights(w_e, 0, c ^ 1)
+    put_weights(packed_a, block, c ^ 2)
+    put_weights(packed_e, block, c ^ 3)
+
+    chains = jnp.broadcast_to(chain_v[...], (n, chan))
+    gain0, bias0 = in_gain[0:1, :], in_bias[0:1, :]
+    other, same = embed[0:1, :], embed[1:2, :]
+
+    spread = (
+        lax.broadcasted_iota(jnp.int32, (MASK_ROWS, rows * chan), 1) // chan
+        == lax.broadcasted_iota(jnp.int32, (MASK_ROWS, rows * chan), 0)
+    ).astype(BF16)
+
+    def load_rows(pair, pair_at, position, first, count, masks):
+        z = jnp.concatenate(
+            [
+                jnp.where(chains == chain_s[position * rows + i], same, other)
+                for i in range(first, first + count)
+            ],
+            axis=0,
+        ) + pair[pair_at : pair_at + count * n, :].astype(F32)
+        zn = normalize(z, gain0, bias0)
+        spread_mask = jnp.concatenate(
+            [masks[:, i * chan : (i + 1) * chan] for i in range(first, first + count)], axis=0
+        ).astype(BF16)
+        at = pl.ds(pl.multiple_of(position * block + first * n, 16), count * n)
+        z_ref[at, :] = z
+        zn_ref[at, :] = zn
+        mask_ref[at, :] = spread_mask
+        zm_ref[at, :] = zn * spread_mask
+
+    def spread_masks(ref, at):
+        masks = ref[at : at + MASK_ROWS, 0:n]
+        return lax.dot_general(masks, spread, (((0,), (0,)), ((), ())), preferred_element_type=F32)
+
+    def load_block(ref, position):
+        masks = spread_masks(ref, masks_at)
+        for first, count in pieces(rows, 8):
+            load_rows(ref, first * n, position, first, count, masks)
+
+    load_block(packed_o, r)
+    load_block(packed_a, r ^ (1 + core))
+    load_block(packed_e, r ^ (2 - core))
+    masks = spread_masks(half_b, half * n)
+    rest = rows - half
+
+    @pl.when(core == 0)
+    def _():
+        load_rows(half_b, 0, r ^ 3, 0, half, masks)
+        load_rows(half_f, (half - rest) * n, r ^ 3, half, rest, masks)
+
+    @pl.when(core == 1)
+    def _():
+        load_rows(half_f, 0, r ^ 3, 0, half, masks)
+        load_rows(half_b, (half - rest) * n, r ^ 3, half, rest, masks)
+
+    many = 8
+
+    def project(u, transposed_right):
+        weights = [w_ref[u, q].reshape(4 * hid, chan) for q in range(4)]
+
+        def some(t, _):
+            at = pl.ds(pl.multiple_of(t * many * n, 16), many * n)
+            zm = zm_ref[at, :]
+            left_ref[at, :] = (jnp.tanh(nt_dot(zm, weights[0])) + 1.0) * nt_dot(zm, weights[1])
+            right = (jnp.tanh(nt_dot(zm, weights[2])) + 1.0) * nt_dot(zm, weights[3])
+            if transposed_right:
+                for k in range(many):
+                    right_ref[pl.ds(many * t + k, n, stride=n), :] = right[k * n : (k + 1) * n]
+            else:
+                right_ref[at, :] = right
+            return 0
+
+        lax.fori_loop(0, n // many, some, 0)
+
+    def triangle(count, left_at, step, out_at):
+        def body(k, accs):
+            right = right_ref[pl.ds(pl.multiple_of(k * n, 8), n), :]
+            return tuple(
+                acc + left_ref[pl.ds(left_at(i) + k * step, 1), :] * right for i, acc in enumerate(accs)
+            )
+
+        accs = lax.fori_loop(0, n, body, tuple(jnp.zeros((n, chan), F32) for _ in range(count)), unroll=8)
+        for i, acc in enumerate(accs):
+            x_ref[pl.ds(pl.multiple_of(out_at + i * n, 8), n), :] = acc
+
+    def finish(u, x_at, z_at, size):
+        x = x_ref[pl.ds(x_at, size), :]
+        mean = jnp.mean(x, axis=-1, keepdims=True)
+        meansq = jnp.mean(x * x, axis=-1, keepdims=True)
+        scale = lax.rsqrt(meansq - mean * mean + EPS)
+        hidden = ((x - mean) * scale * out_gain[u : u + 1, :] + out_bias[u : u + 1, :]).astype(BF16)
+        update = nn_dot(hidden, out_w[u])
+        gate = jax.nn.sigmoid(nn_dot(zn_ref[pl.ds(z_at, size), :], gate_w[u]))
+        return z_ref[pl.ds(z_at, size), :] + gate * update
+
+    project(0, True)
+    group = 4
+
+    def some_rows(t, _):
+        triangle(group, lambda i: (t * group + i) * n, 1, t * group * n)
+        return 0
+
+    lax.fori_loop(0, n // group, some_rows, 0)
+
+    def first_finish(t, _):
+        at = pl.multiple_of(t * many * n, 16)
+        z1 = finish(0, at, at, many * n).astype(BF16).astype(F32)
+        where = pl.ds(at, many * n)
+        z_ref[where, :] = z1
+        zn = normalize(z1, in_gain[1:2, :], in_bias[1:2, :])
+        zn_ref[where, :] = zn
+        zm_ref[where, :] = zn * mask_ref[where, :]
+        return 0
+
+    lax.fori_loop(0, n // many, first_finish, 0)
+
+    project(1, False)
+    start = r * rows
+    for first, count in pieces(rows, group):
+        triangle(count, lambda i: start + first + i, n, first * n)
+    for first, count in pieces(rows, 8):
+        out = finish(1, first * n, pl.multiple_of(r * block + first * n, 16), count * n)
+        for i in range(count):
+            result[first + i] = out[i * n : (i + 1) * n].astype(BF16)
+
+
+def in_one_phase(
+    pair, chain_ids, mask, pair_embed, in_gain, in_bias, proj_weight, gate_weight, out_gain, out_bias, out_weight
+):
+    rows, n, chan = pair.shape
+    hid = proj_weight.shape[3]
+    size = 8 * hid
+    weights = jnp.transpose(proj_weight, (0, 1, 3, 2)).reshape(size, chan)
+    half = (rows // 2 + 1) // 2 * 2
+    both = ("row", "ch")
+    vmem = pl.BlockSpec(memory_space=pltpu.VMEM)
+    smem = pl.BlockSpec(memory_space=pltpu.SMEM)
+
+    def pairs_of(source):
+        return [(source(r, c), r * 4 + c) for r in range(4) for c in range(4)]
+
+    first = pairs_of(lambda r, c: (r ^ (1 + c % 2)) * 4 + (c ^ 2))
+    second = pairs_of(lambda r, c: (r ^ 3) * 4 + c)
+    cores = [(c, c ^ 1) for c in range(4)]
+
+    packed, halved = pl.pallas_call(
+        functools.partial(pack_kernel, n, rows, half),
+        out_shape=(
+            jax.ShapeDtypeStruct((rows * n + size + MASK_ROWS, chan), BF16),
+            jax.ShapeDtypeStruct((half * n + MASK_ROWS, chan), BF16),
+        ),
+        in_specs=[vmem] * 3,
+        out_specs=(vmem, vmem),
+        name="pack",
+    )(pair.reshape(rows * n, chan), mask, weights)
+    packed_a = lax.ppermute(packed, both, first)
+    half_b = lax.ppermute(halved, both, second)
+    w_e = lax.ppermute(weights, "ch", cores)
+    packed_e = lax.ppermute(packed_a, "ch", cores)
+    half_f = lax.ppermute(half_b, "ch", cores)
+
+    flat = n * n
+    return pl.pallas_call(
+        functools.partial(whole_kernel, n, rows, half),
+        out_shape=jax.ShapeDtypeStruct((rows, n, chan), BF16),
+        in_specs=[vmem] * 6 + [smem] + [vmem] * 8,
+        out_specs=vmem,
+        scratch_shapes=[
+            pltpu.VMEM((flat, chan), F32),
+            pltpu.VMEM((flat, chan), BF16),
+            pltpu.VMEM((flat, chan), BF16),
+            pltpu.VMEM((flat, chan), BF16),
+            pltpu.VMEM((flat, 4 * hid), F32),
+            pltpu.VMEM((flat, 4 * hid), F32),
+            pltpu.VMEM((flat, 4 * hid), F32),
+            pltpu.VMEM((2, 4, 4, hid, chan), BF16),
+        ],
+        compiler_params=pltpu.CompilerParams(vmem_limit_bytes=40 * 1024 * 1024),
+        name="both_updates",
+    )(
+        packed, packed_a, packed_e, half_b, half_f, w_e,
+        chain_ids, chain_ids[:, None], pair_embed, in_gain, in_bias, gate_weight, out_gain, out_bias, out_weight,
+    )
 
 
 def layer_norm(values, gain, bias):
@@ -59,6 +320,24 @@
     )
     update = jnp.einsum("hrn,hc->rnc", hidden, weight, preferred_element_type=jnp.float32)
     return update
+
+
+def fits(pair_shape, weight_shape):
+    rows, n, chan = pair_shape
+    hid = weight_shape[3]
+    return (
+        lax.axis_size("row") == 4
+        and lax.axis_size("ch") == 4
+        and rows * 4 == n
+        and rows <= MASK_ROWS
+        and rows % 2 == 0
+        and n % 8 == 0
+        and n <= chan
+        and hid % 16 == 0
+        and hid * 4 == chan
+        and chan % 128 == 0
+        and n * n * chan * 4 * 6 <= 16 * 1024 * 1024
+    )
 
 
 def per_device(
@@ -75,6 +354,10 @@
     out_weight,
 ):
     rows = pair.shape[0]
+    if fits(pair.shape, proj_weight.shape):
+        return in_one_phase(
+            pair, chain_ids, mask, pair_embed, in_gain, in_bias, proj_weight, gate_weight, out_gain, out_bias, out_weight
+        )
     start_row = lax.axis_index("row") * rows
     own_chain = lax.dynamic_slice_in_dim(chain_ids, start_row, rows, 0)
     same = (own_chain[:, None] == chain_ids[None, :])[:, :, None]

time: 86.1 us -> 43.1 us (0.50)
  blocking collectives: 30.4 us -> 0 us
  Pallas kernels: 0 us -> 20.8 us
  waiting for transfers between devices: 26.2 us -> 12.2 us
  between operations: 13.6 us -> 0.09 us
  starting transfers between devices: 0.01 us -> 8.77 us
  matrix products: 5.57 us -> 0 us
  other arithmetic: 4.68 us -> 0 us
  local copies, waits for them, and re-layouts: 5.31 us -> 1.08 us
    all_gather x3 -> x0, blocking collectives: 30.4 us -> none  [the longest x1 16.8 us: outgoing(): lax.all_gather(right, 'row', axis=1, tiled=True)]
    reduce_scatter x1 -> x0, waiting for transfers between devices: 26.1 us -> none  [incoming(): lax.psum_scatter(jnp.einsum('hki,hkj->ihj', left, right, preferred_elemen...]
    pallas_call x0 -> x2, Pallas kernels: none -> 20.8 us  [the longest x1 19.1 us: in_one_phase(): pl.pallas_call(functools.partial(whole_kernel, n, rows, half), out_shape=...]
    ppermute x0 -> x5, waiting for transfers between devices: none -> 12.2 us  [the longest x1 7.15 us: in_one_phase(): packed_a = lax.ppermute(packed, both, first)]
    ppermute x0 -> x5, starting transfers between devices: none -> 8.77 us  [the longest x1 3.95 us: in_one_phase(): packed_a = lax.ppermute(packed, both, first)]
    dot_general x10 -> x0, matrix products: 5.57 us -> none  [the longest x4 2.07 us: gated(): proj = jnp.einsum(form, normed, weights, preferred_element_type=jnp.float32)]
    reduce_sum x6 -> x0, other arithmetic: 2.67 us -> none  [the longest x2 1.43 us: layer_norm(): mean = jnp.mean(values, axis=-1, keepdims=True)]
    transpose x1 -> x0, local copies, waits for them, and re-layouts: 1.61 us -> none  [incoming(): jnp.einsum('hki,hkj->ihj', left, right, preferred_element_type=jnp.float32)]
  transfers between devices with their start and end apart: 1 -> 5, of which waited for: 1 -> 3; matrix products, arithmetic and copies ran while one was open for 0% -> 0% of each run, Pallas kernels for 0% -> 0%
where the time goes in v1:
time: 43.1 us; the launch traced here: 42.9 us
  Pallas kernels  20.8 us (48%)
  waiting for transfers between devices  12.2 us (28%)
  starting transfers between devices  8.77 us (20%)
  local copies, waits for them, and re-layouts  1.08 us (3%)
    pallas_call x1, Pallas kernels, in_one_phase(): pl.pallas_call(functools.partial(whole_kernel, n, rows, half), out_shape=...  19.1 us
    ppermute x1, waiting for transfers between devices, in_one_phase(): packed_a = lax.ppermute(packed, both, first)  7.15 us
    ppermute x1, waiting for transfers between devices, in_one_phase(): half_b = lax.ppermute(halved, both, second)  4.22 us
    ppermute x1, starting transfers between devices, in_one_phase(): packed_a = lax.ppermute(packed, both, first)  3.95 us
    ppermute x1, starting transfers between devices, in_one_phase(): half_b = lax.ppermute(halved, both, second)  3.89 us
    pallas_call x1, Pallas kernels, in_one_phase(): pl.pallas_call(functools.partial(pack_kernel, n, rows, half), out_shape=(...  1.75 us
    unnamed x20, local copies, waits for them, and re-layouts  0.98 us
  transfers between devices with their start and end apart: 5, of which 3 were waited for; matrix products, arithmetic and copies ran while one was open for 0% of the time, Pallas kernels for 0%

profile of v1, /device:TPU:0, one launch (start us, length us, event | category | flops | bytes accessed | tf_op | source)
XLA Modules:
  0.0 42.9 jit_solution(13614525794434106013)
XLA Ops:
  0.0 1.8 %pack.1 = (bf16[1056,128]{1,0:T(8,128)(2,1)}, bf16[464,128]{1,0:T(8,128)(2,1)}) custom-call(bf16[784,128]{1,0:T(8,128)(2,1)} %bitcast.6, s32[14,56]{1,0:T(8,128)} %mask.1, bf16[256,128]{1,0:T(8,128)(2,1)} %bitcast.7), custom_call_target="tpu_custom_call" | custom-call | tf_op jit(solution)/shard_map/pack/pallas_call | solution.py:230
  1.8 4.0 %collective-permute-start = (bf16[1056,128]{1,0:T(8,128)(2,1)}, bf16[1056,128]{1,0:T(8,128)(2,1)S(1)}, u32[]{:S(2)}, u32[]{:S(2)}) collective-permute-start(bf16[1056,128]{1,0:T(8,128)(2,1)} %get-tuple-element.7.packed_o), channel_id=1, source_target_pairs={{6,0},{11,1},{4,2},{9,3},{2,4},{15,5},{0,6},{13,7},{14,8},{3,9},{1... | collective-permute-start | bytes 811016 | tf_op jit(solution)/shard_map/ppermute | solution.py:240
  5.7 7.1 %collective-permute-done.packed_a = bf16[1056,128]{1,0:T(8,128)(2,1)S(1)} collective-permute-done((bf16[1056,128]{1,0:T(8,128)(2,1)}, bf16[1056,128]{1,0:T(8,128)(2,1)S(1)}, u32[]{:S(2)}, u32[]{:S(2)}) %collective-permute-start) | collective-permute-done | bytes 270368 | tf_op jit(solution)/shard_map/ppermute | solution.py:240
  12.9 0.4 collective-permute-start.1
  13.3 3.9 %collective-permute-start.2 = (bf16[464,128]{1,0:T(8,128)(2,1)}, bf16[464,128]{1,0:T(8,128)(2,1)S(1)}, u32[]{:S(2)}, u32[]{:S(2)}) collective-permute-start(bf16[464,128]{1,0:T(8,128)(2,1)} %get-tuple-element.8), channel_id=1, source_target_pairs={{12,0},{13,1},{14,2},{15,3},{8,4},{9,5},{10,6},{11,7},{4,8},{5,9},... | collective-permute-start | bytes 356360 | tf_op jit(solution)/shard_map/ppermute | solution.py:241
  17.2 4.2 %collective-permute-done.2.half_b = bf16[464,128]{1,0:T(8,128)(2,1)S(1)} collective-permute-done((bf16[464,128]{1,0:T(8,128)(2,1)}, bf16[464,128]{1,0:T(8,128)(2,1)S(1)}, u32[]{:S(2)}, u32[]{:S(2)}) %collective-permute-start.2) | collective-permute-done | bytes 118816 | tf_op jit(solution)/shard_map/ppermute | solution.py:241
  21.4 0.0 collective-permute-start.3
  21.4 0.0 copy-done.9
  21.4 0.5 %collective-permute-start.4 = (bf16[256,128]{1,0:T(8,128)(2,1)S(1)}, bf16[256,128]{1,0:T(8,128)(2,1)S(1)}, u32[]{:S(2)}, u32[]{:S(2)}) collective-permute-start(bf16[256,128]{1,0:T(8,128)(2,1)S(1)} %bitcast.8), channel_id=1, source_target_pairs={{0,1},{1,0},{2,3},{3,2},{4,5},{5,4},{6,7},{7,6},{8,9},{9,8},{10,11... | collective-permute-start | bytes 196616 | tf_op jit(solution)/shard_map/ppermute | solution.py:242
  21.9 0.0 copy-done.3
  21.9 0.0 copy-start.7
  21.9 0.0 copy-start.8
  21.9 0.1 copy.12.chain_v
  22.0 0.8 %collective-permute-done.4.w_e = bf16[256,128]{1,0:T(8,128)(2,1)S(1)} collective-permute-done((bf16[256,128]{1,0:T(8,128)(2,1)S(1)}, bf16[256,128]{1,0:T(8,128)(2,1)S(1)}, u32[]{:S(2)}, u32[]{:S(2)}) %collective-permute-start.4) | collective-permute-done | bytes 65568 | tf_op jit(solution)/shard_map/ppermute | solution.py:242
  22.8 0.0 collective-permute-done.3.half_f
  22.8 0.0 collective-permute-done.1.packed_e
  22.8 0.0 copy-done.1
  22.8 0.0 copy-done.2
  22.8 0.0 copy-done.4
  22.8 0.0 copy-done.5
  22.9 0.0 copy-done.6
  22.9 0.0 copy-done.7
  22.9 0.9 %copy-done = bf16[1056,128]{1,0:T(8,128)(2,1)S(1)} copy-done((bf16[1056,128]{1,0:T(8,128)(2,1)S(1)}, bf16[1056,128]{1,0:T(8,128)(2,1)}, u32[]{:S(2)}) %copy-start) | copy-done | bytes 270360
  23.8 19.1 %both_updates.1 = bf16[14,56,128]{2,1,0:T(8,128)(2,1)} custom-call(bf16[1056,128]{1,0:T(8,128)(2,1)S(1)} %copy-done, bf16[1056,128]{1,0:T(8,128)(2,1)S(1)} %collective-permute-done.packed_a, bf16[1056,128]{1,0:T(8,128)(2,1)S(1)} %collective-permute-done.1.packed_e, bf16[464,128]{1,0:T(8,128)(2,1)S(1)} %collective-permute-done.2.half_b, ...), custom_call_target="tpu_custom_call" | custom-call | tf_op jit(solution)/shard_map/both_updates/pallas_call | solution.py:247
  (9 shorter events, 0.0 us)
Async XLA Ops:
  0.0 21.4 %copy-start.9 = (bf16[2,4,128,32]{2,3,1,0:T(8,128)(2,1)S(1)}, bf16[2,4,128,32]{2,3,1,0:T(8,128)(2,1)}, u32[]{:S(2)}) copy-start(bf16[2,4,128,32]{2,3,1,0:T(8,128)(2,1)} %param.17) | copy-start | bytes 196612
  0.0 22.8 %copy-start.1 = (bf16[2,128,128]{2,1,0:T(8,128)(2,1)S(1)}, bf16[2,128,128]{2,1,0:T(8,128)(2,1)}, u32[]{:S(2)}) copy-start(bf16[2,128,128]{2,1,0:T(8,128)(2,1)} %gate_w.1) | copy-start | bytes 196612
  0.0 22.8 %copy-start.2 = (bf16[2,128,128]{2,1,0:T(8,128)(2,1)S(1)}, bf16[2,128,128]{2,1,0:T(8,128)(2,1)}, u32[]{:S(2)}) copy-start(bf16[2,128,128]{2,1,0:T(8,128)(2,1)} %out_w.1) | copy-start | bytes 196612
  1.8 11.1 %collective-permute-start = (bf16[1056,128]{1,0:T(8,128)(2,1)}, bf16[1056,128]{1,0:T(8,128)(2,1)S(1)}, u32[]{:S(2)}, u32[]{:S(2)}) collective-permute-start(bf16[1056,128]{1,0:T(8,128)(2,1)} %get-tuple-element.7.packed_o), channel_id=1, source_target_pairs={{6,0},{11,1},{4,2},{9,3},{2,4},{15,5},{0,6},{13,7},{14,8},{3,9},{1... | collective-permute-start | bytes 811016 | tf_op jit(solution)/shard_map/ppermute | solution.py:240
  12.9 10.0 %collective-permute-start.1 = (bf16[1056,128]{1,0:T(8,128)(2,1)S(1)}, bf16[1056,128]{1,0:T(8,128)(2,1)S(1)}, u32[]{:S(2)}, u32[]{:S(2)}) collective-permute-start(bf16[1056,128]{1,0:T(8,128)(2,1)S(1)} %collective-permute-done.packed_a), channel_id=1, source_target_pairs={{0,1},{1,0},{2,3},{3,2},{4,5},{5,4},{6,7},{7,6},{8,9},{9,8},{10,11... | collective-permute-start | bytes 811016 | tf_op jit(solution)/shard_map/ppermute | solution.py:243
  13.3 8.6 %copy-start.3 = (s32[56]{0:T(128)S(1)}, s32[56]{0:T(128)}, u32[]{:S(2)}) copy-start(s32[56]{0:T(128)} %chain_s.1) | copy-start | bytes 676
  13.3 8.1 %collective-permute-start.2 = (bf16[464,128]{1,0:T(8,128)(2,1)}, bf16[464,128]{1,0:T(8,128)(2,1)S(1)}, u32[]{:S(2)}, u32[]{:S(2)}) collective-permute-start(bf16[464,128]{1,0:T(8,128)(2,1)} %get-tuple-element.8), channel_id=1, source_target_pairs={{12,0},{13,1},{14,2},{15,3},{8,4},{9,5},{10,6},{11,7},{4,8},{5,9},... | collective-permute-start | bytes 356360 | tf_op jit(solution)/shard_map/ppermute | solution.py:241
  21.4 1.4 %collective-permute-start.3 = (bf16[464,128]{1,0:T(8,128)(2,1)S(1)}, bf16[464,128]{1,0:T(8,128)(2,1)S(1)}, u32[]{:S(2)}, u32[]{:S(2)}) collective-permute-start(bf16[464,128]{1,0:T(8,128)(2,1)S(1)} %collective-permute-done.2.half_b), channel_id=1, source_target_pairs={{0,1},{1,0},{2,3},{3,2},{4,5},{5,4},{6,7},{7,6},{8,9},{9,8},{10,11... | collective-permute-start | bytes 356360 | tf_op jit(solution)/shard_map/ppermute | solution.py:244
  21.4 1.4 %collective-permute-start.4 = (bf16[256,128]{1,0:T(8,128)(2,1)S(1)}, bf16[256,128]{1,0:T(8,128)(2,1)S(1)}, u32[]{:S(2)}, u32[]{:S(2)}) collective-permute-start(bf16[256,128]{1,0:T(8,128)(2,1)S(1)} %bitcast.8), channel_id=1, source_target_pairs={{0,1},{1,0},{2,3},{3,2},{4,5},{5,4},{6,7},{7,6},{8,9},{9,8},{10,11... | collective-permute-start | bytes 196616 | tf_op jit(solution)/shard_map/ppermute | solution.py:242
  21.9 0.9 %copy-start.4 = (f32[2,128]{1,0:T(2,128)S(1)}, f32[2,128]{1,0:T(2,128)}, u32[]{:S(2)}) copy-start(f32[2,128]{1,0:T(2,128)} %embed.1) | copy-start | bytes 3076
  21.9 0.9 %copy-start.5 = (f32[2,128]{1,0:T(2,128)S(1)}, f32[2,128]{1,0:T(2,128)}, u32[]{:S(2)}) copy-start(f32[2,128]{1,0:T(2,128)} %in_gain.1) | copy-start | bytes 3076
  21.9 0.9 %copy-start.6 = (f32[2,128]{1,0:T(2,128)S(1)}, f32[2,128]{1,0:T(2,128)}, u32[]{:S(2)}) copy-start(f32[2,128]{1,0:T(2,128)} %in_bias.1) | copy-start | bytes 3076
  21.9 1.0 %copy-start.7 = (f32[2,128]{1,0:T(2,128)S(1)}, f32[2,128]{1,0:T(2,128)}, u32[]{:S(2)}) copy-start(f32[2,128]{1,0:T(2,128)} %out_gain.1) | copy-start | bytes 3076
  21.9 1.0 %copy-start.8 = (f32[2,128]{1,0:T(2,128)S(1)}, f32[2,128]{1,0:T(2,128)}, u32[]{:S(2)}) copy-start(f32[2,128]{1,0:T(2,128)} %out_bias.1) | copy-start | bytes 3076
  22.9 1.0 %copy-start = (bf16[1056,128]{1,0:T(8,128)(2,1)S(1)}, bf16[1056,128]{1,0:T(8,128)(2,1)}, u32[]{:S(2)}) copy-start(bf16[1056,128]{1,0:T(8,128)(2,1)} %get-tuple-element.7.packed_o) | copy-start | bytes 811012

commit v2 on v0

--- a/solution.py
+++ b/solution.py
@@ -1,9 +1,394 @@
+import functools
+
 import jax
 import jax.numpy as jnp
 from jax import lax
+from jax.experimental import pallas as pl
+from jax.experimental.pallas import tpu as pltpu
 from jax.sharding import PartitionSpec as P
 
 EPS = 1e-05
+F32 = jnp.float32
+BF16 = jnp.bfloat16
+MASK_ROWS = 16
+
+
+def nt_dot(a, b):
+    return lax.dot_general(a, b, (((1,), (1,)), ((), ())), preferred_element_type=F32)
+
+
+def nn_dot(a, b):
+    return lax.dot_general(a, b, (((1,), (0,)), ((), ())), preferred_element_type=F32)
+
+
+def half_sigmoid(half):
+    return 0.5 * jnp.tanh(half) + 0.5
+
+
+def normalize(values, gain, bias):
+    mean = jnp.mean(values, axis=-1, keepdims=True)
+    centered = values - mean
+    var = jnp.mean(centered * centered, axis=-1, keepdims=True)
+    return (centered * lax.rsqrt(var + EPS) * gain + bias).astype(BF16)
+
+
+def pieces(rows, most):
+    out, first = [], 0
+    while first < rows:
+        count = min(most, rows - first)
+        out.append((first, count))
+        first += count
+    return out
+
+
+def spread_masks(mask, rows, n, chan):
+    spread = (
+        lax.broadcasted_iota(jnp.int32, (rows, rows * chan), 1) // chan
+        == lax.broadcasted_iota(jnp.int32, (rows, rows * chan), 0)
+    ).astype(BF16)
+    return lax.dot_general(mask.astype(BF16), spread, (((0,), (0,)), ((), ())), preferred_element_type=F32)
+
+
+def lift(pair_rows, masks, chains, chain_s, embed, gain, bias, position, first, count):
+    other, same = embed[0:1, :], embed[1:2, :]
+    chan = chains.shape[1]
+    z = jnp.concatenate(
+        [jnp.where(chains == chain_s[position + i], same, other) for i in range(first, first + count)], axis=0
+    ) + pair_rows.astype(F32)
+    spread = jnp.concatenate([masks[:, i * chan : (i + 1) * chan] for i in range(first, first + count)], axis=0)
+    return z, normalize(z, gain, bias), spread
+
+
+def gated_side(zm, weights, u, side, chan):
+    base = (u * 4 + side * 2) * chan
+    both = nt_dot(zm, weights[base : base + 2 * chan, :])
+    return (jnp.tanh(both[:, :chan]) + 1.0) * both[:, chan:]
+
+
+def pack_kernel(n, rows, half, pair, mask, halved):
+    core = lax.rem(lax.axis_index("ch"), 2)
+    chan = pair.shape[1]
+    masks = jnp.concatenate([mask[...].astype(F32), jnp.zeros((rows, chan - n), F32)], axis=1)
+    masks = jnp.concatenate([masks, jnp.zeros((MASK_ROWS - rows, chan), F32)], axis=0).astype(BF16)
+    start = pl.multiple_of(core * (rows - half) * n, 16)
+    halved[0 : half * n, :] = pair[pl.ds(start, half * n), :]
+    halved[half * n : half * n + MASK_ROWS, :] = masks
+
+
+def weights_kernel(w_o, w_e, w_a, w_f, weights):
+    c = lax.axis_index("ch")
+    hid = w_o.shape[0] // 8
+    for at, ref in enumerate((w_o, w_e, w_a, w_f)):
+        for q in range(8):
+            first = pl.multiple_of(q * 4 * hid + (c ^ at) * hid, 16)
+            weights[pl.ds(first, hid), :] = ref[q * hid : (q + 1) * hid, :] * jnp.asarray(0.5, BF16)
+
+
+def block_kernel(
+    n, rows, which,
+    pair, mask, weights, chain_s, chain_v, embed, in_gain, in_bias, gate_w,
+    z_ref, g_ref, m_ref, left_ref, right_ref,
+):
+    r = lax.axis_index("row")
+    core = lax.rem(lax.axis_index("ch"), 2)
+    position = (r ^ which(core)) * rows
+    chan = pair.shape[1]
+    chains = jnp.broadcast_to(chain_v[...], (n, chan))
+    masks = spread_masks(mask[...].astype(F32), rows, n, chan)
+    for first, count in pieces(rows, 8):
+        at = pl.ds(first * n, count * n)
+        z, zn, spread = lift(
+            pair[at, :], masks, chains, chain_s, embed, in_gain[0:1, :], in_bias[0:1, :], position, first, count
+        )
+        zm = zn * spread.astype(BF16)
+        z_ref[at, :] = z
+        m_ref[at, :] = spread
+        g_ref[at, :] = jax.nn.sigmoid(nn_dot(zn, gate_w[0]))
+        left_ref[at, :] = gated_side(zm, weights, 0, 0, chan)
+        right_ref[at, :] = gated_side(zm, weights, 0, 1, chan)
+
+
+def tiles_of(n, count, left_at, left_ref, left_step, steps, right_ref, right_at, width, right_step):
+    def body(k, accs):
+        right = right_ref[pl.ds(pl.multiple_of(right_at + k * right_step, 8), width), :]
+        return tuple(acc + left_ref[pl.ds(left_at(i) + k * left_step, 1), :] * right for i, acc in enumerate(accs))
+
+    chan = left_ref.shape[1]
+    zeros = tuple(jnp.zeros((width, chan), F32) for _ in range(count))
+    return lax.fori_loop(0, steps, body, zeros, unroll=min(8, steps))
+
+
+def early_kernel(
+    n, rows, early,
+    z_o, z_a, z_e, g_o, g_a, g_e, m_o, m_a, m_e, left_o, left_a, left_e, right_o, right_a, right_e,
+    x_ref, right_ref, z_ref, g_ref, m_ref, left_ref,
+):
+    core = lax.rem(lax.axis_index("ch"), 2)
+    block, mid = rows * n, rows // 2 * n
+
+    @pl.when(core == 0)
+    def _():
+        for out, o, a in ((z_ref, z_o, z_a), (g_ref, g_o, g_a), (m_ref, m_o, m_a), (left_ref, left_o, left_a)):
+            out[0:block, :] = o[...]
+            out[block : block + mid, :] = a[0:mid, :]
+
+    @pl.when(core == 1)
+    def _():
+        for out, a, e in ((z_ref, z_a, z_e), (g_ref, g_a, g_e), (m_ref, m_a, m_e), (left_ref, left_a, left_e)):
+            out[0:block, :] = a[...]
+            out[block : block + mid, :] = e[mid:block, :]
+
+    for j in range(rows):
+        rows_of_j = slice(j * n, (j + 1) * n)
+        right_ref[pl.ds(j, n, stride=n), :] = right_o[rows_of_j, :]
+        right_ref[pl.ds(rows * (1 + core) + j, n, stride=n), :] = right_a[rows_of_j, :]
+        right_ref[pl.ds(rows * (2 - core) + j, n, stride=n), :] = right_e[rows_of_j, :]
+
+    group = rows // 2
+
+    def some(t, _):
+        first = t * group * n
+        accs = tiles_of(n, group, lambda i: first + i * n, left_ref, 1, n, right_ref, 0, early, n)
+        for i, acc in enumerate(accs):
+            x_ref[pl.ds(pl.multiple_of(first + i * n, 8), early), :] = acc
+        return 0
+
+    lax.fori_loop(0, 3, some, 0)
+
+
+def late_kernel(
+    n, rows, half, early,
+    half_b, half_f, weights, chain_s, chain_v, embed, in_gain, in_bias, gate_w, out_gain, out_bias, out_w,
+    x_in, right_in, z_in, g_in, m_in, left_in,
+    z1_ref, own_ref, m_ref,
+    x_ref, late_ref, left_ref, z_ref, g_ref, zn_ref, mf_ref, zf_ref,
+):
+    r = lax.axis_index("row")
+    core = lax.rem(lax.axis_index("ch"), 2)
+    even = core == 0
+    block, mid = rows * n, rows // 2 * n
+    chan = half_b.shape[1]
+    rest = rows - half
+    late = n - early
+    chains = jnp.broadcast_to(chain_v[...], (n, chan))
+    masks = spread_masks(half_b[half * n : half * n + MASK_ROWS, 0:n][0:rows], rows, n, chan)
+    skip = (half - rest) * n
+
+    first_late = 3 * rows - early
+    for t in range(first_late):
+        late_ref[pl.ds(t, n, stride=late), :] = right_in[pl.ds(early + t, n, stride=n), :]
+    for first, count in ((0, half), (half, rest)):
+        size = count * n
+        if first == 0:
+            pair_rows = jnp.where(even, half_b[0:size, :], half_f[0:size, :])
+        else:
+            pair_rows = jnp.where(even, half_f[skip : skip + size, :], half_b[skip : skip + size, :])
+        z, zn, spread = lift(
+            pair_rows, masks, chains, chain_s, embed, in_gain[0:1, :], in_bias[0:1, :], (r ^ 3) * rows, first, count
+        )
+        zm = zn * spread.astype(BF16)
+        right = gated_side(zm, weights, 0, 1, chan)
+        for j in range(count):
+            late_ref[pl.ds(first_late + first + j, n, stride=late), :] = right[j * n : (j + 1) * n]
+        at = pl.ds(first * n, size)
+        zf_ref[at, :] = z
+        mf_ref[at, :] = spread
+        zn_ref[at, :] = zn.astype(F32)
+
+    own = pl.ds(pl.multiple_of(core * mid, 8), mid)
+    tail = pl.ds(block + mid, mid)
+    zn = zn_ref[own, :].astype(BF16)
+    spread = mf_ref[own, :]
+    left_ref[tail, :] = gated_side(zn * spread.astype(BF16), weights, 0, 0, chan)
+    z_ref[tail, :] = zf_ref[own, :]
+    g_ref[tail, :] = jax.nn.sigmoid(nn_dot(zn, gate_w[0]))
+    m_ref[tail, :] = spread
+    head = pl.ds(0, block + mid)
+    left_ref[head, :] = left_in[...]
+    z_ref[head, :] = z_in[...]
+    g_ref[head, :] = g_in[...]
+    m_ref[head, :] = m_in[...]
+
+    group = rows // 2
+    x_ref[head, :] = x_in[...]
+    for i, acc in enumerate(
+        tiles_of(n, group, lambda i: block + mid + i * n, left_ref, 1, n, right_in, 0, early, n)
+    ):
+        x_ref[pl.ds(block + mid + i * n, early), :] = acc
+    for t in range(2):
+        for i, acc in enumerate(
+            tiles_of(n, rows, lambda i: t * block + i * n, left_ref, 1, n, late_ref, 0, late, late)
+        ):
+            x_ref[pl.ds(t * block + i * n + early, late), :] = acc
+
+    def ordered(first, count):
+        out = []
+        for i in range(first, first + count):
+            for b in range(4):
+                out.append(x_ref[pl.ds(i * n + (r ^ b) * rows, rows), :])
+        return jnp.concatenate(out, axis=0)
+
+    for first, count in pieces(2 * rows, 8):
+        at = pl.ds(first * n, count * n)
+        update = hidden_update(ordered(first, count), out_gain[0:1, :], out_bias[0:1, :], out_w[0])
+        z1 = (z_ref[at, :] + g_ref[at, :] * update).astype(BF16)
+        z1_ref[at, :] = z1
+        own_count = max(0, min(count, rows - first))
+        if own_count:
+            own_ref[pl.ds(first * n, own_count * n), :] = z1[: own_count * n]
+
+
+def hidden_update(x, gain, bias, weight):
+    mean = jnp.mean(x, axis=-1, keepdims=True)
+    meansq = jnp.mean(x * x, axis=-1, keepdims=True)
+    scale = lax.rsqrt(meansq - mean * mean + EPS)
+    return nn_dot(((x - mean) * scale * gain + bias).astype(BF16), weight)
+
+
+def incoming_kernel(n, rows, z1, masks, weights, in_gain, in_bias, part, left_ref, right_ref, sums_ref):
+    r = lax.axis_index("row")
+    chan = z1.shape[1]
+    for first, count in pieces(2 * rows, 8):
+        at = pl.ds(first * n, count * n)
+        zn = normalize(z1[at, :].astype(F32), in_gain[1:2, :], in_bias[1:2, :])
+        zm = zn * masks[at, :].astype(BF16)
+        left_ref[at, :] = gated_side(zm, weights, 1, 0, chan)
+        right_ref[at, :] = gated_side(zm, weights, 1, 1, chan)
+    group = rows // 2
+    wide = (n // 8 + 1) // 2 * 8
+    for t in range(2):
+        start = r * rows + t * group
+        sums = [
+            tiles_of(n, group, lambda i: start + i, left_ref, n, 2 * rows, right_ref, at, width, n)
+            for at, width in ((0, wide), (wide, n - wide))
+        ]
+        for i in range(group):
+            for (at, width), accs in zip(((0, wide), (wide, n - wide)), sums):
+                left = (t * group + i) * n + at
+                sums_ref[left : left + width, :] = accs[i]
+    part[...] = sums_ref[...].astype(BF16)
+
+
+def gate_kernel(own, received, in_gain, in_bias, gate_w, z_ref, g_ref):
+    even = lax.rem(lax.axis_index("ch"), 2) == 0
+    z = jnp.where(even, own[...], received[...]).astype(F32)
+    z_ref[...] = z
+    zn = normalize(z, in_gain[1:2, :], in_bias[1:2, :])
+    g_ref[...] = jax.nn.sigmoid(nn_dot(zn, gate_w[1]))
+
+
+def last_kernel(n, rows, part, received, z_ref, g_ref, out_gain, out_bias, out_w, result):
+    for first, count in pieces(rows, 8):
+        at = pl.ds(first * n, count * n)
+        x = part[at, :].astype(F32) + received[at, :].astype(F32)
+        update = hidden_update(x, out_gain[1:2, :], out_bias[1:2, :], out_w[1])
+        out = (z_ref[at, :] + g_ref[at, :] * update).astype(BF16)
+        for i in range(count):
+            result[first + i] = out[i * n : (i + 1) * n]
+
+
+def in_one_phase(
+    pair, chain_ids, mask, pair_embed, in_gain, in_bias, proj_weight, gate_weight, out_gain, out_bias, out_weight
+):
+    rows, n, chan = pair.shape
+    hid = proj_weight.shape[3]
+    size = 8 * hid
+    block, mid = rows * n, rows // 2 * n
+    flat_pair = pair.reshape(block, chan)
+    weights = jnp.transpose(proj_weight, (0, 1, 3, 2)).reshape(size, chan)
+    half = (rows // 2 + 1) // 2 * 2
+    early = 3 * rows // 8 * 8
+    both = ("row", "ch")
+    vmem = pl.BlockSpec(memory_space=pltpu.VMEM)
+    smem = pl.BlockSpec(memory_space=pltpu.SMEM)
+
+    def pairs_of(source):
+        return [(source(r, c), r * 4 + c) for r in range(4) for c in range(4)]
+
+    first = pairs_of(lambda r, c: (r ^ (1 + c % 2)) * 4 + (c ^ 2))
+    second = pairs_of(lambda r, c: (r ^ 3) * 4 + c)
+    cores = [(c, c ^ 1) for c in range(4)]
+
+    def call(kernel, name, outs, ins, scalars=(), scratch=(), us=1.0):
+        kept = [pltpu.with_memory_space_constraint(v, pltpu.VMEM) if id(v) in in_vmem else v for v in ins]
+        specs = [smem if id(v) in scalars else vmem for v in ins]
+        got = pl.pallas_call(
+            kernel,
+            out_shape=tuple(outs),
+            in_specs=specs,
+            out_specs=tuple(vmem for _ in outs),
+            scratch_shapes=[pltpu.VMEM(s, F32) for s in scratch],
+            compiler_params=pltpu.CompilerParams(vmem_limit_bytes=32 * 1024 * 1024),
+            cost_estimate=pl.CostEstimate(flops=int(us * 1e9), bytes_accessed=0, transcendentals=0),
+            name=name,
+        )(*kept)
+        for v in got:
+            in_vmem[id(v)] = v
+        return got
+
+    in_vmem = {}
+    f32 = lambda count: pltpu.VMEM((count, chan), F32)
+    bf16 = lambda count: pltpu.VMEM((count, chan), BF16)
+    chain_v = chain_ids[:, None]
+    scalars = (id(chain_ids),)
+
+    w_e = lax.ppermute(weights, "ch", cores)
+    w_a, pair_a, mask_a = (lax.ppermute(v, both, first) for v in (weights, flat_pair, mask))
+    (halved,) = call(
+        functools.partial(pack_kernel, n, rows, half), "pack", [bf16(half * n + MASK_ROWS)], [flat_pair, mask]
+    )
+    half_b = lax.ppermute(halved, both, second)
+    w_f, pair_e, mask_e = (lax.ppermute(v, "ch", cores) for v in (w_a, pair_a, mask_a))
+    (w_all,) = call(weights_kernel, "weights", [bf16(4 * size)], [weights, w_e, w_a, w_f], us=0.1)
+    half_f = lax.ppermute(half_b, "ch", cores)
+
+    def one_block(name, which, pair_rows, mask_rows):
+        return call(
+            functools.partial(block_kernel, n, rows, which),
+            name,
+            [f32(block)] * 5,
+            [pair_rows, mask_rows, w_all, chain_ids, chain_v, pair_embed, in_gain, in_bias, gate_weight],
+            scalars,
+        )
+
+    at_o = one_block("own_block", lambda core: 0, flat_pair, mask)
+    at_a = one_block("first_block", lambda core: 1 + core, pair_a, mask_a)
+    at_e = one_block("second_block", lambda core: 2 - core, pair_e, mask_e)
+    at_early = call(
+        functools.partial(early_kernel, n, rows, early),
+        "early",
+        [f32(block + mid), f32(n * n)] + [f32(block + mid)] * 4,
+        [v for three in zip(at_o, at_a, at_e) for v in three],
+        us=2.0,
+    )
+    z1, own, masks = call(
+        functools.partial(late_kernel, n, rows, half, early),
+        "late",
+        [bf16(2 * block), bf16(block), f32(2 * block)],
+        [half_b, half_f, w_all, chain_ids, chain_v, pair_embed, in_gain, in_bias, gate_weight, out_gain, out_bias, out_weight]
+        + list(at_early),
+        scalars,
+        [(2 * block, chan), (n * (n - early), chan)] + [(2 * block, chan)] * 3 + [(block, chan)] * 3,
+        us=4.0,
+    )
+    own_n = lax.ppermute(own, "ch", cores)
+    (part,) = call(
+        functools.partial(incoming_kernel, n, rows),
+        "incoming",
+        [bf16(block)],
+        [z1, masks, w_all, in_gain, in_bias],
+        scratch=[(2 * block, chan)] * 2 + [(block, chan)],
+        us=3.0,
+    )
+    part_n = lax.ppermute(part, "ch", cores)
+    z1_own, gate = call(gate_kernel, "gate", [f32(block)] * 2, [own, own_n, in_gain, in_bias, gate_weight])
+    (result,) = call(
+        functools.partial(last_kernel, n, rows),
+        "last",
+        [jax.ShapeDtypeStruct((rows, n, chan), BF16)],
+        [part, part_n, z1_own, gate, out_gain, out_bias, out_weight],
+    )
+    return result
 
 
 def layer_norm(values, gain, bias):
@@ -59,6 +444,24 @@
     )
     update = jnp.einsum("hrn,hc->rnc", hidden, weight, preferred_element_type=jnp.float32)
     return update
+
+
+def fits(pair_shape, weight_shape):
+    rows, n, chan = pair_shape
+    hid = weight_shape[3]
+    return (
+        lax.axis_size("row") == 4
+        and lax.axis_size("ch") == 4
+        and rows * 4 == n
+        and rows <= MASK_ROWS
+        and rows % 2 == 0
+        and n % 8 == 0
+        and n <= chan
+        and hid % 16 == 0
+        and hid * 4 == chan
+        and chan % 128 == 0
+        and n * n * chan * 4 * 6 <= 16 * 1024 * 1024
+    )
 
 
 def per_device(
@@ -75,6 +478,10 @@
     out_weight,
 ):
     rows = pair.shape[0]
+    if fits(pair.shape, proj_weight.shape):
+        return in_one_phase(
+            pair, chain_ids, mask, pair_embed, in_gain, in_bias, proj_weight, gate_weight, out_gain, out_bias, out_weight
+        )
     start_row = lax.axis_index("row") * rows
     own_chain = lax.dynamic_slice_in_dim(chain_ids, start_row, rows, 0)
     same = (own_chain[:, None] == chain_ids[None, :])[:, :, None]

time: 86.1 us -> 34.8 us (0.40)
  blocking collectives: 30.4 us -> 0 us
  waiting for transfers between devices: 26.2 us -> 6.93 us
  Pallas kernels: 0 us -> 13.9 us
  between operations: 13.6 us -> 0.2 us
  starting transfers between devices: 0.01 us -> 11.8 us
  matrix products: 5.57 us -> 0 us
  other arithmetic: 4.68 us -> 0 us
  local copies, waits for them, and re-layouts: 5.31 us -> 1.8 us
    all_gather x3 -> x0, blocking collectives: 30.4 us -> none  [the longest x1 16.8 us: outgoing(): lax.all_gather(right, 'row', axis=1, tiled=True)]
    reduce_scatter x1 -> x0, waiting for transfers between devices: 26.1 us -> none  [incoming(): lax.psum_scatter(jnp.einsum('hki,hkj->ihj', left, right, preferred_elemen...]
    pallas_call x0 -> x10, Pallas kernels: none -> 13.9 us  [call(): pl.pallas_call(kernel, out_shape=tuple(outs), in_specs=specs, out_specs=t...]
    ppermute x0 -> x11, starting transfers between devices: none -> 11.8 us  [the longest x3 4.41 us: in_one_phase(): lax.ppermute(v, both, first)]
    ppermute x0 -> x11, waiting for transfers between devices: none -> 6.93 us  [the longest x3 6.34 us: in_one_phase(): lax.ppermute(v, both, first)]
    dot_general x10 -> x0, matrix products: 5.57 us -> none  [the longest x4 2.07 us: gated(): proj = jnp.einsum(form, normed, weights, preferred_element_type=jnp.float32)]
    reduce_sum x6 -> x0, other arithmetic: 2.67 us -> none  [the longest x2 1.43 us: layer_norm(): mean = jnp.mean(values, axis=-1, keepdims=True)]
    transpose x1 -> x0, local copies, waits for them, and re-layouts: 1.61 us -> none  [incoming(): jnp.einsum('hki,hkj->ihj', left, right, preferred_element_type=jnp.float32)]
  transfers between devices with their start and end apart: 1 -> 11, of which waited for: 1 -> 3; matrix products, arithmetic and copies ran while one was open for 0% -> 0% of each run, Pallas kernels for 0% -> 26%
where the time goes in v2:
time: 34.8 us; the launch traced here: 34.6 us
  Pallas kernels  13.9 us (40%)
  starting transfers between devices  11.8 us (34%)
  waiting for transfers between devices  6.93 us (20%)
  local copies, waits for them, and re-layouts  1.8 us (5%)
    pallas_call x10, Pallas kernels, call(): pl.pallas_call(kernel, out_shape=tuple(outs), in_specs=specs, out_specs=t...  13.9 us
    ppermute x3, waiting for transfers between devices, in_one_phase(): lax.ppermute(v, both, first)  6.34 us
    ppermute x3, starting transfers between devices, in_one_phase(): lax.ppermute(v, both, first)  4.41 us
    ppermute x1, starting transfers between devices, in_one_phase(): half_b = lax.ppermute(halved, both, second)  4.02 us
    ppermute x3, starting transfers between devices, in_one_phase(): lax.ppermute(v, 'ch', cores)  2.19 us
    unnamed x26, local copies, waits for them, and re-layouts  1.71 us
  transfers between devices with their start and end apart: 11, of which 3 were waited for; matrix products, arithmetic and copies ran while one was open for 0% of the time, Pallas kernels for 26%

profile of v2, /device:TPU:0, one launch (start us, length us, event | category | flops | bytes accessed | tf_op | source)
XLA Modules:
  0.0 34.6 jit_solution(4002803356875122563)
XLA Ops:
  0.0 4.0 %collective-permute-start.3 = (bf16[256,128]{1,0:T(8,128)(2,1)}, bf16[256,128]{1,0:T(8,128)(2,1)S(1)}, u32[]{:S(2)}, u32[]{:S(2)}) collective-permute-start(bf16[256,128]{1,0:T(8,128)(2,1)} %bitcast.5), channel_id=1, source_target_pairs={{6,0},{11,1},{4,2},{9,3},{2,4},{15,5},{0,6},{13,7},{14,8},{3,9},{1... | collective-permute-start | bytes 196616 | tf_op jit(solution)/shard_map/ppermute | solution.py:336
  4.0 0.1 collective-permute-start.5
  4.0 1.0 %copy-done.2 = bf16[14,56,128]{2,1,0:T(8,128)(2,1)S(1)} copy-done((bf16[14,56,128]{2,1,0:T(8,128)(2,1)S(1)}, bf16[14,56,128]{2,1,0:T(8,128)(2,1)}, u32[]{:S(2)}) %copy-start.2) | copy-done | bytes 200728
  5.0 0.7 %copy-done.6 = s32[14,56]{1,0:T(8,128)S(1)} copy-done((s32[14,56]{1,0:T(8,128)S(1)}, s32[14,56]{1,0:T(8,128)}, u32[]{:S(2)}) %copy-start.6) | copy-done | bytes 3160
  5.7 4.0 %collective-permute-start = (bf16[464,128]{1,0:T(8,128)(2,1)S(1)}, bf16[464,128]{1,0:T(8,128)(2,1)S(1)}, u32[]{:S(2)}, u32[]{:S(2)}) collective-permute-start(bf16[464,128]{1,0:T(8,128)(2,1)S(1)} %pack.1), channel_id=1, source_target_pairs={{12,0},{13,1},{14,2},{15,3},{8,4},{9,5},{10,6},{11,7},{4,8},{5,9},... | collective-permute-start | bytes 356360 | tf_op jit(solution)/shard_map/ppermute | solution.py:340
  9.8 0.5 %collective-permute-start.4 = (bf16[256,128]{1,0:T(8,128)(2,1)S(1)}, bf16[256,128]{1,0:T(8,128)(2,1)S(1)}, u32[]{:S(2)}, u32[]{:S(2)}) collective-permute-start(bf16[256,128]{1,0:T(8,128)(2,1)S(1)} %collective-permute-done.3.w_a), channel_id=1, source_target_pairs={{0,1},{1,0},{2,3},{3,2},{4,5},{5,4},{6,7},{7,6},{8,9},{9,8},{10,11... | collective-permute-start | bytes 196616 | tf_op jit(solution)/shard_map/ppermute | solution.py:341
  10.3 2.3 %collective-permute-done.5.pair = bf16[784,128]{1,0:T(8,128)(2,1)S(1)} collective-permute-done((bf16[784,128]{1,0:T(8,128)(2,1)}, bf16[784,128]{1,0:T(8,128)(2,1)S(1)}, u32[]{:S(2)}, u32[]{:S(2)}) %collective-permute-start.5) | collective-permute-done | bytes 200736 | tf_op jit(solution)/shard_map/ppermute | solution.py:336
  12.5 1.7 %collective-permute-start.7 = (bf16[784,128]{1,0:T(8,128)(2,1)S(1)}, bf16[784,128]{1,0:T(8,128)(2,1)S(1)}, u32[]{:S(2)}, u32[]{:S(2)}) collective-permute-start(bf16[784,128]{1,0:T(8,128)(2,1)S(1)} %collective-permute-done.5.pair), channel_id=1, source_target_pairs={{0,1},{1,0},{2,3},{3,2},{4,5},{5,4},{6,7},{7,6},{8,9},{9,8},{10,11... | collective-permute-start | bytes 602120 | tf_op jit(solution)/shard_map/ppermute | solution.py:341
  14.2 0.4 %collective-permute-start.6 = (s32[14,56]{1,0:T(8,128)S(1)}, s32[14,56]{1,0:T(8,128)S(1)}, u32[]{:S(2)}, u32[]{:S(2)}) collective-permute-start(s32[14,56]{1,0:T(8,128)S(1)} %copy-done.7), channel_id=1, source_target_pairs={{6,0},{11,1},{4,2},{9,3},{2,4},{15,5},{0,6},{13,7},{14,8},{3,9},{1... | collective-permute-start | bytes 9416 | tf_op jit(solution)/shard_map/ppermute | solution.py:336
  14.6 0.1 copy.15.chain_v
  14.7 4.1 %collective-permute-done.6.mask = s32[14,56]{1,0:T(8,128)S(1)} collective-permute-done((s32[14,56]{1,0:T(8,128)S(1)}, s32[14,56]{1,0:T(8,128)S(1)}, u32[]{:S(2)}, u32[]{:S(2)}) %collective-permute-start.6) | collective-permute-done | bytes 3168 | tf_op jit(solution)/shard_map/ppermute | solution.py:336
  18.8 0.5 %collective-permute-start.1 = (bf16[464,128]{1,0:T(8,128)(2,1)S(1)}, bf16[464,128]{1,0:T(8,128)(2,1)S(1)}, u32[]{:S(2)}, u32[]{:S(2)}) collective-permute-start(bf16[464,128]{1,0:T(8,128)(2,1)S(1)} %collective-permute-done.half_b), channel_id=1, source_target_pairs={{0,1},{1,0},{2,3},{3,2},{4,5},{5,4},{6,7},{7,6},{8,9},{9,8},{10,11... | collective-permute-start | bytes 356360 | tf_op jit(solution)/shard_map/ppermute | solution.py:343
  19.3 0.1 weights.1
  19.4 1.3 %own_block.1 = (f32[784,128]{1,0:T(8,128)S(1)}, f32[784,128]{1,0:T(8,128)S(1)}, f32[784,128]{1,0:T(8,128)S(1)}, f32[784,128]{1,0:T(8,128)S(1)}, f32[784,128]{1,0:T(8,128)S(1)}) custom-call(bf16[784,128]{1,0:T(8,128)(2,1)S(1)} %bitcast.11, s32[14,56]{1,0:T(8,128)S(1)} %copy-done.7, bf16[1024,128]{1,0:T(8,128)(2,1)S(1)} %weights.1, s32[56]{0:T(128)S(1)} %copy-done.1, ...), custom_call_target="tpu_custom_call" | custom-call | flops 1000000000 | tf_op jit(solution)/shard_map/own_block/pallas_call | solution.py:315
  20.8 1.3 %first_block.1 = (f32[784,128]{1,0:T(8,128)S(1)}, f32[784,128]{1,0:T(8,128)S(1)}, f32[784,128]{1,0:T(8,128)S(1)}, f32[784,128]{1,0:T(8,128)S(1)}, f32[784,128]{1,0:T(8,128)S(1)}) custom-call(bf16[784,128]{1,0:T(8,128)(2,1)S(1)} %collective-permute-done.5.pair, s32[14,56]{1,0:T(8,128)S(1)} %collective-permute-done.6.mask, bf16[1024,128]{1,0:T(8,128)(2,1)S(1)} %weights.1, ...), custom_call_target="tpu_custom_call" | custom-call | flops 1000000000 | tf_op jit(solution)/shard_map/first_block/pallas_call | solution.py:315
  22.1 1.3 %second_block.1 = (f32[784,128]{1,0:T(8,128)S(1)}, f32[784,128]{1,0:T(8,128)S(1)}, f32[784,128]{1,0:T(8,128)S(1)}, f32[784,128]{1,0:T(8,128)S(1)}, f32[784,128]{1,0:T(8,128)S(1)}) custom-call(bf16[784,128]{1,0:T(8,128)(2,1)S(1)} %collective-permute-done.7.pair, s32[14,56]{1,0:T(8,128)S(1)} %collective-permute-done.8.mask, bf16[1024,128]{1,0:T(8,128)(2,1)S(1)} %weights.1, ...), custom_call_target="tpu_custom_call" | custom-call | flops 1000000000 | tf_op jit(solution)/shard_map/second_block/pallas_call | solution.py:315
  23.5 2.2 %early.1 = (f32[1176,128]{1,0:T(8,128)S(1)}, f32[3136,128]{1,0:T(8,128)S(1)}, f32[1176,128]{1,0:T(8,128)S(1)}, f32[1176,128]{1,0:T(8,128)S(1)}, f32[1176,128]{1,0:T(8,128)S(1)}, /*index=5*/f32[1176,128]{1,0:T(8,128)S(1)}) custom-call(f32[784,128]{1,0:T(8,128)S(1)} %get-tuple-element.31.z_o, f32[784,128]{1,0:T(8,128)S(1)} %get-tuple-element.32.z_a, ...), custom_call_target="tpu_custom_call" | custom-call | flops 2000000000 | tf_op jit(solution)/shard_map/early/pallas_call | solution.py:315
  25.8 3.7 %late.1 = (bf16[1568,128]{1,0:T(8,128)(2,1)S(1)}, bf16[784,128]{1,0:T(8,128)(2,1)S(1)}, f32[1568,128]{1,0:T(8,128)S(1)}) custom-call(bf16[464,128]{1,0:T(8,128)(2,1)S(1)} %collective-permute-done.half_b, bf16[464,128]{1,0:T(8,128)(2,1)S(1)} %collective-permute-done.1.half_f, bf16[1024,128]{1,0:T(8,128)(2,1)S(1)} %weights.1, s32[56]{0:T(128)S(1)} %copy-done.1, ...), custom_call_target="tpu_custom_call" | custom-call | flops 4000000000 | tf_op jit(solution)/shard_map/late/pallas_call | solution.py:315
  29.6 0.1 collective-permute-start.10
  29.6 2.2 %incoming.1.part = bf16[784,128]{1,0:T(8,128)(2,1)S(1)} custom-call(bf16[1568,128]{1,0:T(8,128)(2,1)S(1)} %get-tuple-element.52.z1, f32[1568,128]{1,0:T(8,128)S(1)} %get-tuple-element.53.masks, bf16[1024,128]{1,0:T(8,128)(2,1)S(1)} %weights.1, f32[2,128]{1,0:T(2,128)S(1)} %copy-done.9, f32[2,128]{1,0:T(2,128)S(1)} %copy-done.10), custom_call_target="tpu_custom_call" | custom-call | flops 3000000000 | tf_op jit(solution)/shard_map/incoming/pallas_call | solution.py:315
  31.9 0.6 %collective-permute-start.9 = (bf16[784,128]{1,0:T(8,128)(2,1)S(1)}, bf16[784,128]{1,0:T(8,128)(2,1)S(1)}, u32[]{:S(2)}, u32[]{:S(2)}) collective-permute-start(bf16[784,128]{1,0:T(8,128)(2,1)S(1)} %incoming.1.part), channel_id=1, source_target_pairs={{0,1},{1,0},{2,3},{3,2},{4,5},{5,4},{6,7},{7,6},{8,9},{9,8},{10,11... | collective-permute-start | bytes 602120 | tf_op jit(solution)/shard_map/ppermute | solution.py:383
  32.4 0.5 %gate.1 = (f32[784,128]{1,0:T(8,128)S(1)}, f32[784,128]{1,0:T(8,128)S(1)}) custom-call(bf16[784,128]{1,0:T(8,128)(2,1)S(1)} %get-tuple-element.54.own, bf16[784,128]{1,0:T(8,128)(2,1)S(1)} %collective-permute-done.10.received, f32[2,128]{1,0:T(2,128)S(1)} %copy-done.9, f32[2,128]{1,0:T(2,128)S(1)} %copy-done.10, bf16[2,128,128]{2,1,0:T(8,128)(2,1)S(1)} %copy-done.4), custom_call_target="tpu_custom_call" | custom-call | flops 1000000000 | tf_op jit(solution)/shard_map/gate/pallas_call | solution.py:315
  32.9 0.6 %collective-permute-done.9.received = bf16[784,128]{1,0:T(8,128)(2,1)S(1)} collective-permute-done((bf16[784,128]{1,0:T(8,128)(2,1)S(1)}, bf16[784,128]{1,0:T(8,128)(2,1)S(1)}, u32[]{:S(2)}, u32[]{:S(2)}) %collective-permute-start.9) | collective-permute-done | bytes 200736 | tf_op jit(solution)/shard_map/ppermute | solution.py:383
  33.5 1.1 %last.1 = bf16[14,56,128]{2,1,0:T(8,128)(2,1)} custom-call(bf16[784,128]{1,0:T(8,128)(2,1)S(1)} %incoming.1.part, bf16[784,128]{1,0:T(8,128)(2,1)S(1)} %collective-permute-done.9.received, f32[784,128]{1,0:T(8,128)S(1)} %get-tuple-element.55.z_ref, f32[784,128]{1,0:T(8,128)S(1)} %get-tuple-element.56.g_ref, f32[2,128]{1,0:T(2,128)S(1)} %copy-done.11, ...), custom_call_target="tpu_custom_call" | custom-call | flops 1000000000 | tf_op jit(solution)/shard_map/last/pallas_call | solution.py:315
  (35 shorter events, 0.1 us)
Async XLA Ops:
  0.0 9.8 %collective-permute-start.3 = (bf16[256,128]{1,0:T(8,128)(2,1)}, bf16[256,128]{1,0:T(8,128)(2,1)S(1)}, u32[]{:S(2)}, u32[]{:S(2)}) collective-permute-start(bf16[256,128]{1,0:T(8,128)(2,1)} %bitcast.5), channel_id=1, source_target_pairs={{6,0},{11,1},{4,2},{9,3},{2,4},{15,5},{0,6},{13,7},{14,8},{3,9},{1... | collective-permute-start | bytes 196616 | tf_op jit(solution)/shard_map/ppermute | solution.py:336
  4.0 5.8 %copy-start = (bf16[2,4,128,32]{2,3,1,0:T(8,128)(2,1)S(1)}, bf16[2,4,128,32]{2,3,1,0:T(8,128)(2,1)}, u32[]{:S(2)}) copy-start(bf16[2,4,128,32]{2,3,1,0:T(8,128)(2,1)} %param.17) | copy-start | bytes 196612
  4.0 10.7 %copy-start.1 = (s32[56]{0:T(128)S(1)}, s32[56]{0:T(128)}, u32[]{:S(2)}) copy-start(s32[56]{0:T(128)} %chain_s.7) | copy-start | bytes 676
  4.0 8.6 %collective-permute-start.5 = (bf16[784,128]{1,0:T(8,128)(2,1)}, bf16[784,128]{1,0:T(8,128)(2,1)S(1)}, u32[]{:S(2)}, u32[]{:S(2)}) collective-permute-start(bf16[784,128]{1,0:T(8,128)(2,1)} %bitcast.9), channel_id=1, source_target_pairs={{6,0},{11,1},{4,2},{9,3},{2,4},{15,5},{0,6},{13,7},{14,8},{3,9},{1... | collective-permute-start | bytes 602120 | tf_op jit(solution)/shard_map/ppermute | solution.py:336
  4.0 1.0 %copy-start.2 = (bf16[14,56,128]{2,1,0:T(8,128)(2,1)S(1)}, bf16[14,56,128]{2,1,0:T(8,128)(2,1)}, u32[]{:S(2)}) copy-start(bf16[14,56,128]{2,1,0:T(8,128)(2,1)} %param.11) | copy-start | bytes 602116
  5.0 0.7 %copy-start.6 = (s32[14,56]{1,0:T(8,128)S(1)}, s32[14,56]{1,0:T(8,128)}, u32[]{:S(2)}) copy-start(s32[14,56]{1,0:T(8,128)} %mask.3) | copy-start | bytes 9412
  5.7 8.5 %copy-start.7 = (s32[14,56]{1,0:T(8,128)S(1)}, s32[14,56]{1,0:T(8,128)}, u32[]{:S(2)}) copy-start(s32[14,56]{1,0:T(8,128)} %mask.3) | copy-start | bytes 9412
  5.7 13.7 %copy-start.3 = (bf16[14,56,128]{2,1,0:T(8,128)(2,1)S(1)}, bf16[14,56,128]{2,1,0:T(8,128)(2,1)}, u32[]{:S(2)}) copy-start(bf16[14,56,128]{2,1,0:T(8,128)(2,1)} %param.11) | copy-start | bytes 602116
  5.7 13.7 %copy-start.4 = (bf16[2,128,128]{2,1,0:T(8,128)(2,1)S(1)}, bf16[2,128,128]{2,1,0:T(8,128)(2,1)}, u32[]{:S(2)}) copy-start(bf16[2,128,128]{2,1,0:T(8,128)(2,1)} %gate_w.9) | copy-start | bytes 196612
  5.7 13.7 %copy-start.8 = (f32[2,128]{1,0:T(2,128)S(1)}, f32[2,128]{1,0:T(2,128)}, u32[]{:S(2)}) copy-start(f32[2,128]{1,0:T(2,128)} %embed.7) | copy-start | bytes 3076
  5.7 13.7 %copy-start.9 = (f32[2,128]{1,0:T(2,128)S(1)}, f32[2,128]{1,0:T(2,128)}, u32[]{:S(2)}) copy-start(f32[2,128]{1,0:T(2,128)} %in_gain.11) | copy-start | bytes 3076
  5.7 13.7 %copy-start.10 = (f32[2,128]{1,0:T(2,128)S(1)}, f32[2,128]{1,0:T(2,128)}, u32[]{:S(2)}) copy-start(f32[2,128]{1,0:T(2,128)} %in_bias.11) | copy-start | bytes 3076
  5.7 13.0 %collective-permute-start = (bf16[464,128]{1,0:T(8,128)(2,1)S(1)}, bf16[464,128]{1,0:T(8,128)(2,1)S(1)}, u32[]{:S(2)}, u32[]{:S(2)}) collective-permute-start(bf16[464,128]{1,0:T(8,128)(2,1)S(1)} %pack.1), channel_id=1, source_target_pairs={{12,0},{13,1},{14,2},{15,3},{8,4},{9,5},{10,6},{11,7},{4,8},{5,9},... | collective-permute-start | bytes 356360 | tf_op jit(solution)/shard_map/ppermute | solution.py:340
  9.8 9.5 %collective-permute-start.2 = (bf16[256,128]{1,0:T(8,128)(2,1)S(1)}, bf16[256,128]{1,0:T(8,128)(2,1)S(1)}, u32[]{:S(2)}, u32[]{:S(2)}) collective-permute-start(bf16[256,128]{1,0:T(8,128)(2,1)S(1)} %bitcast.6), channel_id=1, source_target_pairs={{0,1},{1,0},{2,3},{3,2},{4,5},{5,4},{6,7},{7,6},{8,9},{9,8},{10,11... | collective-permute-start | bytes 196616 | tf_op jit(solution)/shard_map/ppermute | solution.py:335
  9.8 9.5 %collective-permute-start.4 = (bf16[256,128]{1,0:T(8,128)(2,1)S(1)}, bf16[256,128]{1,0:T(8,128)(2,1)S(1)}, u32[]{:S(2)}, u32[]{:S(2)}) collective-permute-start(bf16[256,128]{1,0:T(8,128)(2,1)S(1)} %collective-permute-done.3.w_a), channel_id=1, source_target_pairs={{0,1},{1,0},{2,3},{3,2},{4,5},{5,4},{6,7},{7,6},{8,9},{9,8},{10,11... | collective-permute-start | bytes 196616 | tf_op jit(solution)/shard_map/ppermute | solution.py:341
  12.5 9.6 %collective-permute-start.7 = (bf16[784,128]{1,0:T(8,128)(2,1)S(1)}, bf16[784,128]{1,0:T(8,128)(2,1)S(1)}, u32[]{:S(2)}, u32[]{:S(2)}) collective-permute-start(bf16[784,128]{1,0:T(8,128)(2,1)S(1)} %collective-permute-done.5.pair), channel_id=1, source_target_pairs={{0,1},{1,0},{2,3},{3,2},{4,5},{5,4},{6,7},{7,6},{8,9},{9,8},{10,11... | collective-permute-start | bytes 602120 | tf_op jit(solution)/shard_map/ppermute | solution.py:341
  14.2 4.6 %collective-permute-start.6 = (s32[14,56]{1,0:T(8,128)S(1)}, s32[14,56]{1,0:T(8,128)S(1)}, u32[]{:S(2)}, u32[]{:S(2)}) collective-permute-start(s32[14,56]{1,0:T(8,128)S(1)} %copy-done.7), channel_id=1, source_target_pairs={{6,0},{11,1},{4,2},{9,3},{2,4},{15,5},{0,6},{13,7},{14,8},{3,9},{1... | collective-permute-start | bytes 9416 | tf_op jit(solution)/shard_map/ppermute | solution.py:336
  18.8 3.3 %collective-permute-start.8 = (s32[14,56]{1,0:T(8,128)S(1)}, s32[14,56]{1,0:T(8,128)S(1)}, u32[]{:S(2)}, u32[]{:S(2)}) collective-permute-start(s32[14,56]{1,0:T(8,128)S(1)} %collective-permute-done.6.mask), channel_id=1, source_target_pairs={{0,1},{1,0},{2,3},{3,2},{4,5},{5,4},{6,7},{7,6},{8,9},{9,8},{10,11... | collective-permute-start | bytes 9416 | tf_op jit(solution)/shard_map/ppermute | solution.py:341
  18.8 7.0 %collective-permute-start.1 = (bf16[464,128]{1,0:T(8,128)(2,1)S(1)}, bf16[464,128]{1,0:T(8,128)(2,1)S(1)}, u32[]{:S(2)}, u32[]{:S(2)}) collective-permute-start(bf16[464,128]{1,0:T(8,128)(2,1)S(1)} %collective-permute-done.half_b), channel_id=1, source_target_pairs={{0,1},{1,0},{2,3},{3,2},{4,5},{5,4},{6,7},{7,6},{8,9},{9,8},{10,11... | collective-permute-start | bytes 356360 | tf_op jit(solution)/shard_map/ppermute | solution.py:343
  23.5 2.3 %copy-start.5 = (bf16[2,128,128]{2,1,0:T(8,128)(2,1)S(1)}, bf16[2,128,128]{2,1,0:T(8,128)(2,1)}, u32[]{:S(2)}) copy-start(bf16[2,128,128]{2,1,0:T(8,128)(2,1)} %out_w.3) | copy-start | bytes 196612
  23.5 2.3 %copy-start.11 = (f32[2,128]{1,0:T(2,128)S(1)}, f32[2,128]{1,0:T(2,128)}, u32[]{:S(2)}) copy-start(f32[2,128]{1,0:T(2,128)} %out_gain.3) | copy-start | bytes 3076
  23.5 2.3 %copy-start.12 = (f32[2,128]{1,0:T(2,128)S(1)}, f32[2,128]{1,0:T(2,128)}, u32[]{:S(2)}) copy-start(f32[2,128]{1,0:T(2,128)} %out_bias.3) | copy-start | bytes 3076
  29.6 2.9 %collective-permute-start.10 = (bf16[784,128]{1,0:T(8,128)(2,1)S(1)}, bf16[784,128]{1,0:T(8,128)(2,1)S(1)}, u32[]{:S(2)}, u32[]{:S(2)}) collective-permute-start(bf16[784,128]{1,0:T(8,128)(2,1)S(1)} %get-tuple-element.54.own), channel_id=1, source_target_pairs={{0,1},{1,0},{2,3},{3,2},{4,5},{5,4},{6,7},{7,6},{8,9},{9,8},{10,11... | collective-permute-start | bytes 602120 | tf_op jit(solution)/shard_map/ppermute | solution.py:374
  31.9 1.6 %collective-permute-start.9 = (bf16[784,128]{1,0:T(8,128)(2,1)S(1)}, bf16[784,128]{1,0:T(8,128)(2,1)S(1)}, u32[]{:S(2)}, u32[]{:S(2)}) collective-permute-start(bf16[784,128]{1,0:T(8,128)(2,1)S(1)} %incoming.1.part), channel_id=1, source_target_pairs={{0,1},{1,0},{2,3},{3,2},{4,5},{5,4},{6,7},{7,6},{8,9},{9,8},{10,11... | collective-permute-start | bytes 602120 | tf_op jit(solution)/shard_map/ppermute | solution.py:383

commit v3 on v2

--- a/solution.py
+++ b/solution.py
@@ -49,11 +49,15 @@
     return lax.dot_general(mask.astype(BF16), spread, (((0,), (0,)), ((), ())), preferred_element_type=F32)
 
 
-def lift(pair_rows, masks, chains, chain_s, embed, gain, bias, position, first, count):
+def lift(pair_rows, masks, chains, embed, gain, bias, position, first, count):
     other, same = embed[0:1, :], embed[1:2, :]
     chan = chains.shape[1]
     z = jnp.concatenate(
-        [jnp.where(chains == chain_s[position + i], same, other) for i in range(first, first + count)], axis=0
+        [
+            jnp.where(chains[...] == chains[pl.ds(position + i, 1), :], same, other)
+            for i in range(first, first + count)
+        ],
+        axis=0,
     ) + pair_rows.astype(F32)
     spread = jnp.concatenate([masks[:, i * chan : (i + 1) * chan] for i in range(first, first + count)], axis=0)
     return z, normalize(z, gain, bias), spread
@@ -65,45 +69,84 @@
     return (jnp.tanh(both[:, :chan]) + 1.0) * both[:, chan:]
 
 
-def pack_kernel(n, rows, half, pair, mask, halved):
+def pack_kernel(n, rows, part, pair, mask, packed, halved, mask_v, sems):
     core = lax.rem(lax.axis_index("ch"), 2)
-    chan = pair.shape[1]
-    masks = jnp.concatenate([mask[...].astype(F32), jnp.zeros((rows, chan - n), F32)], axis=1)
+    block, chan = pair.shape
+    start = pl.multiple_of(core * (block - part), 16)
+    copies = [
+        pltpu.make_async_copy(mask, mask_v, sems.at[0]),
+        pltpu.make_async_copy(pair, packed.at[pl.ds(0, block)], sems.at[1]),
+        pltpu.make_async_copy(pair.at[pl.ds(start, part)], halved.at[pl.ds(0, part)], sems.at[2]),
+    ]
+    for copy in copies:
+        copy.start()
+    copies[0].wait()
+    masks = jnp.concatenate([mask_v[...].astype(F32), jnp.zeros((rows, chan - n), F32)], axis=1)
     masks = jnp.concatenate([masks, jnp.zeros((MASK_ROWS - rows, chan), F32)], axis=0).astype(BF16)
-    start = pl.multiple_of(core * (rows - half) * n, 16)
-    halved[0 : half * n, :] = pair[pl.ds(start, half * n), :]
-    halved[half * n : half * n + MASK_ROWS, :] = masks
+    packed[block : block + MASK_ROWS, :] = masks
+    halved[part : part + MASK_ROWS, :] = masks
+    copies[1].wait()
+    copies[2].wait()
+
+
+def constants_kernel(chain_row, *refs):
+    count = (len(refs) - 3) // 2
+    sources, outs = refs[:count], refs[count : 2 * count]
+    chains, row, sems = refs[2 * count :]
+    first = pltpu.make_async_copy(chain_row, row, sems.at[count])
+    first.start()
+    copies = [pltpu.make_async_copy(a, b, sems.at[i]) for i, (a, b) in enumerate(zip(sources, outs))]
+    for copy in copies:
+        copy.start()
+    first.wait()
+    ones = jnp.ones((1, chains.shape[1]), BF16)
+    chains[...] = lax.dot_general(
+        row[...].astype(F32).astype(BF16), ones, (((0,), (0,)), ((), ())), preferred_element_type=F32
+    )
+    for copy in copies:
+        copy.wait()
+
+
+def pass_kernel(value, after, out):
+    out[...] = value[...]
 
 
 def weights_kernel(w_o, w_e, w_a, w_f, weights):
     c = lax.axis_index("ch")
-    hid = w_o.shape[0] // 8
+    hid = w_e.shape[0] // 8
     for at, ref in enumerate((w_o, w_e, w_a, w_f)):
         for q in range(8):
             first = pl.multiple_of(q * 4 * hid + (c ^ at) * hid, 16)
             weights[pl.ds(first, hid), :] = ref[q * hid : (q + 1) * hid, :] * jnp.asarray(0.5, BF16)
 
 
-def block_kernel(
+def lift_kernel(
     n, rows, which,
-    pair, mask, weights, chain_s, chain_v, embed, in_gain, in_bias, gate_w,
-    z_ref, g_ref, m_ref, left_ref, right_ref,
+    packed, chains, embed, in_gain, in_bias, gate_w,
+    z_ref, g_ref, m_ref, zm_ref,
 ):
     r = lax.axis_index("row")
     core = lax.rem(lax.axis_index("ch"), 2)
     position = (r ^ which(core)) * rows
-    chan = pair.shape[1]
-    chains = jnp.broadcast_to(chain_v[...], (n, chan))
-    masks = spread_masks(mask[...].astype(F32), rows, n, chan)
+    chan = packed.shape[1]
+    masks_at = packed.shape[0] - MASK_ROWS
+    masks = spread_masks(packed[masks_at : masks_at + MASK_ROWS, 0:n][0:rows], rows, n, chan)
     for first, count in pieces(rows, 8):
         at = pl.ds(first * n, count * n)
         z, zn, spread = lift(
-            pair[at, :], masks, chains, chain_s, embed, in_gain[0:1, :], in_bias[0:1, :], position, first, count
+            packed[at, :], masks, chains, embed, in_gain[0:1, :], in_bias[0:1, :], position, first, count
         )
-        zm = zn * spread.astype(BF16)
         z_ref[at, :] = z
         m_ref[at, :] = spread
         g_ref[at, :] = jax.nn.sigmoid(nn_dot(zn, gate_w[0]))
+        zm_ref[at, :] = zn * spread.astype(BF16)
+
+
+def project_kernel(n, rows, zm_ref, weights, left_ref, right_ref):
+    chan = zm_ref.shape[1]
+    for first, count in pieces(rows, 8):
+        at = pl.ds(first * n, count * n)
+        zm = zm_ref[at, :]
         left_ref[at, :] = gated_side(zm, weights, 0, 0, chan)
         right_ref[at, :] = gated_side(zm, weights, 0, 1, chan)
 
@@ -157,8 +200,8 @@
 
 
 def late_kernel(
-    n, rows, half, early,
-    half_b, half_f, weights, chain_s, chain_v, embed, in_gain, in_bias, gate_w, out_gain, out_bias, out_w,
+    n, rows, part, early,
+    half_b, half_f, weights, chains, embed, in_gain, in_bias, gate_w, out_gain, out_bias, out_w,
     x_in, right_in, z_in, g_in, m_in, left_in,
     z1_ref, own_ref, m_ref,
     x_ref, late_ref, left_ref, z_ref, g_ref, zn_ref, mf_ref, zf_ref,
@@ -168,23 +211,25 @@
     even = core == 0
     block, mid = rows * n, rows // 2 * n
     chan = half_b.shape[1]
-    rest = rows - half
     late = n - early
-    chains = jnp.broadcast_to(chain_v[...], (n, chan))
-    masks = spread_masks(half_b[half * n : half * n + MASK_ROWS, 0:n][0:rows], rows, n, chan)
-    skip = (half - rest) * n
+    masks = spread_masks(half_b[part : part + MASK_ROWS, 0:n][0:rows], rows, n, chan)
+    skip = 2 * part - block
+    pair_rows = jnp.concatenate(
+        [
+            jnp.where(even, half_b[0:part, :], half_f[0:part, :]),
+            jnp.where(even, half_f[skip:part, :], half_b[skip:part, :]),
+        ],
+        axis=0,
+    )
 
     first_late = 3 * rows - early
     for t in range(first_late):
         late_ref[pl.ds(t, n, stride=late), :] = right_in[pl.ds(early + t, n, stride=n), :]
-    for first, count in ((0, half), (half, rest)):
+    for first, count in pieces(rows, 8):
         size = count * n
-        if first == 0:
-            pair_rows = jnp.where(even, half_b[0:size, :], half_f[0:size, :])
-        else:
-            pair_rows = jnp.where(even, half_f[skip : skip + size, :], half_b[skip : skip + size, :])
         z, zn, spread = lift(
-            pair_rows, masks, chains, chain_s, embed, in_gain[0:1, :], in_bias[0:1, :], (r ^ 3) * rows, first, count
+            pair_rows[first * n : first * n + size], masks, chains, embed, in_gain[0:1, :], in_bias[0:1, :],
+            (r ^ 3) * rows, first, count,
         )
         zm = zn * spread.astype(BF16)
         right = gated_side(zm, weights, 0, 1, chan)
@@ -296,26 +341,25 @@
     block, mid = rows * n, rows // 2 * n
     flat_pair = pair.reshape(block, chan)
     weights = jnp.transpose(proj_weight, (0, 1, 3, 2)).reshape(size, chan)
-    half = (rows // 2 + 1) // 2 * 2
+    part = (block // 2 + 15) // 16 * 16
     early = 3 * rows // 8 * 8
     both = ("row", "ch")
     vmem = pl.BlockSpec(memory_space=pltpu.VMEM)
-    smem = pl.BlockSpec(memory_space=pltpu.SMEM)
 
     def pairs_of(source):
         return [(source(r, c), r * 4 + c) for r in range(4) for c in range(4)]
 
-    first = pairs_of(lambda r, c: (r ^ (1 + c % 2)) * 4 + (c ^ 2))
+    first = pairs_of(lambda r, c: (r ^ (1 + c % 2)) * 4 + c)
     second = pairs_of(lambda r, c: (r ^ 3) * 4 + c)
     cores = [(c, c ^ 1) for c in range(4)]
-
-    def call(kernel, name, outs, ins, scalars=(), scratch=(), us=1.0):
+    chips = [(c, c ^ 2) for c in range(4)]
+
+    def call(kernel, name, outs, ins, scratch=(), us=1.0):
         kept = [pltpu.with_memory_space_constraint(v, pltpu.VMEM) if id(v) in in_vmem else v for v in ins]
-        specs = [smem if id(v) in scalars else vmem for v in ins]
         got = pl.pallas_call(
             kernel,
             out_shape=tuple(outs),
-            in_specs=specs,
+            in_specs=[vmem] * len(ins),
             out_specs=tuple(vmem for _ in outs),
             scratch_shapes=[pltpu.VMEM(s, F32) for s in scratch],
             compiler_params=pltpu.CompilerParams(vmem_limit_bytes=32 * 1024 * 1024),
@@ -329,31 +373,56 @@
     in_vmem = {}
     f32 = lambda count: pltpu.VMEM((count, chan), F32)
     bf16 = lambda count: pltpu.VMEM((count, chan), BF16)
-    chain_v = chain_ids[:, None]
-    scalars = (id(chain_ids),)
-
+
+    packed, halved = pl.pallas_call(
+        functools.partial(pack_kernel, n, rows, part),
+        out_shape=(bf16(block + MASK_ROWS), bf16(part + MASK_ROWS)),
+        in_specs=[pl.BlockSpec(memory_space=pl.ANY)] * 2,
+        out_specs=(vmem, vmem),
+        scratch_shapes=[pltpu.VMEM((rows, n), jnp.int32), pltpu.SemaphoreType.DMA((3,))],
+        name="pack",
+    )(*(pltpu.with_memory_space_constraint(v, pltpu.HBM) for v in (flat_pair, mask)))
+    sources = (weights, pair_embed, in_gain, in_bias, gate_weight, out_gain, out_bias, out_weight)
+    constants = pl.pallas_call(
+        constants_kernel,
+        out_shape=tuple(pltpu.VMEM(v.shape, v.dtype) for v in sources) + (pltpu.VMEM((n, chan), F32),),
+        in_specs=[pl.BlockSpec(memory_space=pl.ANY)] * (1 + len(sources)),
+        out_specs=tuple(vmem for _ in range(1 + len(sources))),
+        scratch_shapes=[pltpu.VMEM((1, n), jnp.int32), pltpu.SemaphoreType.DMA((1 + len(sources),))],
+        name="constants",
+    )(*(pltpu.with_memory_space_constraint(v, pltpu.HBM) for v in (chain_ids.reshape(1, n),) + sources))
+    in_vmem.update({id(v): v for v in (packed, halved) + tuple(constants)})
+    w_own, pair_embed, in_gain, in_bias, gate_weight, out_gain, out_bias, out_weight, chains = constants
+    packed_a = lax.ppermute(packed, both, first)
+    half_b = lax.ppermute(halved, both, second)
     w_e = lax.ppermute(weights, "ch", cores)
-    w_a, pair_a, mask_a = (lax.ppermute(v, both, first) for v in (weights, flat_pair, mask))
-    (halved,) = call(
-        functools.partial(pack_kernel, n, rows, half), "pack", [bf16(half * n + MASK_ROWS)], [flat_pair, mask]
-    )
-    half_b = lax.ppermute(halved, both, second)
-    w_f, pair_e, mask_e = (lax.ppermute(v, "ch", cores) for v in (w_a, pair_a, mask_a))
-    (w_all,) = call(weights_kernel, "weights", [bf16(4 * size)], [weights, w_e, w_a, w_f], us=0.1)
+    w_a = lax.ppermute(weights, "ch", chips)
+    w_f = lax.ppermute(w_a, "ch", cores)
+    packed_e = lax.ppermute(packed_a, "ch", cores)
+
+    def one_block(name, which, source):
+        return call(
+            functools.partial(lift_kernel, n, rows, which),
+            name,
+            [f32(block)] * 3 + [bf16(block)],
+            [source, chains, pair_embed, in_gain, in_bias, gate_weight],
+            us=0.8,
+        )
+
+    at_o = one_block("lift_own", lambda core: 0, packed)
+    at_a = one_block("lift_first", lambda core: 1 + core, packed_a)
+    (w_all,) = call(weights_kernel, "weights", [bf16(4 * size)], [w_own, w_e, w_a, w_f], us=0.1)
+    at_e = one_block("lift_second", lambda core: 2 - core, packed_e)
+
+    def project(name, lifted):
+        sides = call(functools.partial(project_kernel, n, rows), name, [f32(block)] * 2, [lifted[3], w_all], us=0.6)
+        return list(lifted[:3]) + list(sides)
+
+    at_o, at_a, at_e = (
+        project(name, v) for name, v in (("project_own", at_o), ("project_first", at_a), ("project_second", at_e))
+    )
+    (half_b,) = call(pass_kernel, "pass_on", [bf16(part + MASK_ROWS)], [half_b, at_e[4]], us=0.1)
     half_f = lax.ppermute(half_b, "ch", cores)
-
-    def one_block(name, which, pair_rows, mask_rows):
-        return call(
-            functools.partial(block_kernel, n, rows, which),
-            name,
-            [f32(block)] * 5,
-            [pair_rows, mask_rows, w_all, chain_ids, chain_v, pair_embed, in_gain, in_bias, gate_weight],
-            scalars,
-        )
-
-    at_o = one_block("own_block", lambda core: 0, flat_pair, mask)
-    at_a = one_block("first_block", lambda core: 1 + core, pair_a, mask_a)
-    at_e = one_block("second_block", lambda core: 2 - core, pair_e, mask_e)
     at_early = call(
         functools.partial(early_kernel, n, rows, early),
         "early",
@@ -362,12 +431,11 @@
         us=2.0,
     )
     z1, own, masks = call(
-        functools.partial(late_kernel, n, rows, half, early),
+        functools.partial(late_kernel, n, rows, part, early),
         "late",
         [bf16(2 * block), bf16(block), f32(2 * block)],
-        [half_b, half_f, w_all, chain_ids, chain_v, pair_embed, in_gain, in_bias, gate_weight, out_gain, out_bias, out_weight]
+        [half_b, half_f, w_all, chains, pair_embed, in_gain, in_bias, gate_weight, out_gain, out_bias, out_weight]
         + list(at_early),
-        scalars,
         [(2 * block, chan), (n * (n - early), chan)] + [(2 * block, chan)] * 3 + [(block, chan)] * 3,
         us=4.0,
     )

time: 34.8 us -> 26 us (0.75)
  the two profiles are of different devices: /device:TPU:0 before, /device:TPU:31 now
where the time goes in v3:
time: 26 us; the launch traced here: 25.8 us
  Pallas kernels  13.9 us (53%)
  waiting for transfers between devices  5.88 us (23%)
  starting transfers between devices  5.79 us (22%)
    pallas_call x13, Pallas kernels, call(): pl.pallas_call(kernel, out_shape=tuple(outs), in_specs=[vmem] * len(ins),...  11.8 us
    ppermute x1, waiting for transfers between devices, in_one_phase(): packed_a = lax.ppermute(packed, both, first)  5.28 us
    ppermute x1, starting transfers between devices, in_one_phase(): w_f = lax.ppermute(w_a, 'ch', cores)  1.78 us
    ppermute x1, starting transfers between devices, in_one_phase(): w_e = lax.ppermute(weights, 'ch', cores)  1.33 us
    pallas_call x1, Pallas kernels, in_one_phase(): pl.pallas_call(constants_kernel, out_shape=tuple((pltpu.VMEM(v.shape, v.d...  1.08 us
    ppermute x1, starting transfers between devices, in_one_phase(): half_b = lax.ppermute(halved, both, second)  1.07 us
    pallas_call x1, Pallas kernels, in_one_phase(): pl.pallas_call(functools.partial(pack_kernel, n, rows, part), out_shape=(...  1.03 us
    ppermute x1, waiting for transfers between devices, in_one_phase(): part_n = lax.ppermute(part, 'ch', cores)  0.58 us
  transfers between devices with their start and end apart: 9, of which 2 were waited for; matrix products, arithmetic and copies ran while one was open for 0% of the time, Pallas kernels for 34%

profile of v3, /device:TPU:31, one launch (start us, length us, event | category | flops | bytes accessed | tf_op | source)
XLA Modules:
  0.0 25.8 jit_solution(18279419386769060442)
XLA Ops:
  0.0 1.0 %pack.1 = (bf16[800,128]{1,0:T(8,128)(2,1)S(1)}, bf16[416,128]{1,0:T(8,128)(2,1)S(1)}) custom-call(bf16[784,128]{1,0:T(8,128)(2,1)} %bitcast.5, s32[14,56]{1,0:T(8,128)} %mask.1), custom_call_target="tpu_custom_call" | custom-call | tf_op jit(solution)/shard_map/pack/pallas_call | solution.py:377
  1.0 0.1 collective-permute-start.1
  1.2 0.3 %collective-permute-start.4 = (bf16[256,128]{1,0:T(8,128)(2,1)}, bf16[256,128]{1,0:T(8,128)(2,1)S(1)}, u32[]{:S(2)}, u32[]{:S(2)}) collective-permute-start(bf16[256,128]{1,0:T(8,128)(2,1)} %bitcast.6), channel_id=1, source_target_pairs={{0,2},{1,3},{2,0},{3,1},{4,6},{5,7},{6,4},{7,5},{8,10},{9,11},{10,... | collective-permute-start | bytes 196616 | tf_op jit(solution)/shard_map/ppermute | solution.py:399
  1.4 1.3 %collective-permute-start.3 = (bf16[256,128]{1,0:T(8,128)(2,1)}, bf16[256,128]{1,0:T(8,128)(2,1)S(1)}, u32[]{:S(2)}, u32[]{:S(2)}) collective-permute-start(bf16[256,128]{1,0:T(8,128)(2,1)} %bitcast.7), channel_id=1, source_target_pairs={{0,1},{1,0},{2,3},{3,2},{4,5},{5,4},{6,7},{7,6},{8,9},{9,8},{10,11... | collective-permute-start | bytes 196616 | tf_op jit(solution)/shard_map/ppermute | solution.py:398
  2.8 1.1 %collective-permute-start = (bf16[416,128]{1,0:T(8,128)(2,1)S(1)}, bf16[416,128]{1,0:T(8,128)(2,1)S(1)}, u32[]{:S(2)}, u32[]{:S(2)}) collective-permute-start(bf16[416,128]{1,0:T(8,128)(2,1)S(1)} %get-tuple-element.45), channel_id=1, source_target_pairs={{12,0},{13,1},{14,2},{15,3},{8,4},{9,5},{10,6},{11,7},{4,8},{5,9},... | collective-permute-start | bytes 319496 | tf_op jit(solution)/shard_map/ppermute | solution.py:397
  3.8 1.1 %constants.1 = (bf16[256,128]{1,0:T(8,128)(2,1)S(1)}, f32[2,128]{1,0:T(2,128)S(1)}, f32[2,128]{1,0:T(2,128)S(1)}, f32[2,128]{1,0:T(2,128)S(1)}, bf16[2,128,128]{...) custom-call(s32[1,56]{1,0:T(1,128)} %bitcast.9, ...), custom_call_target="tpu_custom_call" | custom-call | tf_op jit(solution)/shard_map/constants/pallas_call | solution.py:386
  4.9 1.8 %collective-permute-start.5 = (bf16[256,128]{1,0:T(8,128)(2,1)S(1)}, bf16[256,128]{1,0:T(8,128)(2,1)S(1)}, u32[]{:S(2)}, u32[]{:S(2)}) collective-permute-start(bf16[256,128]{1,0:T(8,128)(2,1)S(1)} %collective-permute-done.4.w_a), channel_id=1, source_target_pairs={{0,1},{1,0},{2,3},{3,2},{4,5},{5,4},{6,7},{7,6},{8,9},{9,8},{10,11... | collective-permute-start | bytes 196616 | tf_op jit(solution)/shard_map/ppermute | solution.py:400
  6.7 5.3 %collective-permute-done.1.packed = bf16[800,128]{1,0:T(8,128)(2,1)S(1)} collective-permute-done((bf16[800,128]{1,0:T(8,128)(2,1)S(1)}, bf16[800,128]{1,0:T(8,128)(2,1)S(1)}, u32[]{:S(2)}, u32[]{:S(2)}) %collective-permute-start.1) | collective-permute-done | bytes 204832 | tf_op jit(solution)/shard_map/ppermute | solution.py:396
  12.0 0.5 %lift_own.1 = (f32[784,128]{1,0:T(8,128)S(1)}, f32[784,128]{1,0:T(8,128)S(1)}, f32[784,128]{1,0:T(8,128)S(1)}, bf16[784,128]{1,0:T(8,128)(2,1)S(1)}) custom-call(bf16[800,128]{1,0:T(8,128)(2,1)S(1)} %get-tuple-element.46.packed, f32[56,128]{1,0:T(8,128)S(1)} %get-tuple-element.47.chains, f32[2,128]{1,0:T(2,128)S(1)} %get-tuple-element.48.embed, ...), custom_call_target="tpu_custom_call" | custom-call | flops 800000000 | tf_op jit(solution)/shard_map/lift_own/pallas_call | solution.py:359
  12.5 0.1 weights.1
  12.6 0.4 %project_own.1 = (f32[784,128]{1,0:T(8,128)S(1)}, f32[784,128]{1,0:T(8,128)S(1)}) custom-call(bf16[784,128]{1,0:T(8,128)(2,1)S(1)} %get-tuple-element.67.zm_ref, bf16[1024,128]{1,0:T(8,128)(2,1)S(1)} %weights.1), custom_call_target="tpu_custom_call" | custom-call | flops 600000000 | tf_op jit(solution)/shard_map/project_own/pallas_call | solution.py:359
  13.0 0.5 %lift_first.1 = (f32[784,128]{1,0:T(8,128)S(1)}, f32[784,128]{1,0:T(8,128)S(1)}, f32[784,128]{1,0:T(8,128)S(1)}, bf16[784,128]{1,0:T(8,128)(2,1)S(1)}) custom-call(bf16[800,128]{1,0:T(8,128)(2,1)S(1)} %collective-permute-done.1.packed, f32[56,128]{1,0:T(8,128)S(1)} %get-tuple-element.47.chains, f32[2,128]{1,0:T(2,128)S(1)} %get-tuple-element.48.embed, ...), custom_call_target="tpu_custom_call" | custom-call | flops 800000000 | tf_op jit(solution)/shard_map/lift_first/pallas_call | solution.py:359
  13.5 0.4 %project_first.1 = (f32[784,128]{1,0:T(8,128)S(1)}, f32[784,128]{1,0:T(8,128)S(1)}) custom-call(bf16[784,128]{1,0:T(8,128)(2,1)S(1)} %get-tuple-element.69.zm_ref, bf16[1024,128]{1,0:T(8,128)(2,1)S(1)} %weights.1), custom_call_target="tpu_custom_call" | custom-call | flops 600000000 | tf_op jit(solution)/shard_map/project_first/pallas_call | solution.py:359
  13.9 0.5 %lift_second.1 = (f32[784,128]{1,0:T(8,128)S(1)}, f32[784,128]{1,0:T(8,128)S(1)}, f32[784,128]{1,0:T(8,128)S(1)}, bf16[784,128]{1,0:T(8,128)(2,1)S(1)}) custom-call(bf16[800,128]{1,0:T(8,128)(2,1)S(1)} %collective-permute-done.2.packed, f32[56,128]{1,0:T(8,128)S(1)} %get-tuple-element.47.chains, f32[2,128]{1,0:T(2,128)S(1)} %get-tuple-element.48.embed, ...), custom_call_target="tpu_custom_call" | custom-call | flops 800000000 | tf_op jit(solution)/shard_map/lift_second/pallas_call | solution.py:359
  14.4 0.4 %project_second.1 = (f32[784,128]{1,0:T(8,128)S(1)}, f32[784,128]{1,0:T(8,128)S(1)}) custom-call(bf16[784,128]{1,0:T(8,128)(2,1)S(1)} %get-tuple-element.52.zm_ref, bf16[1024,128]{1,0:T(8,128)(2,1)S(1)} %weights.1), custom_call_target="tpu_custom_call" | custom-call | flops 600000000 | tf_op jit(solution)/shard_map/project_second/pallas_call | solution.py:359
  14.8 0.6 %collective-permute-start.6 = (bf16[416,128]{1,0:T(8,128)(2,1)S(1)}, bf16[416,128]{1,0:T(8,128)(2,1)S(1)}, u32[]{:S(2)}, u32[]{:S(2)}) collective-permute-start(bf16[416,128]{1,0:T(8,128)(2,1)S(1)} %pass_on.1.half_b), channel_id=1, source_target_pairs={{0,1},{1,0},{2,3},{3,2},{4,5},{5,4},{6,7},{7,6},{8,9},{9,8},{10,11... | collective-permute-start | bytes 319496 | tf_op jit(solution)/shard_map/ppermute | solution.py:425
  15.4 2.2 %early.1 = (f32[1176,128]{1,0:T(8,128)S(1)}, f32[3136,128]{1,0:T(8,128)S(1)}, f32[1176,128]{1,0:T(8,128)S(1)}, f32[1176,128]{1,0:T(8,128)S(1)}, f32[1176,128]{1,0:T(8,128)S(1)}, /*index=5*/f32[1176,128]{1,0:T(8,128)S(1)}) custom-call(f32[784,128]{1,0:T(8,128)S(1)} %get-tuple-element.58.z_o, f32[784,128]{1,0:T(8,128)S(1)} %get-tuple-element.59.z_a, ...), custom_call_target="tpu_custom_call" | custom-call | flops 2000000000 | tf_op jit(solution)/shard_map/early/pallas_call | solution.py:359
  17.6 3.1 %late.1 = (bf16[1568,128]{1,0:T(8,128)(2,1)S(1)}, bf16[784,128]{1,0:T(8,128)(2,1)S(1)}, f32[1568,128]{1,0:T(8,128)S(1)}) custom-call(bf16[416,128]{1,0:T(8,128)(2,1)S(1)} %pass_on.1.half_b, bf16[416,128]{1,0:T(8,128)(2,1)S(1)} %collective-permute-done.6.half_f, bf16[1024,128]{1,0:T(8,128)(2,1)S(1)} %weights.1, f32[56,128]{1,0:T(8,128)S(1)} %get-tuple-element.47.chains, ...), custom_call_target="tpu_custom_call" | custom-call | flops 4000000000 | tf_op jit(solution)/shard_map/late/pallas_call | solution.py:359
  20.7 0.1 collective-permute-start.8
  20.8 2.2 %incoming.1.part = bf16[784,128]{1,0:T(8,128)(2,1)S(1)} custom-call(bf16[1568,128]{1,0:T(8,128)(2,1)S(1)} %get-tuple-element.80.z1, f32[1568,128]{1,0:T(8,128)S(1)} %get-tuple-element.81.masks, bf16[1024,128]{1,0:T(8,128)(2,1)S(1)} %weights.1, f32[2,128]{1,0:T(2,128)S(1)} %get-tuple-element.49.in_gain, f32[2,128]{1,0:T(2,128)S(1)} %get-tuple-element.50.in_bias), custom_call_target="tpu_custom_call" | custom-call | flops 3000000000 | tf_op jit(solution)/shard_map/incoming/pallas_call | solution.py:359
  23.0 0.5 %collective-permute-start.7 = (bf16[784,128]{1,0:T(8,128)(2,1)S(1)}, bf16[784,128]{1,0:T(8,128)(2,1)S(1)}, u32[]{:S(2)}, u32[]{:S(2)}) collective-permute-start(bf16[784,128]{1,0:T(8,128)(2,1)S(1)} %incoming.1.part), channel_id=1, source_target_pairs={{0,1},{1,0},{2,3},{3,2},{4,5},{5,4},{6,7},{7,6},{8,9},{9,8},{10,11... | collective-permute-start | bytes 602120 | tf_op jit(solution)/shard_map/ppermute | solution.py:451
  23.6 0.5 %gate.1 = (f32[784,128]{1,0:T(8,128)S(1)}, f32[784,128]{1,0:T(8,128)S(1)}) custom-call(bf16[784,128]{1,0:T(8,128)(2,1)S(1)} %get-tuple-element.82.own, bf16[784,128]{1,0:T(8,128)(2,1)S(1)} %collective-permute-done.8.received, f32[2,128]{1,0:T(2,128)S(1)} %get-tuple-element.49.in_gain, f32[2,128]{1,0:T(2,128)S(1)} %get-tuple-element.50.in_bias, ...), custom_call_target="tpu_custom_call" | custom-call | flops 1000000000 | tf_op jit(solution)/shard_map/gate/pallas_call | solution.py:359
  24.1 0.6 %collective-permute-done.7.received = bf16[784,128]{1,0:T(8,128)(2,1)S(1)} collective-permute-done((bf16[784,128]{1,0:T(8,128)(2,1)S(1)}, bf16[784,128]{1,0:T(8,128)(2,1)S(1)}, u32[]{:S(2)}, u32[]{:S(2)}) %collective-permute-start.7) | collective-permute-done | bytes 200736 | tf_op jit(solution)/shard_map/ppermute | solution.py:451
  24.7 1.1 %last.1 = bf16[14,56,128]{2,1,0:T(8,128)(2,1)} custom-call(bf16[784,128]{1,0:T(8,128)(2,1)S(1)} %incoming.1.part, bf16[784,128]{1,0:T(8,128)(2,1)S(1)} %collective-permute-done.7.received, f32[784,128]{1,0:T(8,128)S(1)} %get-tuple-element.83.z_ref, f32[784,128]{1,0:T(8,128)S(1)} %get-tuple-element.84.g_ref, f32[2,128]{1,0:T(2,128)S(1)} %get-tuple-element.55.out_gain, ...), custom_call_target="tpu_custom_call" | custom-call | flops 1000000000 | tf_op jit(solution)/shard_map/last/pallas_call | solution.py:359
  (9 shorter events, 0.0 us)
Async XLA Ops:
  1.0 11.0 %collective-permute-start.1 = (bf16[800,128]{1,0:T(8,128)(2,1)S(1)}, bf16[800,128]{1,0:T(8,128)(2,1)S(1)}, u32[]{:S(2)}, u32[]{:S(2)}) collective-permute-start(bf16[800,128]{1,0:T(8,128)(2,1)S(1)} %get-tuple-element.46.packed), channel_id=1, source_target_pairs={{4,0},{9,1},{6,2},{11,3},{0,4},{13,5},{2,6},{15,7},{12,8},{1,9},{1... | collective-permute-start | bytes 614408 | tf_op jit(solution)/shard_map/ppermute | solution.py:396
  1.2 3.8 %collective-permute-start.4 = (bf16[256,128]{1,0:T(8,128)(2,1)}, bf16[256,128]{1,0:T(8,128)(2,1)S(1)}, u32[]{:S(2)}, u32[]{:S(2)}) collective-permute-start(bf16[256,128]{1,0:T(8,128)(2,1)} %bitcast.6), channel_id=1, source_target_pairs={{0,2},{1,3},{2,0},{3,1},{4,6},{5,7},{6,4},{7,5},{8,10},{9,11},{10,... | collective-permute-start | bytes 196616 | tf_op jit(solution)/shard_map/ppermute | solution.py:399
  1.4 11.1 %collective-permute-start.3 = (bf16[256,128]{1,0:T(8,128)(2,1)}, bf16[256,128]{1,0:T(8,128)(2,1)S(1)}, u32[]{:S(2)}, u32[]{:S(2)}) collective-permute-start(bf16[256,128]{1,0:T(8,128)(2,1)} %bitcast.7), channel_id=1, source_target_pairs={{0,1},{1,0},{2,3},{3,2},{4,5},{5,4},{6,7},{7,6},{8,9},{9,8},{10,11... | collective-permute-start | bytes 196616 | tf_op jit(solution)/shard_map/ppermute | solution.py:398
  2.8 12.0 %collective-permute-start = (bf16[416,128]{1,0:T(8,128)(2,1)S(1)}, bf16[416,128]{1,0:T(8,128)(2,1)S(1)}, u32[]{:S(2)}, u32[]{:S(2)}) collective-permute-start(bf16[416,128]{1,0:T(8,128)(2,1)S(1)} %get-tuple-element.45), channel_id=1, source_target_pairs={{12,0},{13,1},{14,2},{15,3},{8,4},{9,5},{10,6},{11,7},{4,8},{5,9},... | collective-permute-start | bytes 319496 | tf_op jit(solution)/shard_map/ppermute | solution.py:397
  4.9 7.6 %collective-permute-start.5 = (bf16[256,128]{1,0:T(8,128)(2,1)S(1)}, bf16[256,128]{1,0:T(8,128)(2,1)S(1)}, u32[]{:S(2)}, u32[]{:S(2)}) collective-permute-start(bf16[256,128]{1,0:T(8,128)(2,1)S(1)} %collective-permute-done.4.w_a), channel_id=1, source_target_pairs={{0,1},{1,0},{2,3},{3,2},{4,5},{5,4},{6,7},{7,6},{8,9},{9,8},{10,11... | collective-permute-start | bytes 196616 | tf_op jit(solution)/shard_map/ppermute | solution.py:400
  12.0 1.9 %collective-permute-start.2 = (bf16[800,128]{1,0:T(8,128)(2,1)S(1)}, bf16[800,128]{1,0:T(8,128)(2,1)S(1)}, u32[]{:S(2)}, u32[]{:S(2)}) collective-permute-start(bf16[800,128]{1,0:T(8,128)(2,1)S(1)} %collective-permute-done.1.packed), channel_id=1, source_target_pairs={{0,1},{1,0},{2,3},{3,2},{4,5},{5,4},{6,7},{7,6},{8,9},{9,8},{10,11... | collective-permute-start | bytes 614408 | tf_op jit(solution)/shard_map/ppermute | solution.py:401
  14.8 2.8 %collective-permute-start.6 = (bf16[416,128]{1,0:T(8,128)(2,1)S(1)}, bf16[416,128]{1,0:T(8,128)(2,1)S(1)}, u32[]{:S(2)}, u32[]{:S(2)}) collective-permute-start(bf16[416,128]{1,0:T(8,128)(2,1)S(1)} %pass_on.1.half_b), channel_id=1, source_target_pairs={{0,1},{1,0},{2,3},{3,2},{4,5},{5,4},{6,7},{7,6},{8,9},{9,8},{10,11... | collective-permute-start | bytes 319496 | tf_op jit(solution)/shard_map/ppermute | solution.py:425
  20.7 2.9 %collective-permute-start.8 = (bf16[784,128]{1,0:T(8,128)(2,1)S(1)}, bf16[784,128]{1,0:T(8,128)(2,1)S(1)}, u32[]{:S(2)}, u32[]{:S(2)}) collective-permute-start(bf16[784,128]{1,0:T(8,128)(2,1)S(1)} %get-tuple-element.82.own), channel_id=1, source_target_pairs={{0,1},{1,0},{2,3},{3,2},{4,5},{5,4},{6,7},{7,6},{8,9},{9,8},{10,11... | collective-permute-start | bytes 602120 | tf_op jit(solution)/shard_map/ppermute | solution.py:442
  23.0 1.6 %collective-permute-start.7 = (bf16[784,128]{1,0:T(8,128)(2,1)S(1)}, bf16[784,128]{1,0:T(8,128)(2,1)S(1)}, u32[]{:S(2)}, u32[]{:S(2)}) collective-permute-start(bf16[784,128]{1,0:T(8,128)(2,1)S(1)} %incoming.1.part), channel_id=1, source_target_pairs={{0,1},{1,0},{2,3},{3,2},{4,5},{5,4},{6,7},{7,6},{8,9},{9,8},{10,11... | collective-permute-start | bytes 602120 | tf_op jit(solution)/shard_map/ppermute | solution.py:451

commit v4 on v3

--- a/solution.py
+++ b/solution.py
@@ -69,35 +69,36 @@
     return (jnp.tanh(both[:, :chan]) + 1.0) * both[:, chan:]
 
 
-def pack_kernel(n, rows, part, pair, mask, packed, halved, mask_v, sems):
-    core = lax.rem(lax.axis_index("ch"), 2)
+def pack_kernel(n, rows, pair, mask, packed, mask_v, sems):
     block, chan = pair.shape
-    start = pl.multiple_of(core * (block - part), 16)
     copies = [
         pltpu.make_async_copy(mask, mask_v, sems.at[0]),
         pltpu.make_async_copy(pair, packed.at[pl.ds(0, block)], sems.at[1]),
-        pltpu.make_async_copy(pair.at[pl.ds(start, part)], halved.at[pl.ds(0, part)], sems.at[2]),
     ]
     for copy in copies:
         copy.start()
     copies[0].wait()
-    masks = jnp.concatenate([mask_v[...].astype(F32), jnp.zeros((rows, chan - n), F32)], axis=1)
-    masks = jnp.concatenate([masks, jnp.zeros((MASK_ROWS - rows, chan), F32)], axis=0).astype(BF16)
-    packed[block : block + MASK_ROWS, :] = masks
-    halved[part : part + MASK_ROWS, :] = masks
+    wide = jnp.concatenate([mask_v[...].astype(F32), jnp.zeros((rows, chan - n), F32)], axis=1)
+    packed[block : block + MASK_ROWS, :] = jnp.concatenate(
+        [wide, jnp.zeros((MASK_ROWS - rows, chan), F32)], axis=0
+    ).astype(BF16)
     copies[1].wait()
-    copies[2].wait()
-
-
-def constants_kernel(chain_row, *refs):
-    count = (len(refs) - 3) // 2
+
+
+def constants_kernel(part, packed, chain_row, *refs):
+    count = (len(refs) - 4) // 2
     sources, outs = refs[:count], refs[count : 2 * count]
-    chains, row, sems = refs[2 * count :]
+    chains, halved, row, sems = refs[2 * count :]
     first = pltpu.make_async_copy(chain_row, row, sems.at[count])
     first.start()
     copies = [pltpu.make_async_copy(a, b, sems.at[i]) for i, (a, b) in enumerate(zip(sources, outs))]
     for copy in copies:
         copy.start()
+    core = lax.rem(lax.axis_index("ch"), 2)
+    block = packed.shape[0] - MASK_ROWS
+    start = pl.multiple_of(core * (block - part), 16)
+    halved[0:part, :] = packed[pl.ds(start, part), :]
+    halved[part : part + MASK_ROWS, :] = packed[block : block + MASK_ROWS, :]
     first.wait()
     ones = jnp.ones((1, chains.shape[1]), BF16)
     chains[...] = lax.dot_general(
@@ -363,7 +364,7 @@
             out_specs=tuple(vmem for _ in outs),
             scratch_shapes=[pltpu.VMEM(s, F32) for s in scratch],
             compiler_params=pltpu.CompilerParams(vmem_limit_bytes=32 * 1024 * 1024),
-            cost_estimate=pl.CostEstimate(flops=int(us * 1e9), bytes_accessed=0, transcendentals=0),
+            cost_estimate=pl.CostEstimate(flops=int(us * 1.2e9), bytes_accessed=0, transcendentals=0),
             name=name,
         )(*kept)
         for v in got:
@@ -374,32 +375,35 @@
     f32 = lambda count: pltpu.VMEM((count, chan), F32)
     bf16 = lambda count: pltpu.VMEM((count, chan), BF16)
 
-    packed, halved = pl.pallas_call(
-        functools.partial(pack_kernel, n, rows, part),
-        out_shape=(bf16(block + MASK_ROWS), bf16(part + MASK_ROWS)),
-        in_specs=[pl.BlockSpec(memory_space=pl.ANY)] * 2,
-        out_specs=(vmem, vmem),
-        scratch_shapes=[pltpu.VMEM((rows, n), jnp.int32), pltpu.SemaphoreType.DMA((3,))],
+    hbm = pl.BlockSpec(memory_space=pl.ANY)
+    (packed,) = pl.pallas_call(
+        functools.partial(pack_kernel, n, rows),
+        out_shape=(bf16(block + MASK_ROWS),),
+        in_specs=[hbm] * 2,
+        out_specs=(vmem,),
+        scratch_shapes=[pltpu.VMEM((rows, n), jnp.int32), pltpu.SemaphoreType.DMA((2,))],
         name="pack",
     )(*(pltpu.with_memory_space_constraint(v, pltpu.HBM) for v in (flat_pair, mask)))
     sources = (weights, pair_embed, in_gain, in_bias, gate_weight, out_gain, out_bias, out_weight)
     constants = pl.pallas_call(
-        constants_kernel,
-        out_shape=tuple(pltpu.VMEM(v.shape, v.dtype) for v in sources) + (pltpu.VMEM((n, chan), F32),),
-        in_specs=[pl.BlockSpec(memory_space=pl.ANY)] * (1 + len(sources)),
-        out_specs=tuple(vmem for _ in range(1 + len(sources))),
+        functools.partial(constants_kernel, part),
+        out_shape=tuple(pltpu.VMEM(v.shape, v.dtype) for v in sources) + (f32(n), bf16(part + MASK_ROWS)),
+        in_specs=[vmem] + [hbm] * (1 + len(sources)),
+        out_specs=(vmem,) * (2 + len(sources)),
         scratch_shapes=[pltpu.VMEM((1, n), jnp.int32), pltpu.SemaphoreType.DMA((1 + len(sources),))],
+        cost_estimate=pl.CostEstimate(flops=10**7, bytes_accessed=0, transcendentals=0),
         name="constants",
-    )(*(pltpu.with_memory_space_constraint(v, pltpu.HBM) for v in (chain_ids.reshape(1, n),) + sources))
-    in_vmem.update({id(v): v for v in (packed, halved) + tuple(constants)})
-    w_own, pair_embed, in_gain, in_bias, gate_weight, out_gain, out_bias, out_weight, chains = constants
+    )(
+        pltpu.with_memory_space_constraint(packed, pltpu.VMEM),
+        *(pltpu.with_memory_space_constraint(v, pltpu.HBM) for v in (chain_ids.reshape(1, n),) + sources),
+    )
+    in_vmem.update({id(v): v for v in (packed,) + tuple(constants)})
+    w_own, pair_embed, in_gain, in_bias, gate_weight, out_gain, out_bias, out_weight, chains, halved = constants
     packed_a = lax.ppermute(packed, both, first)
     half_b = lax.ppermute(halved, both, second)
     w_e = lax.ppermute(weights, "ch", cores)
     w_a = lax.ppermute(weights, "ch", chips)
     w_f = lax.ppermute(w_a, "ch", cores)
-    packed_e = lax.ppermute(packed_a, "ch", cores)
-
     def one_block(name, which, source):
         return call(
             functools.partial(lift_kernel, n, rows, which),
@@ -410,17 +414,18 @@
         )
 
     at_o = one_block("lift_own", lambda core: 0, packed)
-    at_a = one_block("lift_first", lambda core: 1 + core, packed_a)
     (w_all,) = call(weights_kernel, "weights", [bf16(4 * size)], [w_own, w_e, w_a, w_f], us=0.1)
-    at_e = one_block("lift_second", lambda core: 2 - core, packed_e)
 
     def project(name, lifted):
         sides = call(functools.partial(project_kernel, n, rows), name, [f32(block)] * 2, [lifted[3], w_all], us=0.6)
         return list(lifted[:3]) + list(sides)
 
-    at_o, at_a, at_e = (
-        project(name, v) for name, v in (("project_own", at_o), ("project_first", at_a), ("project_second", at_e))
-    )
+    (packed_a,) = call(pass_kernel, "pass_first", [bf16(block + MASK_ROWS)], [packed_a, at_o[0]], us=0.1)
+    at_o = project("project_own", at_o)
+    packed_e = lax.ppermute(packed_a, "ch", cores)
+    at_a = one_block("lift_first", lambda core: 1 + core, packed_a)
+    at_e = one_block("lift_second", lambda core: 2 - core, packed_e)
+    at_a, at_e = (project(name, v) for name, v in (("project_first", at_a), ("project_second", at_e)))
     (half_b,) = call(pass_kernel, "pass_on", [bf16(part + MASK_ROWS)], [half_b, at_e[4]], us=0.1)
     half_f = lax.ppermute(half_b, "ch", cores)
     at_early = call(

time: 26 us -> 25 us (0.962)
  the two profiles are of different devices: /device:TPU:31 before, /device:TPU:0 now
where the time goes in v4:
time: 25 us; the launch traced here: 24.8 us
  Pallas kernels  13.9 us (56%)
  starting transfers between devices  8.35 us (33%)
  waiting for transfers between devices  2.44 us (10%)
    pallas_call x14, Pallas kernels, call(): pl.pallas_call(kernel, out_shape=tuple(outs), in_specs=[vmem] * len(ins),...  11.8 us
    ppermute x1, starting transfers between devices, in_one_phase(): packed_a = lax.ppermute(packed, both, first)  3.09 us
    ppermute x1, starting transfers between devices, in_one_phase(): half_b = lax.ppermute(halved, both, second)  2.26 us
    ppermute x1, starting transfers between devices, in_one_phase(): w_a = lax.ppermute(weights, 'ch', chips)  1.49 us
    pallas_call x1, Pallas kernels, in_one_phase(): pl.pallas_call(functools.partial(constants_kernel, part), out_shape=tuple...  1.08 us
    ppermute x1, waiting for transfers between devices, in_one_phase(): half_b = lax.ppermute(halved, both, second)  0.99 us
    pallas_call x1, Pallas kernels, in_one_phase(): pl.pallas_call(functools.partial(pack_kernel, n, rows), out_shape=(bf16(b...  0.96 us
    ppermute x1, waiting for transfers between devices, in_one_phase(): part_n = lax.ppermute(part, 'ch', cores)  0.92 us
  transfers between devices with their start and end apart: 9, of which 3 were waited for; matrix products, arithmetic and copies ran while one was open for 0% of the time, Pallas kernels for 35%

profile of v4, /device:TPU:0, one launch (start us, length us, event | category | flops | bytes accessed | tf_op | source)
XLA Modules:
  0.0 24.8 jit_solution(11765678268716598578)
XLA Ops:
  0.0 1.0 %pack.1.packed = bf16[800,128]{1,0:T(8,128)(2,1)S(1)} custom-call(bf16[784,128]{1,0:T(8,128)(2,1)} %bitcast.5, s32[14,56]{1,0:T(8,128)} %mask.1), custom_call_target="tpu_custom_call" | custom-call | tf_op jit(solution)/shard_map/pack/pallas_call | solution.py:379
  1.0 3.1 %collective-permute-start.1 = (bf16[800,128]{1,0:T(8,128)(2,1)S(1)}, bf16[800,128]{1,0:T(8,128)(2,1)S(1)}, u32[]{:S(2)}, u32[]{:S(2)}) collective-permute-start(bf16[800,128]{1,0:T(8,128)(2,1)S(1)} %pack.1.packed), channel_id=1, source_target_pairs={{4,0},{9,1},{6,2},{11,3},{0,4},{13,5},{2,6},{15,7},{12,8},{1,9},{1... | collective-permute-start | bytes 614408 | tf_op jit(solution)/shard_map/ppermute | solution.py:402
  4.1 1.5 %collective-permute-start.4 = (bf16[256,128]{1,0:T(8,128)(2,1)}, bf16[256,128]{1,0:T(8,128)(2,1)S(1)}, u32[]{:S(2)}, u32[]{:S(2)}) collective-permute-start(bf16[256,128]{1,0:T(8,128)(2,1)} %bitcast.6), channel_id=1, source_target_pairs={{0,2},{1,3},{2,0},{3,1},{4,6},{5,7},{6,4},{7,5},{8,10},{9,11},{10,... | collective-permute-start | bytes 196616 | tf_op jit(solution)/shard_map/ppermute | solution.py:405
  5.6 0.3 %collective-permute-start.3 = (bf16[256,128]{1,0:T(8,128)(2,1)}, bf16[256,128]{1,0:T(8,128)(2,1)S(1)}, u32[]{:S(2)}, u32[]{:S(2)}) collective-permute-start(bf16[256,128]{1,0:T(8,128)(2,1)} %bitcast.7), channel_id=1, source_target_pairs={{0,1},{1,0},{2,3},{3,2},{4,5},{5,4},{6,7},{7,6},{8,9},{9,8},{10,11... | collective-permute-start | bytes 196616 | tf_op jit(solution)/shard_map/ppermute | solution.py:404
  5.8 1.1 %constants.1 = (bf16[256,128]{1,0:T(8,128)(2,1)S(1)}, f32[2,128]{1,0:T(2,128)S(1)}, f32[2,128]{1,0:T(2,128)S(1)}, f32[2,128]{1,0:T(2,128)S(1)}, bf16[2,128,128]{...) custom-call(bf16[800,128]{1,0:T(8,128)(2,1)S(1)} %pack.1.packed, ...), custom_call_target="tpu_custom_call" | custom-call | flops 10000000 | tf_op jit(solution)/shard_map/constants/pallas_call | solution.py:388
  6.9 2.3 %collective-permute-start = (bf16[416,128]{1,0:T(8,128)(2,1)S(1)}, bf16[416,128]{1,0:T(8,128)(2,1)S(1)}, u32[]{:S(2)}, u32[]{:S(2)}) collective-permute-start(bf16[416,128]{1,0:T(8,128)(2,1)S(1)} %get-tuple-element.44), channel_id=1, source_target_pairs={{12,0},{13,1},{14,2},{15,3},{8,4},{9,5},{10,6},{11,7},{4,8},{5,9},... | collective-permute-start | bytes 319496 | tf_op jit(solution)/shard_map/ppermute | solution.py:403
  9.2 0.2 collective-permute-start.5
  9.4 0.5 %lift_own.1 = (f32[784,128]{1,0:T(8,128)S(1)}, f32[784,128]{1,0:T(8,128)S(1)}, f32[784,128]{1,0:T(8,128)S(1)}, bf16[784,128]{1,0:T(8,128)(2,1)S(1)}) custom-call(bf16[800,128]{1,0:T(8,128)(2,1)S(1)} %pack.1.packed, f32[56,128]{1,0:T(8,128)S(1)} %get-tuple-element.45.chains, f32[2,128]{1,0:T(2,128)S(1)} %get-tuple-element.46.embed, ...), custom_call_target="tpu_custom_call" | custom-call | flops 960000000 | tf_op jit(solution)/shard_map/lift_own/pallas_call | solution.py:360
  9.9 0.5 %collective-permute-done.5.w_f = bf16[256,128]{1,0:T(8,128)(2,1)S(1)} collective-permute-done((bf16[256,128]{1,0:T(8,128)(2,1)S(1)}, bf16[256,128]{1,0:T(8,128)(2,1)S(1)}, u32[]{:S(2)}, u32[]{:S(2)}) %collective-permute-start.5) | collective-permute-done | bytes 65568 | tf_op jit(solution)/shard_map/ppermute | solution.py:406
  10.5 0.3 %collective-permute-start.2 = (bf16[800,128]{1,0:T(8,128)(2,1)S(1)}, bf16[800,128]{1,0:T(8,128)(2,1)S(1)}, u32[]{:S(2)}, u32[]{:S(2)}) collective-permute-start(bf16[800,128]{1,0:T(8,128)(2,1)S(1)} %pass_first.1.packed), channel_id=1, source_target_pairs={{0,1},{1,0},{2,3},{3,2},{4,5},{5,4},{6,7},{7,6},{8,9},{9,8},{10,11... | collective-permute-start | bytes 614408 | tf_op jit(solution)/shard_map/ppermute | solution.py:425
  10.8 0.4 %project_own.1 = (f32[784,128]{1,0:T(8,128)S(1)}, f32[784,128]{1,0:T(8,128)S(1)}) custom-call(bf16[784,128]{1,0:T(8,128)(2,1)S(1)} %get-tuple-element.65.zm_ref, bf16[1024,128]{1,0:T(8,128)(2,1)S(1)} %weights.1), custom_call_target="tpu_custom_call" | custom-call | flops 720000000 | tf_op jit(solution)/shard_map/project_own/pallas_call | solution.py:360
  11.2 0.5 %lift_first.1 = (f32[784,128]{1,0:T(8,128)S(1)}, f32[784,128]{1,0:T(8,128)S(1)}, f32[784,128]{1,0:T(8,128)S(1)}, bf16[784,128]{1,0:T(8,128)(2,1)S(1)}) custom-call(bf16[800,128]{1,0:T(8,128)(2,1)S(1)} %pass_first.1.packed, f32[56,128]{1,0:T(8,128)S(1)} %get-tuple-element.45.chains, f32[2,128]{1,0:T(2,128)S(1)} %get-tuple-element.46.embed, ...), custom_call_target="tpu_custom_call" | custom-call | flops 960000000 | tf_op jit(solution)/shard_map/lift_first/pallas_call | solution.py:360
  11.7 0.4 %project_first.1 = (f32[784,128]{1,0:T(8,128)S(1)}, f32[784,128]{1,0:T(8,128)S(1)}) custom-call(bf16[784,128]{1,0:T(8,128)(2,1)S(1)} %get-tuple-element.67.zm_ref, bf16[1024,128]{1,0:T(8,128)(2,1)S(1)} %weights.1), custom_call_target="tpu_custom_call" | custom-call | flops 720000000 | tf_op jit(solution)/shard_map/project_first/pallas_call | solution.py:360
  12.1 0.5 %lift_second.1 = (f32[784,128]{1,0:T(8,128)S(1)}, f32[784,128]{1,0:T(8,128)S(1)}, f32[784,128]{1,0:T(8,128)S(1)}, bf16[784,128]{1,0:T(8,128)(2,1)S(1)}) custom-call(bf16[800,128]{1,0:T(8,128)(2,1)S(1)} %collective-permute-done.2.packed, f32[56,128]{1,0:T(8,128)S(1)} %get-tuple-element.45.chains, f32[2,128]{1,0:T(2,128)S(1)} %get-tuple-element.46.embed, ...), custom_call_target="tpu_custom_call" | custom-call | flops 960000000 | tf_op jit(solution)/shard_map/lift_second/pallas_call | solution.py:360
  12.6 0.4 %project_second.1 = (f32[784,128]{1,0:T(8,128)S(1)}, f32[784,128]{1,0:T(8,128)S(1)}) custom-call(bf16[784,128]{1,0:T(8,128)(2,1)S(1)} %get-tuple-element.51.zm_ref, bf16[1024,128]{1,0:T(8,128)(2,1)S(1)} %weights.1), custom_call_target="tpu_custom_call" | custom-call | flops 720000000 | tf_op jit(solution)/shard_map/project_second/pallas_call | solution.py:360
  13.0 1.0 %collective-permute-done.value = bf16[416,128]{1,0:T(8,128)(2,1)S(1)} collective-permute-done((bf16[416,128]{1,0:T(8,128)(2,1)S(1)}, bf16[416,128]{1,0:T(8,128)(2,1)S(1)}, u32[]{:S(2)}, u32[]{:S(2)}) %collective-permute-start) | collective-permute-done | bytes 106528 | tf_op jit(solution)/shard_map/ppermute | solution.py:403
  14.1 2.2 %early.1 = (f32[1176,128]{1,0:T(8,128)S(1)}, f32[3136,128]{1,0:T(8,128)S(1)}, f32[1176,128]{1,0:T(8,128)S(1)}, f32[1176,128]{1,0:T(8,128)S(1)}, f32[1176,128]{1,0:T(8,128)S(1)}, /*index=5*/f32[1176,128]{1,0:T(8,128)S(1)}) custom-call(f32[784,128]{1,0:T(8,128)S(1)} %get-tuple-element.50.after.z_o, f32[784,128]{1,0:T(8,128)S(1)} %get-tuple-element.57.z_a, ...), custom_call_target="tpu_custom_call" | custom-call | flops 2400000000 | tf_op jit(solution)/shard_map/early/pallas_call | solution.py:360
  16.3 3.1 %late.1 = (bf16[1568,128]{1,0:T(8,128)(2,1)S(1)}, bf16[784,128]{1,0:T(8,128)(2,1)S(1)}, f32[1568,128]{1,0:T(8,128)S(1)}) custom-call(bf16[416,128]{1,0:T(8,128)(2,1)S(1)} %pass_on.1.half_b, bf16[416,128]{1,0:T(8,128)(2,1)S(1)} %collective-permute-done.6.half_f, bf16[1024,128]{1,0:T(8,128)(2,1)S(1)} %weights.1, f32[56,128]{1,0:T(8,128)S(1)} %get-tuple-element.45.chains, ...), custom_call_target="tpu_custom_call" | custom-call | flops 4800000000 | tf_op jit(solution)/shard_map/late/pallas_call | solution.py:360
  19.4 0.5 %collective-permute-start.8 = (bf16[784,128]{1,0:T(8,128)(2,1)S(1)}, bf16[784,128]{1,0:T(8,128)(2,1)S(1)}, u32[]{:S(2)}, u32[]{:S(2)}) collective-permute-start(bf16[784,128]{1,0:T(8,128)(2,1)S(1)} %get-tuple-element.80.own), channel_id=1, source_target_pairs={{0,1},{1,0},{2,3},{3,2},{4,5},{5,4},{6,7},{7,6},{8,9},{9,8},{10,11... | collective-permute-start | bytes 602120 | tf_op jit(solution)/shard_map/ppermute | solution.py:447
  20.0 2.2 %incoming.1.part = bf16[784,128]{1,0:T(8,128)(2,1)S(1)} custom-call(bf16[1568,128]{1,0:T(8,128)(2,1)S(1)} %get-tuple-element.78.z1, f32[1568,128]{1,0:T(8,128)S(1)} %get-tuple-element.79.masks, bf16[1024,128]{1,0:T(8,128)(2,1)S(1)} %weights.1, f32[2,128]{1,0:T(2,128)S(1)} %get-tuple-element.47.in_gain, f32[2,128]{1,0:T(2,128)S(1)} %get-tuple-element.48.in_bias), custom_call_target="tpu_custom_call" | custom-call | flops 3600000000 | tf_op jit(solution)/shard_map/incoming/pallas_call | solution.py:360
  22.2 0.1 collective-permute-start.7
  22.3 0.5 %gate.1 = (f32[784,128]{1,0:T(8,128)S(1)}, f32[784,128]{1,0:T(8,128)S(1)}) custom-call(bf16[784,128]{1,0:T(8,128)(2,1)S(1)} %get-tuple-element.80.own, bf16[784,128]{1,0:T(8,128)(2,1)S(1)} %collective-permute-done.8.received, f32[2,128]{1,0:T(2,128)S(1)} %get-tuple-element.47.in_gain, f32[2,128]{1,0:T(2,128)S(1)} %get-tuple-element.48.in_bias, ...), custom_call_target="tpu_custom_call" | custom-call | flops 1200000000 | tf_op jit(solution)/shard_map/gate/pallas_call | solution.py:360
  22.8 0.9 %collective-permute-done.7.received = bf16[784,128]{1,0:T(8,128)(2,1)S(1)} collective-permute-done((bf16[784,128]{1,0:T(8,128)(2,1)S(1)}, bf16[784,128]{1,0:T(8,128)(2,1)S(1)}, u32[]{:S(2)}, u32[]{:S(2)}) %collective-permute-start.7) | collective-permute-done | bytes 200736 | tf_op jit(solution)/shard_map/ppermute | solution.py:456
  23.7 1.1 %last.1 = bf16[14,56,128]{2,1,0:T(8,128)(2,1)} custom-call(bf16[784,128]{1,0:T(8,128)(2,1)S(1)} %incoming.1.part, bf16[784,128]{1,0:T(8,128)(2,1)S(1)} %collective-permute-done.7.received, f32[784,128]{1,0:T(8,128)S(1)} %get-tuple-element.81.z_ref, f32[784,128]{1,0:T(8,128)S(1)} %get-tuple-element.82.g_ref, f32[2,128]{1,0:T(2,128)S(1)} %get-tuple-element.54.out_gain, ...), custom_call_target="tpu_custom_call" | custom-call | flops 1200000000 | tf_op jit(solution)/shard_map/last/pallas_call | solution.py:360
  (10 shorter events, 0.2 us)
Async XLA Ops:
  1.0 9.5 %collective-permute-start.1 = (bf16[800,128]{1,0:T(8,128)(2,1)S(1)}, bf16[800,128]{1,0:T(8,128)(2,1)S(1)}, u32[]{:S(2)}, u32[]{:S(2)}) collective-permute-start(bf16[800,128]{1,0:T(8,128)(2,1)S(1)} %pack.1.packed), channel_id=1, source_target_pairs={{4,0},{9,1},{6,2},{11,3},{0,4},{13,5},{2,6},{15,7},{12,8},{1,9},{1... | collective-permute-start | bytes 614408 | tf_op jit(solution)/shard_map/ppermute | solution.py:402
  4.1 5.1 %collective-permute-start.4 = (bf16[256,128]{1,0:T(8,128)(2,1)}, bf16[256,128]{1,0:T(8,128)(2,1)S(1)}, u32[]{:S(2)}, u32[]{:S(2)}) collective-permute-start(bf16[256,128]{1,0:T(8,128)(2,1)} %bitcast.6), channel_id=1, source_target_pairs={{0,2},{1,3},{2,0},{3,1},{4,6},{5,7},{6,4},{7,5},{8,10},{9,11},{10,... | collective-permute-start | bytes 196616 | tf_op jit(solution)/shard_map/ppermute | solution.py:405
  5.6 4.4 %collective-permute-start.3 = (bf16[256,128]{1,0:T(8,128)(2,1)}, bf16[256,128]{1,0:T(8,128)(2,1)S(1)}, u32[]{:S(2)}, u32[]{:S(2)}) collective-permute-start(bf16[256,128]{1,0:T(8,128)(2,1)} %bitcast.7), channel_id=1, source_target_pairs={{0,1},{1,0},{2,3},{3,2},{4,5},{5,4},{6,7},{7,6},{8,9},{9,8},{10,11... | collective-permute-start | bytes 196616 | tf_op jit(solution)/shard_map/ppermute | solution.py:404
  6.9 7.1 %collective-permute-start = (bf16[416,128]{1,0:T(8,128)(2,1)S(1)}, bf16[416,128]{1,0:T(8,128)(2,1)S(1)}, u32[]{:S(2)}, u32[]{:S(2)}) collective-permute-start(bf16[416,128]{1,0:T(8,128)(2,1)S(1)} %get-tuple-element.44), channel_id=1, source_target_pairs={{12,0},{13,1},{14,2},{15,3},{8,4},{9,5},{10,6},{11,7},{4,8},{5,9},... | collective-permute-start | bytes 319496 | tf_op jit(solution)/shard_map/ppermute | solution.py:403
  9.2 1.3 %collective-permute-start.5 = (bf16[256,128]{1,0:T(8,128)(2,1)S(1)}, bf16[256,128]{1,0:T(8,128)(2,1)S(1)}, u32[]{:S(2)}, u32[]{:S(2)}) collective-permute-start(bf16[256,128]{1,0:T(8,128)(2,1)S(1)} %collective-permute-done.4.w_a), channel_id=1, source_target_pairs={{0,1},{1,0},{2,3},{3,2},{4,5},{5,4},{6,7},{7,6},{8,9},{9,8},{10,11... | collective-permute-start | bytes 196616 | tf_op jit(solution)/shard_map/ppermute | solution.py:406
  10.5 1.6 %collective-permute-start.2 = (bf16[800,128]{1,0:T(8,128)(2,1)S(1)}, bf16[800,128]{1,0:T(8,128)(2,1)S(1)}, u32[]{:S(2)}, u32[]{:S(2)}) collective-permute-start(bf16[800,128]{1,0:T(8,128)(2,1)S(1)} %pass_first.1.packed), channel_id=1, source_target_pairs={{0,1},{1,0},{2,3},{3,2},{4,5},{5,4},{6,7},{7,6},{8,9},{9,8},{10,11... | collective-permute-start | bytes 614408 | tf_op jit(solution)/shard_map/ppermute | solution.py:425
  14.0 2.3 %collective-permute-start.6 = (bf16[416,128]{1,0:T(8,128)(2,1)S(1)}, bf16[416,128]{1,0:T(8,128)(2,1)S(1)}, u32[]{:S(2)}, u32[]{:S(2)}) collective-permute-start(bf16[416,128]{1,0:T(8,128)(2,1)S(1)} %pass_on.1.half_b), channel_id=1, source_target_pairs={{0,1},{1,0},{2,3},{3,2},{4,5},{5,4},{6,7},{7,6},{8,9},{9,8},{10,11... | collective-permute-start | bytes 319496 | tf_op jit(solution)/shard_map/ppermute | solution.py:430
  19.4 2.9 %collective-permute-start.8 = (bf16[784,128]{1,0:T(8,128)(2,1)S(1)}, bf16[784,128]{1,0:T(8,128)(2,1)S(1)}, u32[]{:S(2)}, u32[]{:S(2)}) collective-permute-start(bf16[784,128]{1,0:T(8,128)(2,1)S(1)} %get-tuple-element.80.own), channel_id=1, source_target_pairs={{0,1},{1,0},{2,3},{3,2},{4,5},{5,4},{6,7},{7,6},{8,9},{9,8},{10,11... | collective-permute-start | bytes 602120 | tf_op jit(solution)/shard_map/ppermute | solution.py:447
  22.2 1.5 %collective-permute-start.7 = (bf16[784,128]{1,0:T(8,128)(2,1)S(1)}, bf16[784,128]{1,0:T(8,128)(2,1)S(1)}, u32[]{:S(2)}, u32[]{:S(2)}) collective-permute-start(bf16[784,128]{1,0:T(8,128)(2,1)S(1)} %incoming.1.part), channel_id=1, source_target_pairs={{0,1},{1,0},{2,3},{3,2},{4,5},{5,4},{6,7},{7,6},{8,9},{9,8},{10,11... | collective-permute-start | bytes 602120 | tf_op jit(solution)/shard_map/ppermute | solution.py:456

commit v5 on v4

--- a/solution.py
+++ b/solution.py
@@ -139,7 +139,7 @@
         )
         z_ref[at, :] = z
         m_ref[at, :] = spread
-        g_ref[at, :] = jax.nn.sigmoid(nn_dot(zn, gate_w[0]))
+        g_ref[at, :] = half_sigmoid(0.5 * nn_dot(zn, gate_w[0]))
         zm_ref[at, :] = zn * spread.astype(BF16)
 
 
@@ -152,35 +152,32 @@
         right_ref[at, :] = gated_side(zm, weights, 0, 1, chan)
 
 
-def tiles_of(n, count, left_at, left_ref, left_step, steps, right_ref, right_at, width, right_step):
+def tiles_of(lefts, steps, right_ref, right_at, width, right_step):
+    chan = right_ref.shape[1]
+
     def body(k, accs):
         right = right_ref[pl.ds(pl.multiple_of(right_at + k * right_step, 8), width), :]
-        return tuple(acc + left_ref[pl.ds(left_at(i) + k * left_step, 1), :] * right for i, acc in enumerate(accs))
-
-    chan = left_ref.shape[1]
-    zeros = tuple(jnp.zeros((width, chan), F32) for _ in range(count))
-    return lax.fori_loop(0, steps, body, zeros, unroll=min(8, steps))
+        return tuple(acc + ref[pl.ds(at + k * step, 1), :] * right for acc, (ref, at, step) in zip(accs, lefts))
+
+    zeros = tuple(jnp.zeros((width, chan), F32) for _ in lefts)
+    return lax.fori_loop(0, steps, body, zeros, unroll=min(28, steps))
 
 
 def early_kernel(
-    n, rows, early,
-    z_o, z_a, z_e, g_o, g_a, g_e, m_o, m_a, m_e, left_o, left_a, left_e, right_o, right_a, right_e,
-    x_ref, right_ref, z_ref, g_ref, m_ref, left_ref,
+    n, rows, early, left_o, left_a, left_e, right_o, right_a, right_e, x_ref, right_ref, left_ref,
 ):
     core = lax.rem(lax.axis_index("ch"), 2)
     block, mid = rows * n, rows // 2 * n
 
     @pl.when(core == 0)
     def _():
-        for out, o, a in ((z_ref, z_o, z_a), (g_ref, g_o, g_a), (m_ref, m_o, m_a), (left_ref, left_o, left_a)):
-            out[0:block, :] = o[...]
-            out[block : block + mid, :] = a[0:mid, :]
+        left_ref[0:block, :] = left_o[...]
+        left_ref[block : block + mid, :] = left_a[0:mid, :]
 
     @pl.when(core == 1)
     def _():
-        for out, a, e in ((z_ref, z_a, z_e), (g_ref, g_a, g_e), (m_ref, m_a, m_e), (left_ref, left_a, left_e)):
-            out[0:block, :] = a[...]
-            out[block : block + mid, :] = e[mid:block, :]
+        left_ref[0:block, :] = left_a[...]
+        left_ref[block : block + mid, :] = left_e[mid:block, :]
 
     for j in range(rows):
         rows_of_j = slice(j * n, (j + 1) * n)
@@ -192,7 +189,7 @@
 
     def some(t, _):
         first = t * group * n
-        accs = tiles_of(n, group, lambda i: first + i * n, left_ref, 1, n, right_ref, 0, early, n)
+        accs = tiles_of([(left_ref, first + i * n, 1) for i in range(group)], n, right_ref, 0, early, n)
         for i, acc in enumerate(accs):
             x_ref[pl.ds(pl.multiple_of(first + i * n, 8), early), :] = acc
         return 0
@@ -203,9 +200,9 @@
 def late_kernel(
     n, rows, part, early,
     half_b, half_f, weights, chains, embed, in_gain, in_bias, gate_w, out_gain, out_bias, out_w,
-    x_in, right_in, z_in, g_in, m_in, left_in,
+    x_in, right_in, left_in, z_o, z_a, z_e, g_o, g_a, g_e,
     z1_ref, own_ref, m_ref,
-    x_ref, late_ref, left_ref, z_ref, g_ref, zn_ref, mf_ref, zf_ref,
+    x_ref, late_ref, left_ref, zn_ref, mf_ref, zf_ref,
 ):
     r = lax.axis_index("row")
     core = lax.rem(lax.axis_index("ch"), 2)
@@ -242,46 +239,47 @@
         zn_ref[at, :] = zn.astype(F32)
 
     own = pl.ds(pl.multiple_of(core * mid, 8), mid)
-    tail = pl.ds(block + mid, mid)
     zn = zn_ref[own, :].astype(BF16)
     spread = mf_ref[own, :]
-    left_ref[tail, :] = gated_side(zn * spread.astype(BF16), weights, 0, 0, chan)
-    z_ref[tail, :] = zf_ref[own, :]
-    g_ref[tail, :] = jax.nn.sigmoid(nn_dot(zn, gate_w[0]))
-    m_ref[tail, :] = spread
-    head = pl.ds(0, block + mid)
-    left_ref[head, :] = left_in[...]
-    z_ref[head, :] = z_in[...]
-    g_ref[head, :] = g_in[...]
-    m_ref[head, :] = m_in[...]
+    left_ref[...] = gated_side(zn * spread.astype(BF16), weights, 0, 0, chan)
+    m_ref[...] = spread
 
     group = rows // 2
-    x_ref[head, :] = x_in[...]
-    for i, acc in enumerate(
-        tiles_of(n, group, lambda i: block + mid + i * n, left_ref, 1, n, right_in, 0, early, n)
-    ):
-        x_ref[pl.ds(block + mid + i * n, early), :] = acc
+    head = block + mid
+    x_ref[0:head, :] = x_in[...]
+    tail_lefts = [(left_ref, i * n, 1) for i in range(group)]
+    for i, acc in enumerate(tiles_of(tail_lefts, n, right_in, 0, early, n)):
+        x_ref[head + i * n : head + i * n + early, :] = acc
+    lefts = [(left_in, i * n, 1) for i in range(3 * group)] + tail_lefts
     for t in range(2):
-        for i, acc in enumerate(
-            tiles_of(n, rows, lambda i: t * block + i * n, left_ref, 1, n, late_ref, 0, late, late)
-        ):
-            x_ref[pl.ds(t * block + i * n + early, late), :] = acc
-
-    def ordered(first, count):
-        out = []
-        for i in range(first, first + count):
-            for b in range(4):
-                out.append(x_ref[pl.ds(i * n + (r ^ b) * rows, rows), :])
-        return jnp.concatenate(out, axis=0)
-
-    for first, count in pieces(2 * rows, 8):
-        at = pl.ds(first * n, count * n)
-        update = hidden_update(ordered(first, count), out_gain[0:1, :], out_bias[0:1, :], out_w[0])
-        z1 = (z_ref[at, :] + g_ref[at, :] * update).astype(BF16)
-        z1_ref[at, :] = z1
-        own_count = max(0, min(count, rows - first))
-        if own_count:
-            own_ref[pl.ds(first * n, own_count * n), :] = z1[: own_count * n]
+        for i, acc in enumerate(tiles_of(lefts[t * rows : (t + 1) * rows], n, late_ref, 0, late, late)):
+            row = t * block + i * n + early
+            x_ref[row : row + late, :] = acc
+
+    def finish(first, count, z, gate):
+        x = jnp.concatenate(
+            [
+                x_ref[pl.ds(i * n + (r ^ b) * rows, rows), :]
+                for i in range(first, first + count)
+                for b in range(4)
+            ],
+            axis=0,
+        )
+        update = hidden_update(x, out_gain[0:1, :], out_bias[0:1, :], out_w[0])
+        z1 = (z + gate * update).astype(BF16)
+        z1_ref[first * n : (first + count) * n, :] = z1.astype(F32)
+        return z1
+
+    for first, count in pieces(rows, 8):
+        at = slice(first * n, (first + count) * n)
+        own_ref[at, :] = finish(
+            first, count, jnp.where(even, z_o[at, :], z_a[at, :]), jnp.where(even, g_o[at, :], g_a[at, :])
+        )
+    finish(
+        rows, group,
+        jnp.where(even, z_a[0:mid, :], z_e[mid:block, :]), jnp.where(even, g_a[0:mid, :], g_e[mid:block, :]),
+    )
+    finish(rows + group, group, zf_ref[own, :], half_sigmoid(0.5 * nn_dot(zn, gate_w[0])))
 
 
 def hidden_update(x, gain, bias, weight):
@@ -291,27 +289,33 @@
     return nn_dot(((x - mean) * scale * gain + bias).astype(BF16), weight)
 
 
-def incoming_kernel(n, rows, z1, masks, weights, in_gain, in_bias, part, left_ref, right_ref, sums_ref):
+def incoming_kernel(
+    n, rows, z1, m_o, m_a, m_e, m_f, weights, in_gain, in_bias, part, left_ref, right_ref, sums_ref
+):
     r = lax.axis_index("row")
+    even = lax.rem(lax.axis_index("ch"), 2) == 0
     chan = z1.shape[1]
-    for first, count in pieces(2 * rows, 8):
-        at = pl.ds(first * n, count * n)
-        zn = normalize(z1[at, :].astype(F32), in_gain[1:2, :], in_bias[1:2, :])
-        zm = zn * masks[at, :].astype(BF16)
+    block, mid = rows * n, rows // 2 * n
+    group = rows // 2
+    kept = [
+        (first, count, lambda at: jnp.where(even, m_o[at, :], m_a[at, :])) for first, count in pieces(rows, 8)
+    ]
+    kept.append((rows, group, lambda at: jnp.where(even, m_a[0:mid, :], m_e[mid:block, :])))
+    kept.append((rows + group, group, lambda at: m_f[...]))
+    for first, count, masks in kept:
+        at = slice(first * n, (first + count) * n)
+        zn = normalize(z1[at, :], in_gain[1:2, :], in_bias[1:2, :])
+        zm = zn * masks(at).astype(BF16)
         left_ref[at, :] = gated_side(zm, weights, 1, 0, chan)
         right_ref[at, :] = gated_side(zm, weights, 1, 1, chan)
-    group = rows // 2
     wide = (n // 8 + 1) // 2 * 8
     for t in range(2):
         start = r * rows + t * group
-        sums = [
-            tiles_of(n, group, lambda i: start + i, left_ref, n, 2 * rows, right_ref, at, width, n)
-            for at, width in ((0, wide), (wide, n - wide))
-        ]
-        for i in range(group):
-            for (at, width), accs in zip(((0, wide), (wide, n - wide)), sums):
-                left = (t * group + i) * n + at
-                sums_ref[left : left + width, :] = accs[i]
+        for at, width in ((0, wide), (wide, n - wide)):
+            accs = tiles_of([(left_ref, start + i, n) for i in range(group)], 2 * rows, right_ref, at, width, n)
+            for i, acc in enumerate(accs):
+                row = (t * group + i) * n + at
+                sums_ref[row : row + width, :] = acc
     part[...] = sums_ref[...].astype(BF16)
 
 
@@ -320,7 +324,7 @@
     z = jnp.where(even, own[...], received[...]).astype(F32)
     z_ref[...] = z
     zn = normalize(z, in_gain[1:2, :], in_bias[1:2, :])
-    g_ref[...] = jax.nn.sigmoid(nn_dot(zn, gate_w[1]))
+    g_ref[...] = half_sigmoid(0.5 * nn_dot(zn, gate_w[1]))
 
 
 def last_kernel(n, rows, part, received, z_ref, g_ref, out_gain, out_bias, out_w, result):
@@ -428,20 +432,21 @@
     at_a, at_e = (project(name, v) for name, v in (("project_first", at_a), ("project_second", at_e)))
     (half_b,) = call(pass_kernel, "pass_on", [bf16(part + MASK_ROWS)], [half_b, at_e[4]], us=0.1)
     half_f = lax.ppermute(half_b, "ch", cores)
-    at_early = call(
+    x, right, left = call(
         functools.partial(early_kernel, n, rows, early),
         "early",
-        [f32(block + mid), f32(n * n)] + [f32(block + mid)] * 4,
-        [v for three in zip(at_o, at_a, at_e) for v in three],
+        [f32(block + mid), f32(n * n), f32(block + mid)],
+        [at_o[3], at_a[3], at_e[3], at_o[4], at_a[4], at_e[4]],
         us=2.0,
     )
-    z1, own, masks = call(
+    z1, own, mask_f = call(
         functools.partial(late_kernel, n, rows, part, early),
         "late",
-        [bf16(2 * block), bf16(block), f32(2 * block)],
+        [f32(2 * block), bf16(block), f32(mid)],
         [half_b, half_f, w_all, chains, pair_embed, in_gain, in_bias, gate_weight, out_gain, out_bias, out_weight]
-        + list(at_early),
-        [(2 * block, chan), (n * (n - early), chan)] + [(2 * block, chan)] * 3 + [(block, chan)] * 3,
+        + [x, right, left]
+        + [v[at] for at in (0, 1) for v in (at_o, at_a, at_e)],
+        [(2 * block, chan), (n * (n - early), chan), (mid, chan)] + [(block, chan)] * 3,
         us=4.0,
     )
     own_n = lax.ppermute(own, "ch", cores)
@@ -449,7 +454,7 @@
         functools.partial(incoming_kernel, n, rows),
         "incoming",
         [bf16(block)],
-        [z1, masks, w_all, in_gain, in_bias],
+        [z1, at_o[2], at_a[2], at_e[2], mask_f, w_all, in_gain, in_bias],
         scratch=[(2 * block, chan)] * 2 + [(block, chan)],
         us=3.0,
     )

time: 25 us -> 24.3 us (0.972)
  Pallas kernels: 13.9 us -> 13.1 us
    pallas_call x14, Pallas kernels: 11.8 us -> 11.1 us  [call(): pl.pallas_call(kernel, out_shape=tuple(outs), in_specs=[vmem] * len(ins),...]
  transfers between devices with their start and end apart: 9 -> 9, of which waited for: 3 -> 3; matrix products, arithmetic and copies ran while one was open for 0% -> 0% of each run, Pallas kernels for 35% -> 34%
where the time goes in v5:
time: 24.3 us; the launch traced here: 24.1 us
  Pallas kernels  13.1 us (54%)
  starting transfers between devices  8.36 us (34%)
  waiting for transfers between devices  2.44 us (10%)
    pallas_call x14, Pallas kernels, call(): pl.pallas_call(kernel, out_shape=tuple(outs), in_specs=[vmem] * len(ins),...  11.1 us
    ppermute x1, starting transfers between devices, in_one_phase(): packed_a = lax.ppermute(packed, both, first)  3.09 us
    ppermute x1, starting transfers between devices, in_one_phase(): half_b = lax.ppermute(halved, both, second)  2.26 us
    ppermute x1, starting transfers between devices, in_one_phase(): w_a = lax.ppermute(weights, 'ch', chips)  1.49 us
    pallas_call x1, Pallas kernels, in_one_phase(): pl.pallas_call(functools.partial(constants_kernel, part), out_shape=tuple...  1.08 us
    ppermute x1, waiting for transfers between devices, in_one_phase(): half_b = lax.ppermute(halved, both, second)  0.98 us
    pallas_call x1, Pallas kernels, in_one_phase(): pl.pallas_call(functools.partial(pack_kernel, n, rows), out_shape=(bf16(b...  0.96 us
    ppermute x1, waiting for transfers between devices, in_one_phase(): part_n = lax.ppermute(part, 'ch', cores)  0.92 us
  transfers between devices with their start and end apart: 9, of which 3 were waited for; matrix products, arithmetic and copies ran while one was open for 0% of the time, Pallas kernels for 34%

profile of v5, /device:TPU:0, one launch (start us, length us, event | category | flops | bytes accessed | tf_op | source)
XLA Modules:
  0.0 24.1 jit_solution(2941484156682753935)
XLA Ops:
  0.0 1.0 %pack.1.packed = bf16[800,128]{1,0:T(8,128)(2,1)S(1)} custom-call(bf16[784,128]{1,0:T(8,128)(2,1)} %bitcast.5, s32[14,56]{1,0:T(8,128)} %mask.1), custom_call_target="tpu_custom_call" | custom-call | tf_op jit(solution)/shard_map/pack/pallas_call | solution.py:383
  1.0 3.1 %collective-permute-start.1 = (bf16[800,128]{1,0:T(8,128)(2,1)S(1)}, bf16[800,128]{1,0:T(8,128)(2,1)S(1)}, u32[]{:S(2)}, u32[]{:S(2)}) collective-permute-start(bf16[800,128]{1,0:T(8,128)(2,1)S(1)} %pack.1.packed), channel_id=1, source_target_pairs={{4,0},{9,1},{6,2},{11,3},{0,4},{13,5},{2,6},{15,7},{12,8},{1,9},{1... | collective-permute-start | bytes 614408 | tf_op jit(solution)/shard_map/ppermute | solution.py:406
  4.1 1.5 %collective-permute-start.4 = (bf16[256,128]{1,0:T(8,128)(2,1)}, bf16[256,128]{1,0:T(8,128)(2,1)S(1)}, u32[]{:S(2)}, u32[]{:S(2)}) collective-permute-start(bf16[256,128]{1,0:T(8,128)(2,1)} %bitcast.6), channel_id=1, source_target_pairs={{0,2},{1,3},{2,0},{3,1},{4,6},{5,7},{6,4},{7,5},{8,10},{9,11},{10,... | collective-permute-start | bytes 196616 | tf_op jit(solution)/shard_map/ppermute | solution.py:409
  5.6 0.3 %collective-permute-start.3 = (bf16[256,128]{1,0:T(8,128)(2,1)}, bf16[256,128]{1,0:T(8,128)(2,1)S(1)}, u32[]{:S(2)}, u32[]{:S(2)}) collective-permute-start(bf16[256,128]{1,0:T(8,128)(2,1)} %bitcast.7), channel_id=1, source_target_pairs={{0,1},{1,0},{2,3},{3,2},{4,5},{5,4},{6,7},{7,6},{8,9},{9,8},{10,11... | collective-permute-start | bytes 196616 | tf_op jit(solution)/shard_map/ppermute | solution.py:408
  5.8 1.1 %constants.1 = (bf16[256,128]{1,0:T(8,128)(2,1)S(1)}, f32[2,128]{1,0:T(2,128)S(1)}, f32[2,128]{1,0:T(2,128)S(1)}, f32[2,128]{1,0:T(2,128)S(1)}, bf16[2,128,128]{...) custom-call(bf16[800,128]{1,0:T(8,128)(2,1)S(1)} %pack.1.packed, ...), custom_call_target="tpu_custom_call" | custom-call | flops 10000000 | tf_op jit(solution)/shard_map/constants/pallas_call | solution.py:392
  6.9 2.3 %collective-permute-start = (bf16[416,128]{1,0:T(8,128)(2,1)S(1)}, bf16[416,128]{1,0:T(8,128)(2,1)S(1)}, u32[]{:S(2)}, u32[]{:S(2)}) collective-permute-start(bf16[416,128]{1,0:T(8,128)(2,1)S(1)} %get-tuple-element.41), channel_id=1, source_target_pairs={{12,0},{13,1},{14,2},{15,3},{8,4},{9,5},{10,6},{11,7},{4,8},{5,9},... | collective-permute-start | bytes 319496 | tf_op jit(solution)/shard_map/ppermute | solution.py:407
  9.2 0.2 collective-permute-start.5
  9.4 0.5 %lift_own.1 = (f32[784,128]{1,0:T(8,128)S(1)}, f32[784,128]{1,0:T(8,128)S(1)}, f32[784,128]{1,0:T(8,128)S(1)}, bf16[784,128]{1,0:T(8,128)(2,1)S(1)}) custom-call(bf16[800,128]{1,0:T(8,128)(2,1)S(1)} %pack.1.packed, f32[56,128]{1,0:T(8,128)S(1)} %get-tuple-element.42.chains, f32[2,128]{1,0:T(2,128)S(1)} %get-tuple-element.43.embed, ...), custom_call_target="tpu_custom_call" | custom-call | flops 960000000 | tf_op jit(solution)/shard_map/lift_own/pallas_call | solution.py:364
  9.9 0.5 %collective-permute-done.5.w_f = bf16[256,128]{1,0:T(8,128)(2,1)S(1)} collective-permute-done((bf16[256,128]{1,0:T(8,128)(2,1)S(1)}, bf16[256,128]{1,0:T(8,128)(2,1)S(1)}, u32[]{:S(2)}, u32[]{:S(2)}) %collective-permute-start.5) | collective-permute-done | bytes 65568 | tf_op jit(solution)/shard_map/ppermute | solution.py:410
  10.5 0.3 %collective-permute-start.2 = (bf16[800,128]{1,0:T(8,128)(2,1)S(1)}, bf16[800,128]{1,0:T(8,128)(2,1)S(1)}, u32[]{:S(2)}, u32[]{:S(2)}) collective-permute-start(bf16[800,128]{1,0:T(8,128)(2,1)S(1)} %pass_first.1.packed), channel_id=1, source_target_pairs={{0,1},{1,0},{2,3},{3,2},{4,5},{5,4},{6,7},{7,6},{8,9},{9,8},{10,11... | collective-permute-start | bytes 614408 | tf_op jit(solution)/shard_map/ppermute | solution.py:429
  10.8 0.4 %project_own.1 = (f32[784,128]{1,0:T(8,128)S(1)}, f32[784,128]{1,0:T(8,128)S(1)}) custom-call(bf16[784,128]{1,0:T(8,128)(2,1)S(1)} %get-tuple-element.54.zm_ref, bf16[1024,128]{1,0:T(8,128)(2,1)S(1)} %weights.1), custom_call_target="tpu_custom_call" | custom-call | flops 720000000 | tf_op jit(solution)/shard_map/project_own/pallas_call | solution.py:364
  11.2 0.5 %lift_first.1 = (f32[784,128]{1,0:T(8,128)S(1)}, f32[784,128]{1,0:T(8,128)S(1)}, f32[784,128]{1,0:T(8,128)S(1)}, bf16[784,128]{1,0:T(8,128)(2,1)S(1)}) custom-call(bf16[800,128]{1,0:T(8,128)(2,1)S(1)} %pass_first.1.packed, f32[56,128]{1,0:T(8,128)S(1)} %get-tuple-element.42.chains, f32[2,128]{1,0:T(2,128)S(1)} %get-tuple-element.43.embed, ...), custom_call_target="tpu_custom_call" | custom-call | flops 960000000 | tf_op jit(solution)/shard_map/lift_first/pallas_call | solution.py:364
  11.7 0.4 %project_first.1 = (f32[784,128]{1,0:T(8,128)S(1)}, f32[784,128]{1,0:T(8,128)S(1)}) custom-call(bf16[784,128]{1,0:T(8,128)(2,1)S(1)} %get-tuple-element.56.zm_ref, bf16[1024,128]{1,0:T(8,128)(2,1)S(1)} %weights.1), custom_call_target="tpu_custom_call" | custom-call | flops 720000000 | tf_op jit(solution)/shard_map/project_first/pallas_call | solution.py:364
  12.1 0.5 %lift_second.1 = (f32[784,128]{1,0:T(8,128)S(1)}, f32[784,128]{1,0:T(8,128)S(1)}, f32[784,128]{1,0:T(8,128)S(1)}, bf16[784,128]{1,0:T(8,128)(2,1)S(1)}) custom-call(bf16[800,128]{1,0:T(8,128)(2,1)S(1)} %collective-permute-done.2.packed, f32[56,128]{1,0:T(8,128)S(1)} %get-tuple-element.42.chains, f32[2,128]{1,0:T(2,128)S(1)} %get-tuple-element.43.embed, ...), custom_call_target="tpu_custom_call" | custom-call | flops 960000000 | tf_op jit(solution)/shard_map/lift_second/pallas_call | solution.py:364
  12.6 0.4 %project_second.1 = (f32[784,128]{1,0:T(8,128)S(1)}, f32[784,128]{1,0:T(8,128)S(1)}) custom-call(bf16[784,128]{1,0:T(8,128)(2,1)S(1)} %get-tuple-element.48.zm_ref, bf16[1024,128]{1,0:T(8,128)(2,1)S(1)} %weights.1), custom_call_target="tpu_custom_call" | custom-call | flops 720000000 | tf_op jit(solution)/shard_map/project_second/pallas_call | solution.py:364
  13.0 1.0 %collective-permute-done.value = bf16[416,128]{1,0:T(8,128)(2,1)S(1)} collective-permute-done((bf16[416,128]{1,0:T(8,128)(2,1)S(1)}, bf16[416,128]{1,0:T(8,128)(2,1)S(1)}, u32[]{:S(2)}, u32[]{:S(2)}) %collective-permute-start) | collective-permute-done | bytes 106528 | tf_op jit(solution)/shard_map/ppermute | solution.py:407
  14.1 2.0 %early.1 = (f32[1176,128]{1,0:T(8,128)S(1)}, f32[3136,128]{1,0:T(8,128)S(1)}, f32[1176,128]{1,0:T(8,128)S(1)}) custom-call(f32[784,128]{1,0:T(8,128)S(1)} %get-tuple-element.55.left_o, f32[784,128]{1,0:T(8,128)S(1)} %get-tuple-element.57.left_a, f32[784,128]{1,0:T(8,128)S(1)} %get-tuple-element.58.left_e, f32[784,128]{1,0:T(8,128)S(1)} %get-tuple-element.59.right_o, ...), custom_call_target="tpu_custom_call" | custom-call | flops 2400000000 | tf_op jit(solution)/shard_map/early/pallas_call | solution.py:364
  16.1 2.9 %late.1 = (f32[1568,128]{1,0:T(8,128)S(1)}, bf16[784,128]{1,0:T(8,128)(2,1)S(1)}, f32[392,128]{1,0:T(8,128)S(1)}) custom-call(bf16[416,128]{1,0:T(8,128)(2,1)S(1)} %pass_on.1.half_b, bf16[416,128]{1,0:T(8,128)(2,1)S(1)} %collective-permute-done.6.half_f, bf16[1024,128]{1,0:T(8,128)(2,1)S(1)} %weights.1, f32[56,128]{1,0:T(8,128)S(1)} %get-tuple-element.42.chains, ...), custom_call_target="tpu_custom_call" | custom-call | flops 4800000000 | tf_op jit(solution)/shard_map/late/pallas_call | solution.py:364
  19.0 0.6 %collective-permute-start.8 = (bf16[784,128]{1,0:T(8,128)(2,1)S(1)}, bf16[784,128]{1,0:T(8,128)(2,1)S(1)}, u32[]{:S(2)}, u32[]{:S(2)}) collective-permute-start(bf16[784,128]{1,0:T(8,128)(2,1)S(1)} %get-tuple-element.74.own), channel_id=1, source_target_pairs={{0,1},{1,0},{2,3},{3,2},{4,5},{5,4},{6,7},{7,6},{8,9},{9,8},{10,11... | collective-permute-start | bytes 602120 | tf_op jit(solution)/shard_map/ppermute | solution.py:452
  19.5 1.9 %incoming.1.part = bf16[784,128]{1,0:T(8,128)(2,1)S(1)} custom-call(f32[1568,128]{1,0:T(8,128)S(1)} %get-tuple-element.69.z1, f32[784,128]{1,0:T(8,128)S(1)} %get-tuple-element.70.m_o, f32[784,128]{1,0:T(8,128)S(1)} %get-tuple-element.71.m_a, f32[784,128]{1,0:T(8,128)S(1)} %get-tuple-element.72.m_e, f32[392,128]{1,0:T(8,128)S(1)} %get-tuple-element.73.m_f, ...), custom_call_target="tpu_custom_call" | custom-call | flops 3600000000 | tf_op jit(solution)/shard_map/incoming/pallas_call | solution.py:364
  21.5 0.1 collective-permute-start.7
  21.6 0.5 %gate.1 = (f32[784,128]{1,0:T(8,128)S(1)}, f32[784,128]{1,0:T(8,128)S(1)}) custom-call(bf16[784,128]{1,0:T(8,128)(2,1)S(1)} %get-tuple-element.74.own, bf16[784,128]{1,0:T(8,128)(2,1)S(1)} %collective-permute-done.8.received, f32[2,128]{1,0:T(2,128)S(1)} %get-tuple-element.44.in_gain, f32[2,128]{1,0:T(2,128)S(1)} %get-tuple-element.45.in_bias, ...), custom_call_target="tpu_custom_call" | custom-call | flops 1200000000 | tf_op jit(solution)/shard_map/gate/pallas_call | solution.py:364
  22.1 0.9 %collective-permute-done.7.received = bf16[784,128]{1,0:T(8,128)(2,1)S(1)} collective-permute-done((bf16[784,128]{1,0:T(8,128)(2,1)S(1)}, bf16[784,128]{1,0:T(8,128)(2,1)S(1)}, u32[]{:S(2)}, u32[]{:S(2)}) %collective-permute-start.7) | collective-permute-done | bytes 200736 | tf_op jit(solution)/shard_map/ppermute | solution.py:461
  23.0 1.1 %last.1 = bf16[14,56,128]{2,1,0:T(8,128)(2,1)} custom-call(bf16[784,128]{1,0:T(8,128)(2,1)S(1)} %incoming.1.part, bf16[784,128]{1,0:T(8,128)(2,1)S(1)} %collective-permute-done.7.received, f32[784,128]{1,0:T(8,128)S(1)} %get-tuple-element.75.z_ref, f32[784,128]{1,0:T(8,128)S(1)} %get-tuple-element.76.g_ref, f32[2,128]{1,0:T(2,128)S(1)} %get-tuple-element.51.out_gain, ...), custom_call_target="tpu_custom_call" | custom-call | flops 1200000000 | tf_op jit(solution)/shard_map/last/pallas_call | solution.py:364
  (10 shorter events, 0.2 us)
Async XLA Ops:
  1.0 9.5 %collective-permute-start.1 = (bf16[800,128]{1,0:T(8,128)(2,1)S(1)}, bf16[800,128]{1,0:T(8,128)(2,1)S(1)}, u32[]{:S(2)}, u32[]{:S(2)}) collective-permute-start(bf16[800,128]{1,0:T(8,128)(2,1)S(1)} %pack.1.packed), channel_id=1, source_target_pairs={{4,0},{9,1},{6,2},{11,3},{0,4},{13,5},{2,6},{15,7},{12,8},{1,9},{1... | collective-permute-start | bytes 614408 | tf_op jit(solution)/shard_map/ppermute | solution.py:406
  4.1 5.1 %collective-permute-start.4 = (bf16[256,128]{1,0:T(8,128)(2,1)}, bf16[256,128]{1,0:T(8,128)(2,1)S(1)}, u32[]{:S(2)}, u32[]{:S(2)}) collective-permute-start(bf16[256,128]{1,0:T(8,128)(2,1)} %bitcast.6), channel_id=1, source_target_pairs={{0,2},{1,3},{2,0},{3,1},{4,6},{5,7},{6,4},{7,5},{8,10},{9,11},{10,... | collective-permute-start | bytes 196616 | tf_op jit(solution)/shard_map/ppermute | solution.py:409
  5.6 4.4 %collective-permute-start.3 = (bf16[256,128]{1,0:T(8,128)(2,1)}, bf16[256,128]{1,0:T(8,128)(2,1)S(1)}, u32[]{:S(2)}, u32[]{:S(2)}) collective-permute-start(bf16[256,128]{1,0:T(8,128)(2,1)} %bitcast.7), channel_id=1, source_target_pairs={{0,1},{1,0},{2,3},{3,2},{4,5},{5,4},{6,7},{7,6},{8,9},{9,8},{10,11... | collective-permute-start | bytes 196616 | tf_op jit(solution)/shard_map/ppermute | solution.py:408
  6.9 7.1 %collective-permute-start = (bf16[416,128]{1,0:T(8,128)(2,1)S(1)}, bf16[416,128]{1,0:T(8,128)(2,1)S(1)}, u32[]{:S(2)}, u32[]{:S(2)}) collective-permute-start(bf16[416,128]{1,0:T(8,128)(2,1)S(1)} %get-tuple-element.41), channel_id=1, source_target_pairs={{12,0},{13,1},{14,2},{15,3},{8,4},{9,5},{10,6},{11,7},{4,8},{5,9},... | collective-permute-start | bytes 319496 | tf_op jit(solution)/shard_map/ppermute | solution.py:407
  9.2 1.3 %collective-permute-start.5 = (bf16[256,128]{1,0:T(8,128)(2,1)S(1)}, bf16[256,128]{1,0:T(8,128)(2,1)S(1)}, u32[]{:S(2)}, u32[]{:S(2)}) collective-permute-start(bf16[256,128]{1,0:T(8,128)(2,1)S(1)} %collective-permute-done.4.w_a), channel_id=1, source_target_pairs={{0,1},{1,0},{2,3},{3,2},{4,5},{5,4},{6,7},{7,6},{8,9},{9,8},{10,11... | collective-permute-start | bytes 196616 | tf_op jit(solution)/shard_map/ppermute | solution.py:410
  10.5 1.6 %collective-permute-start.2 = (bf16[800,128]{1,0:T(8,128)(2,1)S(1)}, bf16[800,128]{1,0:T(8,128)(2,1)S(1)}, u32[]{:S(2)}, u32[]{:S(2)}) collective-permute-start(bf16[800,128]{1,0:T(8,128)(2,1)S(1)} %pass_first.1.packed), channel_id=1, source_target_pairs={{0,1},{1,0},{2,3},{3,2},{4,5},{5,4},{6,7},{7,6},{8,9},{9,8},{10,11... | collective-permute-start | bytes 614408 | tf_op jit(solution)/shard_map/ppermute | solution.py:429
  14.0 2.1 %collective-permute-start.6 = (bf16[416,128]{1,0:T(8,128)(2,1)S(1)}, bf16[416,128]{1,0:T(8,128)(2,1)S(1)}, u32[]{:S(2)}, u32[]{:S(2)}) collective-permute-start(bf16[416,128]{1,0:T(8,128)(2,1)S(1)} %pass_on.1.half_b), channel_id=1, source_target_pairs={{0,1},{1,0},{2,3},{3,2},{4,5},{5,4},{6,7},{7,6},{8,9},{9,8},{10,11... | collective-permute-start | bytes 319496 | tf_op jit(solution)/shard_map/ppermute | solution.py:434
  19.0 2.6 %collective-permute-start.8 = (bf16[784,128]{1,0:T(8,128)(2,1)S(1)}, bf16[784,128]{1,0:T(8,128)(2,1)S(1)}, u32[]{:S(2)}, u32[]{:S(2)}) collective-permute-start(bf16[784,128]{1,0:T(8,128)(2,1)S(1)} %get-tuple-element.74.own), channel_id=1, source_target_pairs={{0,1},{1,0},{2,3},{3,2},{4,5},{5,4},{6,7},{7,6},{8,9},{9,8},{10,11... | collective-permute-start | bytes 602120 | tf_op jit(solution)/shard_map/ppermute | solution.py:452
  21.5 1.5 %collective-permute-start.7 = (bf16[784,128]{1,0:T(8,128)(2,1)S(1)}, bf16[784,128]{1,0:T(8,128)(2,1)S(1)}, u32[]{:S(2)}, u32[]{:S(2)}) collective-permute-start(bf16[784,128]{1,0:T(8,128)(2,1)S(1)} %incoming.1.part), channel_id=1, source_target_pairs={{0,1},{1,0},{2,3},{3,2},{4,5},{5,4},{6,7},{7,6},{8,9},{9,8},{10,11... | collective-permute-start | bytes 602120 | tf_op jit(solution)/shard_map/ppermute | solution.py:461

commit v6 on v5

--- a/solution.py
+++ b/solution.py
@@ -163,9 +163,7 @@
     return lax.fori_loop(0, steps, body, zeros, unroll=min(28, steps))
 
 
-def early_kernel(
-    n, rows, early, left_o, left_a, left_e, right_o, right_a, right_e, x_ref, right_ref, left_ref,
-):
+def order_kernel(n, rows, left_o, left_a, left_e, right_o, right_a, right_e, right_ref, left_ref):
     core = lax.rem(lax.axis_index("ch"), 2)
     block, mid = rows * n, rows // 2 * n
 
@@ -185,6 +183,8 @@
         right_ref[pl.ds(rows * (1 + core) + j, n, stride=n), :] = right_a[rows_of_j, :]
         right_ref[pl.ds(rows * (2 - core) + j, n, stride=n), :] = right_e[rows_of_j, :]
 
+
+def early_kernel(n, rows, early, left_ref, right_ref, x_ref):
     group = rows // 2
 
     def some(t, _):
@@ -290,7 +290,7 @@
 
 
 def incoming_kernel(
-    n, rows, z1, m_o, m_a, m_e, m_f, weights, in_gain, in_bias, part, left_ref, right_ref, sums_ref
+    n, rows, z1, m_o, m_a, m_e, m_f, weights, in_gain, in_bias, part, left_ref, right_ref, sums_ref, zm_ref, own_ref
 ):
     r = lax.axis_index("row")
     even = lax.rem(lax.axis_index("ch"), 2) == 0
@@ -306,13 +306,15 @@
         at = slice(first * n, (first + count) * n)
         zn = normalize(z1[at, :], in_gain[1:2, :], in_bias[1:2, :])
         zm = zn * masks(at).astype(BF16)
-        left_ref[at, :] = gated_side(zm, weights, 1, 0, chan)
+        zm_ref[at, :] = zm.astype(F32)
         right_ref[at, :] = gated_side(zm, weights, 1, 1, chan)
+    for k in range(2 * rows):
+        own_ref[k * rows : (k + 1) * rows, :] = zm_ref[pl.ds(k * n + r * rows, rows), :]
+    left_ref[...] = gated_side(own_ref[...].astype(BF16), weights, 1, 0, chan)
     wide = (n // 8 + 1) // 2 * 8
     for t in range(2):
-        start = r * rows + t * group
         for at, width in ((0, wide), (wide, n - wide)):
-            accs = tiles_of([(left_ref, start + i, n) for i in range(group)], 2 * rows, right_ref, at, width, n)
+            accs = tiles_of([(left_ref, t * group + i, rows) for i in range(group)], 2 * rows, right_ref, at, width, n)
             for i, acc in enumerate(accs):
                 row = (t * group + i) * n + at
                 sums_ref[row : row + width, :] = acc
@@ -327,14 +329,18 @@
     g_ref[...] = half_sigmoid(0.5 * nn_dot(zn, gate_w[1]))
 
 
-def last_kernel(n, rows, part, received, z_ref, g_ref, out_gain, out_bias, out_w, result):
+def last_kernel(n, rows, part, received, z_ref, g_ref, out_gain, out_bias, out_w, result, out, sems):
+    copies = []
     for first, count in pieces(rows, 8):
         at = pl.ds(first * n, count * n)
         x = part[at, :].astype(F32) + received[at, :].astype(F32)
         update = hidden_update(x, out_gain[1:2, :], out_bias[1:2, :], out_w[1])
-        out = (z_ref[at, :] + g_ref[at, :] * update).astype(BF16)
-        for i in range(count):
-            result[first + i] = out[i * n : (i + 1) * n]
+        out[at, :] = (z_ref[at, :] + g_ref[at, :] * update).astype(BF16)
+        copy = pltpu.make_async_copy(out.at[at], result.at[at], sems.at[len(copies)])
+        copy.start()
+        copies.append(copy)
+    for copy in copies:
+        copy.wait()
 
 
 def in_one_phase(
@@ -430,14 +436,17 @@
     at_a = one_block("lift_first", lambda core: 1 + core, packed_a)
     at_e = one_block("lift_second", lambda core: 2 - core, packed_e)
     at_a, at_e = (project(name, v) for name, v in (("project_first", at_a), ("project_second", at_e)))
-    (half_b,) = call(pass_kernel, "pass_on", [bf16(part + MASK_ROWS)], [half_b, at_e[4]], us=0.1)
+    right, left = call(
+        functools.partial(order_kernel, n, rows),
+        "order",
+        [f32(n * n), f32(block + mid)],
+        [at_o[3], at_a[3], at_e[3], at_o[4], at_a[4], at_e[4]],
+        us=0.3,
+    )
+    (half_b,) = call(pass_kernel, "pass_on", [bf16(part + MASK_ROWS)], [half_b, right], us=0.1)
     half_f = lax.ppermute(half_b, "ch", cores)
-    x, right, left = call(
-        functools.partial(early_kernel, n, rows, early),
-        "early",
-        [f32(block + mid), f32(n * n), f32(block + mid)],
-        [at_o[3], at_a[3], at_e[3], at_o[4], at_a[4], at_e[4]],
-        us=2.0,
+    (x,) = call(
+        functools.partial(early_kernel, n, rows, early), "early", [f32(block + mid)], [left, right], us=2.0
     )
     z1, own, mask_f = call(
         functools.partial(late_kernel, n, rows, part, early),
@@ -455,18 +464,27 @@
         "incoming",
         [bf16(block)],
         [z1, at_o[2], at_a[2], at_e[2], mask_f, w_all, in_gain, in_bias],
-        scratch=[(2 * block, chan)] * 2 + [(block, chan)],
+        scratch=[(2 * rows * rows, chan), (2 * block, chan), (block, chan), (2 * block, chan), (2 * rows * rows, chan)],
         us=3.0,
     )
     part_n = lax.ppermute(part, "ch", cores)
     z1_own, gate = call(gate_kernel, "gate", [f32(block)] * 2, [own, own_n, in_gain, in_bias, gate_weight])
-    (result,) = call(
+    result = pl.pallas_call(
         functools.partial(last_kernel, n, rows),
-        "last",
-        [jax.ShapeDtypeStruct((rows, n, chan), BF16)],
-        [part, part_n, z1_own, gate, out_gain, out_bias, out_weight],
-    )
-    return result
+        out_shape=jax.ShapeDtypeStruct((block, chan), BF16),
+        in_specs=[vmem] * 7,
+        out_specs=hbm,
+        scratch_shapes=[pltpu.VMEM((block, chan), BF16), pltpu.SemaphoreType.DMA((len(pieces(rows, 8)),))],
+        compiler_params=pltpu.CompilerParams(vmem_limit_bytes=32 * 1024 * 1024),
+        cost_estimate=pl.CostEstimate(flops=10**9, bytes_accessed=0, transcendentals=0),
+        name="last",
+    )(
+        *(
+            pltpu.with_memory_space_constraint(v, pltpu.VMEM) if id(v) in in_vmem else v
+            for v in (part, part_n, z1_own, gate, out_gain, out_bias, out_weight)
+        )
+    )
+    return result.reshape(rows, n, chan)
 
 
 def layer_norm(values, gain, bias):

time: 24.3 us -> 23.9 us (0.984)
  waiting for transfers between devices: 2.44 us -> 2.11 us
    pallas_call x14, Pallas kernels: 11.1 us -> 9.81 us  [call(): pl.pallas_call(kernel, out_shape=tuple(outs), in_specs=[vmem] * len(ins),...]
    pallas_call x0 -> x1, Pallas kernels: none -> 1.08 us  [in_one_phase(): pl.pallas_call(functools.partial(last_kernel, n, rows), out_shape=jax.Sha...]
    ppermute x1, waiting for transfers between devices: 0.98 us -> 0.66 us  [in_one_phase(): half_b = lax.ppermute(halved, both, second)]
where the time goes in v6:
time: 23.9 us; the launch traced here: 23.6 us
  Pallas kernels  12.9 us (54%)
  starting transfers between devices  8.36 us (35%)
  waiting for transfers between devices  2.11 us (9%)
    pallas_call x14, Pallas kernels, call(): pl.pallas_call(kernel, out_shape=tuple(outs), in_specs=[vmem] * len(ins),...  9.81 us
    ppermute x1, starting transfers between devices, in_one_phase(): packed_a = lax.ppermute(packed, both, first)  3.09 us
    ppermute x1, starting transfers between devices, in_one_phase(): half_b = lax.ppermute(halved, both, second)  2.26 us
    ppermute x1, starting transfers between devices, in_one_phase(): w_a = lax.ppermute(weights, 'ch', chips)  1.49 us
    pallas_call x1, Pallas kernels, in_one_phase(): pl.pallas_call(functools.partial(last_kernel, n, rows), out_shape=jax.Sha...  1.08 us
    pallas_call x1, Pallas kernels, in_one_phase(): pl.pallas_call(functools.partial(constants_kernel, part), out_shape=tuple...  1.08 us
    pallas_call x1, Pallas kernels, in_one_phase(): pl.pallas_call(functools.partial(pack_kernel, n, rows), out_shape=(bf16(b...  0.96 us
    ppermute x1, waiting for transfers between devices, in_one_phase(): part_n = lax.ppermute(part, 'ch', cores)  0.92 us
  transfers between devices with their start and end apart: 9, of which 3 were waited for; matrix products, arithmetic and copies ran while one was open for 0% of the time, Pallas kernels for 34%

profile of v6, /device:TPU:0, one launch (start us, length us, event | category | flops | bytes accessed | tf_op | source)
XLA Modules:
  0.0 23.6 jit_solution(1202152436516323157)
XLA Ops:
  0.0 1.0 %pack.1.packed = bf16[800,128]{1,0:T(8,128)(2,1)S(1)} custom-call(bf16[784,128]{1,0:T(8,128)(2,1)} %bitcast.6, s32[14,56]{1,0:T(8,128)} %mask.1), custom_call_target="tpu_custom_call" | custom-call | tf_op jit(solution)/shard_map/pack/pallas_call | solution.py:389
  1.0 3.1 %collective-permute-start.4 = (bf16[800,128]{1,0:T(8,128)(2,1)S(1)}, bf16[800,128]{1,0:T(8,128)(2,1)S(1)}, u32[]{:S(2)}, u32[]{:S(2)}) collective-permute-start(bf16[800,128]{1,0:T(8,128)(2,1)S(1)} %pack.1.packed), channel_id=1, source_target_pairs={{4,0},{9,1},{6,2},{11,3},{0,4},{13,5},{2,6},{15,7},{12,8},{1,9},{1... | collective-permute-start | bytes 614408 | tf_op jit(solution)/shard_map/ppermute | solution.py:412
  4.1 1.5 %collective-permute-start.2 = (bf16[256,128]{1,0:T(8,128)(2,1)}, bf16[256,128]{1,0:T(8,128)(2,1)S(1)}, u32[]{:S(2)}, u32[]{:S(2)}) collective-permute-start(bf16[256,128]{1,0:T(8,128)(2,1)} %bitcast.7), channel_id=1, source_target_pairs={{0,2},{1,3},{2,0},{3,1},{4,6},{5,7},{6,4},{7,5},{8,10},{9,11},{10,... | collective-permute-start | bytes 196616 | tf_op jit(solution)/shard_map/ppermute | solution.py:415
  5.6 0.3 %collective-permute-start.1 = (bf16[256,128]{1,0:T(8,128)(2,1)}, bf16[256,128]{1,0:T(8,128)(2,1)S(1)}, u32[]{:S(2)}, u32[]{:S(2)}) collective-permute-start(bf16[256,128]{1,0:T(8,128)(2,1)} %bitcast.8), channel_id=1, source_target_pairs={{0,1},{1,0},{2,3},{3,2},{4,5},{5,4},{6,7},{7,6},{8,9},{9,8},{10,11... | collective-permute-start | bytes 196616 | tf_op jit(solution)/shard_map/ppermute | solution.py:414
  5.8 1.1 %constants.1 = (bf16[256,128]{1,0:T(8,128)(2,1)S(1)}, f32[2,128]{1,0:T(2,128)S(1)}, f32[2,128]{1,0:T(2,128)S(1)}, f32[2,128]{1,0:T(2,128)S(1)}, bf16[2,128,128]{...) custom-call(bf16[800,128]{1,0:T(8,128)(2,1)S(1)} %pack.1.packed, ...), custom_call_target="tpu_custom_call" | custom-call | flops 10000000 | tf_op jit(solution)/shard_map/constants/pallas_call | solution.py:398
  6.9 2.3 %collective-permute-start = (bf16[416,128]{1,0:T(8,128)(2,1)S(1)}, bf16[416,128]{1,0:T(8,128)(2,1)S(1)}, u32[]{:S(2)}, u32[]{:S(2)}) collective-permute-start(bf16[416,128]{1,0:T(8,128)(2,1)S(1)} %get-tuple-element.40), channel_id=1, source_target_pairs={{12,0},{13,1},{14,2},{15,3},{8,4},{9,5},{10,6},{11,7},{4,8},{5,9},... | collective-permute-start | bytes 319496 | tf_op jit(solution)/shard_map/ppermute | solution.py:413
  9.2 0.2 collective-permute-start.3
  9.4 0.5 %lift_own.1 = (f32[784,128]{1,0:T(8,128)S(1)}, f32[784,128]{1,0:T(8,128)S(1)}, f32[784,128]{1,0:T(8,128)S(1)}, bf16[784,128]{1,0:T(8,128)(2,1)S(1)}) custom-call(bf16[800,128]{1,0:T(8,128)(2,1)S(1)} %pack.1.packed, f32[56,128]{1,0:T(8,128)S(1)} %get-tuple-element.41.chains, f32[2,128]{1,0:T(2,128)S(1)} %get-tuple-element.42.embed, ...), custom_call_target="tpu_custom_call" | custom-call | flops 960000000 | tf_op jit(solution)/shard_map/lift_own/pallas_call | solution.py:370
  9.9 0.5 %collective-permute-done.3.w_f = bf16[256,128]{1,0:T(8,128)(2,1)S(1)} collective-permute-done((bf16[256,128]{1,0:T(8,128)(2,1)S(1)}, bf16[256,128]{1,0:T(8,128)(2,1)S(1)}, u32[]{:S(2)}, u32[]{:S(2)}) %collective-permute-start.3) | collective-permute-done | bytes 65568 | tf_op jit(solution)/shard_map/ppermute | solution.py:416
  10.5 0.3 %collective-permute-start.5 = (bf16[800,128]{1,0:T(8,128)(2,1)S(1)}, bf16[800,128]{1,0:T(8,128)(2,1)S(1)}, u32[]{:S(2)}, u32[]{:S(2)}) collective-permute-start(bf16[800,128]{1,0:T(8,128)(2,1)S(1)} %pass_first.1.packed), channel_id=1, source_target_pairs={{0,1},{1,0},{2,3},{3,2},{4,5},{5,4},{6,7},{7,6},{8,9},{9,8},{10,11... | collective-permute-start | bytes 614408 | tf_op jit(solution)/shard_map/ppermute | solution.py:435
  10.8 0.4 %project_own.1 = (f32[784,128]{1,0:T(8,128)S(1)}, f32[784,128]{1,0:T(8,128)S(1)}) custom-call(bf16[784,128]{1,0:T(8,128)(2,1)S(1)} %get-tuple-element.46.zm_ref, bf16[1024,128]{1,0:T(8,128)(2,1)S(1)} %weights.1), custom_call_target="tpu_custom_call" | custom-call | flops 720000000 | tf_op jit(solution)/shard_map/project_own/pallas_call | solution.py:370
  11.2 0.5 %lift_first.1 = (f32[784,128]{1,0:T(8,128)S(1)}, f32[784,128]{1,0:T(8,128)S(1)}, f32[784,128]{1,0:T(8,128)S(1)}, bf16[784,128]{1,0:T(8,128)(2,1)S(1)}) custom-call(bf16[800,128]{1,0:T(8,128)(2,1)S(1)} %pass_first.1.packed, f32[56,128]{1,0:T(8,128)S(1)} %get-tuple-element.41.chains, f32[2,128]{1,0:T(2,128)S(1)} %get-tuple-element.42.embed, ...), custom_call_target="tpu_custom_call" | custom-call | flops 960000000 | tf_op jit(solution)/shard_map/lift_first/pallas_call | solution.py:370
  11.7 0.4 %project_first.1 = (f32[784,128]{1,0:T(8,128)S(1)}, f32[784,128]{1,0:T(8,128)S(1)}) custom-call(bf16[784,128]{1,0:T(8,128)(2,1)S(1)} %get-tuple-element.50.zm_ref, bf16[1024,128]{1,0:T(8,128)(2,1)S(1)} %weights.1), custom_call_target="tpu_custom_call" | custom-call | flops 720000000 | tf_op jit(solution)/shard_map/project_first/pallas_call | solution.py:370
  12.1 0.5 %lift_second.1 = (f32[784,128]{1,0:T(8,128)S(1)}, f32[784,128]{1,0:T(8,128)S(1)}, f32[784,128]{1,0:T(8,128)S(1)}, bf16[784,128]{1,0:T(8,128)(2,1)S(1)}) custom-call(bf16[800,128]{1,0:T(8,128)(2,1)S(1)} %collective-permute-done.5.packed, f32[56,128]{1,0:T(8,128)S(1)} %get-tuple-element.41.chains, f32[2,128]{1,0:T(2,128)S(1)} %get-tuple-element.42.embed, ...), custom_call_target="tpu_custom_call" | custom-call | flops 960000000 | tf_op jit(solution)/shard_map/lift_second/pallas_call | solution.py:370
  12.6 0.4 %project_second.1 = (f32[784,128]{1,0:T(8,128)S(1)}, f32[784,128]{1,0:T(8,128)S(1)}) custom-call(bf16[784,128]{1,0:T(8,128)(2,1)S(1)} %get-tuple-element.52.zm_ref, bf16[1024,128]{1,0:T(8,128)(2,1)S(1)} %weights.1), custom_call_target="tpu_custom_call" | custom-call | flops 720000000 | tf_op jit(solution)/shard_map/project_second/pallas_call | solution.py:370
  13.0 0.3 %order.1 = (f32[3136,128]{1,0:T(8,128)S(1)}, f32[1176,128]{1,0:T(8,128)S(1)}) custom-call(f32[784,128]{1,0:T(8,128)S(1)} %get-tuple-element.48.left_o, f32[784,128]{1,0:T(8,128)S(1)} %get-tuple-element.51.left_a, f32[784,128]{1,0:T(8,128)S(1)} %get-tuple-element.53.left_e, f32[784,128]{1,0:T(8,128)S(1)} %get-tuple-element.54.right_o, ...), custom_call_target="tpu_custom_call" | custom-call | flops 360000000 | tf_op jit(solution)/shard_map/order/pallas_call | solution.py:370
  13.3 0.7 %collective-permute-done.value = bf16[416,128]{1,0:T(8,128)(2,1)S(1)} collective-permute-done((bf16[416,128]{1,0:T(8,128)(2,1)S(1)}, bf16[416,128]{1,0:T(8,128)(2,1)S(1)}, u32[]{:S(2)}, u32[]{:S(2)}) %collective-permute-start) | collective-permute-done | bytes 106528 | tf_op jit(solution)/shard_map/ppermute | solution.py:413
  14.1 1.7 %early.1.x_in = f32[1176,128]{1,0:T(8,128)S(1)} custom-call(f32[1176,128]{1,0:T(8,128)S(1)} %get-tuple-element.61.left_ref.left_in, f32[3136,128]{1,0:T(8,128)S(1)} %get-tuple-element.57.after.right_ref.right_in), custom_call_target="tpu_custom_call" | custom-call | flops 2400000000 | tf_op jit(solution)/shard_map/early/pallas_call | solution.py:370
  15.8 2.9 %late.1 = (f32[1568,128]{1,0:T(8,128)S(1)}, bf16[784,128]{1,0:T(8,128)(2,1)S(1)}, f32[392,128]{1,0:T(8,128)S(1)}) custom-call(bf16[416,128]{1,0:T(8,128)(2,1)S(1)} %pass_on.1.half_b, bf16[416,128]{1,0:T(8,128)(2,1)S(1)} %collective-permute-done.6.half_f, bf16[1024,128]{1,0:T(8,128)(2,1)S(1)} %weights.1, f32[56,128]{1,0:T(8,128)S(1)} %get-tuple-element.41.chains, ...), custom_call_target="tpu_custom_call" | custom-call | flops 4800000000 | tf_op jit(solution)/shard_map/late/pallas_call | solution.py:370
  18.7 0.6 %collective-permute-start.8 = (bf16[784,128]{1,0:T(8,128)(2,1)S(1)}, bf16[784,128]{1,0:T(8,128)(2,1)S(1)}, u32[]{:S(2)}, u32[]{:S(2)}) collective-permute-start(bf16[784,128]{1,0:T(8,128)(2,1)S(1)} %get-tuple-element.72.own), channel_id=1, source_target_pairs={{0,1},{1,0},{2,3},{3,2},{4,5},{5,4},{6,7},{7,6},{8,9},{9,8},{10,11... | collective-permute-start | bytes 602120 | tf_op jit(solution)/shard_map/ppermute | solution.py:461
  19.3 1.7 %incoming.1.part = bf16[784,128]{1,0:T(8,128)(2,1)S(1)} custom-call(f32[1568,128]{1,0:T(8,128)S(1)} %get-tuple-element.67.z1, f32[784,128]{1,0:T(8,128)S(1)} %get-tuple-element.68.m_o, f32[784,128]{1,0:T(8,128)S(1)} %get-tuple-element.69.m_a, f32[784,128]{1,0:T(8,128)S(1)} %get-tuple-element.70.m_e, f32[392,128]{1,0:T(8,128)S(1)} %get-tuple-element.71.m_f, ...), custom_call_target="tpu_custom_call" | custom-call | flops 3600000000 | tf_op jit(solution)/shard_map/incoming/pallas_call | solution.py:370
  21.0 0.5 %gate.1 = (f32[784,128]{1,0:T(8,128)S(1)}, f32[784,128]{1,0:T(8,128)S(1)}) custom-call(bf16[784,128]{1,0:T(8,128)(2,1)S(1)} %get-tuple-element.72.own, bf16[784,128]{1,0:T(8,128)(2,1)S(1)} %collective-permute-done.8.received, f32[2,128]{1,0:T(2,128)S(1)} %get-tuple-element.43.in_gain, f32[2,128]{1,0:T(2,128)S(1)} %get-tuple-element.44.in_bias, ...), custom_call_target="tpu_custom_call" | custom-call | flops 1200000000 | tf_op jit(solution)/shard_map/gate/pallas_call | solution.py:370
  21.6 0.9 %collective-permute-done.7.received = bf16[784,128]{1,0:T(8,128)(2,1)S(1)} collective-permute-done((bf16[784,128]{1,0:T(8,128)(2,1)S(1)}, bf16[784,128]{1,0:T(8,128)(2,1)S(1)}, u32[]{:S(2)}, u32[]{:S(2)}) %collective-permute-start.7) | collective-permute-done | bytes 200736 | tf_op jit(solution)/shard_map/ppermute | solution.py:470
  22.5 1.1 %last.1 = bf16[784,128]{1,0:T(8,128)(2,1)} custom-call(bf16[784,128]{1,0:T(8,128)(2,1)S(1)} %incoming.1.part, bf16[784,128]{1,0:T(8,128)(2,1)S(1)} %collective-permute-done.7.received, f32[784,128]{1,0:T(8,128)S(1)} %get-tuple-element.73.z_ref, f32[784,128]{1,0:T(8,128)S(1)} %get-tuple-element.74.g_ref, f32[2,128]{1,0:T(2,128)S(1)} %get-tuple-element.58.out_gain, ...), custom_call_target="tpu_custom_call" | custom-call | flops 1000000000 | tf_op jit(solution)/shard_map/last/pallas_call | solution.py:472
  (11 shorter events, 0.3 us)
Async XLA Ops:
  1.0 9.5 %collective-permute-start.4 = (bf16[800,128]{1,0:T(8,128)(2,1)S(1)}, bf16[800,128]{1,0:T(8,128)(2,1)S(1)}, u32[]{:S(2)}, u32[]{:S(2)}) collective-permute-start(bf16[800,128]{1,0:T(8,128)(2,1)S(1)} %pack.1.packed), channel_id=1, source_target_pairs={{4,0},{9,1},{6,2},{11,3},{0,4},{13,5},{2,6},{15,7},{12,8},{1,9},{1... | collective-permute-start | bytes 614408 | tf_op jit(solution)/shard_map/ppermute | solution.py:412
  4.1 5.1 %collective-permute-start.2 = (bf16[256,128]{1,0:T(8,128)(2,1)}, bf16[256,128]{1,0:T(8,128)(2,1)S(1)}, u32[]{:S(2)}, u32[]{:S(2)}) collective-permute-start(bf16[256,128]{1,0:T(8,128)(2,1)} %bitcast.7), channel_id=1, source_target_pairs={{0,2},{1,3},{2,0},{3,1},{4,6},{5,7},{6,4},{7,5},{8,10},{9,11},{10,... | collective-permute-start | bytes 196616 | tf_op jit(solution)/shard_map/ppermute | solution.py:415
  5.6 4.4 %collective-permute-start.1 = (bf16[256,128]{1,0:T(8,128)(2,1)}, bf16[256,128]{1,0:T(8,128)(2,1)S(1)}, u32[]{:S(2)}, u32[]{:S(2)}) collective-permute-start(bf16[256,128]{1,0:T(8,128)(2,1)} %bitcast.8), channel_id=1, source_target_pairs={{0,1},{1,0},{2,3},{3,2},{4,5},{5,4},{6,7},{7,6},{8,9},{9,8},{10,11... | collective-permute-start | bytes 196616 | tf_op jit(solution)/shard_map/ppermute | solution.py:414
  6.9 7.1 %collective-permute-start = (bf16[416,128]{1,0:T(8,128)(2,1)S(1)}, bf16[416,128]{1,0:T(8,128)(2,1)S(1)}, u32[]{:S(2)}, u32[]{:S(2)}) collective-permute-start(bf16[416,128]{1,0:T(8,128)(2,1)S(1)} %get-tuple-element.40), channel_id=1, source_target_pairs={{12,0},{13,1},{14,2},{15,3},{8,4},{9,5},{10,6},{11,7},{4,8},{5,9},... | collective-permute-start | bytes 319496 | tf_op jit(solution)/shard_map/ppermute | solution.py:413
  9.2 1.3 %collective-permute-start.3 = (bf16[256,128]{1,0:T(8,128)(2,1)S(1)}, bf16[256,128]{1,0:T(8,128)(2,1)S(1)}, u32[]{:S(2)}, u32[]{:S(2)}) collective-permute-start(bf16[256,128]{1,0:T(8,128)(2,1)S(1)} %collective-permute-done.2.w_a), channel_id=1, source_target_pairs={{0,1},{1,0},{2,3},{3,2},{4,5},{5,4},{6,7},{7,6},{8,9},{9,8},{10,11... | collective-permute-start | bytes 196616 | tf_op jit(solution)/shard_map/ppermute | solution.py:416
  10.5 1.6 %collective-permute-start.5 = (bf16[800,128]{1,0:T(8,128)(2,1)S(1)}, bf16[800,128]{1,0:T(8,128)(2,1)S(1)}, u32[]{:S(2)}, u32[]{:S(2)}) collective-permute-start(bf16[800,128]{1,0:T(8,128)(2,1)S(1)} %pass_first.1.packed), channel_id=1, source_target_pairs={{0,1},{1,0},{2,3},{3,2},{4,5},{5,4},{6,7},{7,6},{8,9},{9,8},{10,11... | collective-permute-start | bytes 614408 | tf_op jit(solution)/shard_map/ppermute | solution.py:435
  14.0 1.8 %collective-permute-start.6 = (bf16[416,128]{1,0:T(8,128)(2,1)S(1)}, bf16[416,128]{1,0:T(8,128)(2,1)S(1)}, u32[]{:S(2)}, u32[]{:S(2)}) collective-permute-start(bf16[416,128]{1,0:T(8,128)(2,1)S(1)} %pass_on.1.half_b), channel_id=1, source_target_pairs={{0,1},{1,0},{2,3},{3,2},{4,5},{5,4},{6,7},{7,6},{8,9},{9,8},{10,11... | collective-permute-start | bytes 319496 | tf_op jit(solution)/shard_map/ppermute | solution.py:447
  18.7 2.3 %collective-permute-start.8 = (bf16[784,128]{1,0:T(8,128)(2,1)S(1)}, bf16[784,128]{1,0:T(8,128)(2,1)S(1)}, u32[]{:S(2)}, u32[]{:S(2)}) collective-permute-start(bf16[784,128]{1,0:T(8,128)(2,1)S(1)} %get-tuple-element.72.own), channel_id=1, source_target_pairs={{0,1},{1,0},{2,3},{3,2},{4,5},{5,4},{6,7},{7,6},{8,9},{9,8},{10,11... | collective-permute-start | bytes 602120 | tf_op jit(solution)/shard_map/ppermute | solution.py:461
  21.0 1.5 %collective-permute-start.7 = (bf16[784,128]{1,0:T(8,128)(2,1)S(1)}, bf16[784,128]{1,0:T(8,128)(2,1)S(1)}, u32[]{:S(2)}, u32[]{:S(2)}) collective-permute-start(bf16[784,128]{1,0:T(8,128)(2,1)S(1)} %incoming.1.part), channel_id=1, source_target_pairs={{0,1},{1,0},{2,3},{3,2},{4,5},{5,4},{6,7},{7,6},{8,9},{9,8},{10,11... | collective-permute-start | bytes 602120 | tf_op jit(solution)/shard_map/ppermute | solution.py:470

commit v7 on v6

--- a/solution.py
+++ b/solution.py
@@ -121,8 +121,12 @@
             weights[pl.ds(first, hid), :] = ref[q * hid : (q + 1) * hid, :] * jnp.asarray(0.5, BF16)
 
 
+def kept_from(rows, name):
+    return rows // 2 // 2 * 2 if name == "second" else 0
+
+
 def lift_kernel(
-    n, rows, which,
+    n, rows, which, name,
     packed, chains, embed, in_gain, in_bias, gate_w,
     z_ref, g_ref, m_ref, zm_ref,
 ):
@@ -132,24 +136,40 @@
     chan = packed.shape[1]
     masks_at = packed.shape[0] - MASK_ROWS
     masks = spread_masks(packed[masks_at : masks_at + MASK_ROWS, 0:n][0:rows], rows, n, chan)
-    for first, count in pieces(rows, 8):
+    skip = kept_from(rows, name)
+    for first, count in pieces(skip, 8) + [(skip + first, count) for first, count in pieces(rows - skip, 8)]:
         at = pl.ds(first * n, count * n)
         z, zn, spread = lift(
             packed[at, :], masks, chains, embed, in_gain[0:1, :], in_bias[0:1, :], position, first, count
         )
         z_ref[at, :] = z
         m_ref[at, :] = spread
-        g_ref[at, :] = half_sigmoid(0.5 * nn_dot(zn, gate_w[0]))
+        if first >= kept_from(rows, name):
+            g_ref[at, :] = half_sigmoid(0.5 * nn_dot(zn, gate_w[0]))
         zm_ref[at, :] = zn * spread.astype(BF16)
 
 
-def project_kernel(n, rows, zm_ref, weights, left_ref, right_ref):
+def project_kernel(n, rows, name, zm_ref, weights, left_ref, right_ref):
     chan = zm_ref.shape[1]
+    skip = kept_from(rows, name)
+
+    def left(first, count):
+        at = pl.ds(first * n, count * n)
+        left_ref[at, :] = gated_side(zm_ref[at, :], weights, 0, 0, chan)
+
     for first, count in pieces(rows, 8):
         at = pl.ds(first * n, count * n)
-        zm = zm_ref[at, :]
-        left_ref[at, :] = gated_side(zm, weights, 0, 0, chan)
-        right_ref[at, :] = gated_side(zm, weights, 0, 1, chan)
+        right_ref[at, :] = gated_side(zm_ref[at, :], weights, 0, 1, chan)
+    if name == "own":
+
+        @pl.when(lax.rem(lax.axis_index("ch"), 2) == 0)
+        def _():
+            for first, count in pieces(rows, 8):
+                left(first, count)
+
+    else:
+        for first, count in pieces(rows - skip, 8):
+            left(skip + first, count)
 
 
 def tiles_of(lefts, steps, right_ref, right_at, width, right_step):
@@ -416,26 +436,28 @@
     w_f = lax.ppermute(w_a, "ch", cores)
     def one_block(name, which, source):
         return call(
-            functools.partial(lift_kernel, n, rows, which),
-            name,
+            functools.partial(lift_kernel, n, rows, which, name),
+            "lift_" + name,
             [f32(block)] * 3 + [bf16(block)],
             [source, chains, pair_embed, in_gain, in_bias, gate_weight],
             us=0.8,
         )
 
-    at_o = one_block("lift_own", lambda core: 0, packed)
+    at_o = one_block("own", lambda core: 0, packed)
     (w_all,) = call(weights_kernel, "weights", [bf16(4 * size)], [w_own, w_e, w_a, w_f], us=0.1)
 
     def project(name, lifted):
-        sides = call(functools.partial(project_kernel, n, rows), name, [f32(block)] * 2, [lifted[3], w_all], us=0.6)
+        sides = call(
+            functools.partial(project_kernel, n, rows, name), "project_" + name, [f32(block)] * 2, [lifted[3], w_all], us=0.6
+        )
         return list(lifted[:3]) + list(sides)
 
     (packed_a,) = call(pass_kernel, "pass_first", [bf16(block + MASK_ROWS)], [packed_a, at_o[0]], us=0.1)
-    at_o = project("project_own", at_o)
+    at_o = project("own", at_o)
     packed_e = lax.ppermute(packed_a, "ch", cores)
-    at_a = one_block("lift_first", lambda core: 1 + core, packed_a)
-    at_e = one_block("lift_second", lambda core: 2 - core, packed_e)
-    at_a, at_e = (project(name, v) for name, v in (("project_first", at_a), ("project_second", at_e)))
+    at_a = one_block("first", lambda core: 1 + core, packed_a)
+    at_e = one_block("second", lambda core: 2 - core, packed_e)
+    at_a, at_e = (project(name, v) for name, v in (("first", at_a), ("second", at_e)))
     right, left = call(
         functools.partial(order_kernel, n, rows),
         "order",

time: 23.9 us -> 23.9 us (level)
  no operation moved by 1% of the time
where the time goes in v7:
time: 23.9 us; the launch traced here: 23.6 us
  Pallas kernels  13 us (54%)
  starting transfers between devices  8.36 us (35%)
  waiting for transfers between devices  2.07 us (9%)
    pallas_call x14, Pallas kernels, call(): pl.pallas_call(kernel, out_shape=tuple(outs), in_specs=[vmem] * len(ins),...  9.85 us
    ppermute x1, starting transfers between devices, in_one_phase(): packed_a = lax.ppermute(packed, both, first)  3.09 us
    ppermute x1, starting transfers between devices, in_one_phase(): half_b = lax.ppermute(halved, both, second)  2.26 us
    ppermute x1, starting transfers between devices, in_one_phase(): w_a = lax.ppermute(weights, 'ch', chips)  1.49 us
    pallas_call x1, Pallas kernels, in_one_phase(): pl.pallas_call(functools.partial(last_kernel, n, rows), out_shape=jax.Sha...  1.08 us
    pallas_call x1, Pallas kernels, in_one_phase(): pl.pallas_call(functools.partial(constants_kernel, part), out_shape=tuple...  1.08 us
    pallas_call x1, Pallas kernels, in_one_phase(): pl.pallas_call(functools.partial(pack_kernel, n, rows), out_shape=(bf16(b...  0.96 us
    ppermute x1, waiting for transfers between devices, in_one_phase(): part_n = lax.ppermute(part, 'ch', cores)  0.92 us
  transfers between devices with their start and end apart: 9, of which 3 were waited for; matrix products, arithmetic and copies ran while one was open for 0% of the time, Pallas kernels for 34%

profile of v7, /device:TPU:0, one launch (start us, length us, event | category | flops | bytes accessed | tf_op | source)
XLA Modules:
  0.0 23.6 jit_solution(11953826881689418421)
XLA Ops:
  0.0 1.0 %pack.1.packed = bf16[800,128]{1,0:T(8,128)(2,1)S(1)} custom-call(bf16[784,128]{1,0:T(8,128)(2,1)} %bitcast.6, s32[14,56]{1,0:T(8,128)} %mask.1), custom_call_target="tpu_custom_call" | custom-call | tf_op jit(solution)/shard_map/pack/pallas_call | solution.py:409
  1.0 3.1 %collective-permute-start.4 = (bf16[800,128]{1,0:T(8,128)(2,1)S(1)}, bf16[800,128]{1,0:T(8,128)(2,1)S(1)}, u32[]{:S(2)}, u32[]{:S(2)}) collective-permute-start(bf16[800,128]{1,0:T(8,128)(2,1)S(1)} %pack.1.packed), channel_id=1, source_target_pairs={{4,0},{9,1},{6,2},{11,3},{0,4},{13,5},{2,6},{15,7},{12,8},{1,9},{1... | collective-permute-start | bytes 614408 | tf_op jit(solution)/shard_map/ppermute | solution.py:432
  4.1 1.5 %collective-permute-start.2 = (bf16[256,128]{1,0:T(8,128)(2,1)}, bf16[256,128]{1,0:T(8,128)(2,1)S(1)}, u32[]{:S(2)}, u32[]{:S(2)}) collective-permute-start(bf16[256,128]{1,0:T(8,128)(2,1)} %bitcast.7), channel_id=1, source_target_pairs={{0,2},{1,3},{2,0},{3,1},{4,6},{5,7},{6,4},{7,5},{8,10},{9,11},{10,... | collective-permute-start | bytes 196616 | tf_op jit(solution)/shard_map/ppermute | solution.py:435
  5.6 0.3 %collective-permute-start.1 = (bf16[256,128]{1,0:T(8,128)(2,1)}, bf16[256,128]{1,0:T(8,128)(2,1)S(1)}, u32[]{:S(2)}, u32[]{:S(2)}) collective-permute-start(bf16[256,128]{1,0:T(8,128)(2,1)} %bitcast.8), channel_id=1, source_target_pairs={{0,1},{1,0},{2,3},{3,2},{4,5},{5,4},{6,7},{7,6},{8,9},{9,8},{10,11... | collective-permute-start | bytes 196616 | tf_op jit(solution)/shard_map/ppermute | solution.py:434
  5.8 1.1 %constants.1 = (bf16[256,128]{1,0:T(8,128)(2,1)S(1)}, f32[2,128]{1,0:T(2,128)S(1)}, f32[2,128]{1,0:T(2,128)S(1)}, f32[2,128]{1,0:T(2,128)S(1)}, bf16[2,128,128]{...) custom-call(bf16[800,128]{1,0:T(8,128)(2,1)S(1)} %pack.1.packed, ...), custom_call_target="tpu_custom_call" | custom-call | flops 10000000 | tf_op jit(solution)/shard_map/constants/pallas_call | solution.py:418
  6.9 2.3 %collective-permute-start = (bf16[416,128]{1,0:T(8,128)(2,1)S(1)}, bf16[416,128]{1,0:T(8,128)(2,1)S(1)}, u32[]{:S(2)}, u32[]{:S(2)}) collective-permute-start(bf16[416,128]{1,0:T(8,128)(2,1)S(1)} %get-tuple-element.40), channel_id=1, source_target_pairs={{12,0},{13,1},{14,2},{15,3},{8,4},{9,5},{10,6},{11,7},{4,8},{5,9},... | collective-permute-start | bytes 319496 | tf_op jit(solution)/shard_map/ppermute | solution.py:433
  9.2 0.2 collective-permute-start.3
  9.4 0.5 %lift_own.1 = (f32[784,128]{1,0:T(8,128)S(1)}, f32[784,128]{1,0:T(8,128)S(1)}, f32[784,128]{1,0:T(8,128)S(1)}, bf16[784,128]{1,0:T(8,128)(2,1)S(1)}) custom-call(bf16[800,128]{1,0:T(8,128)(2,1)S(1)} %pack.1.packed, f32[56,128]{1,0:T(8,128)S(1)} %get-tuple-element.41.chains, f32[2,128]{1,0:T(2,128)S(1)} %get-tuple-element.42.embed, ...), custom_call_target="tpu_custom_call" | custom-call | flops 960000000 | tf_op jit(solution)/shard_map/lift_own/pallas_call | solution.py:390
  9.9 0.5 %collective-permute-done.3.w_f = bf16[256,128]{1,0:T(8,128)(2,1)S(1)} collective-permute-done((bf16[256,128]{1,0:T(8,128)(2,1)S(1)}, bf16[256,128]{1,0:T(8,128)(2,1)S(1)}, u32[]{:S(2)}, u32[]{:S(2)}) %collective-permute-start.3) | collective-permute-done | bytes 65568 | tf_op jit(solution)/shard_map/ppermute | solution.py:436
  10.5 0.3 %collective-permute-start.5 = (bf16[800,128]{1,0:T(8,128)(2,1)S(1)}, bf16[800,128]{1,0:T(8,128)(2,1)S(1)}, u32[]{:S(2)}, u32[]{:S(2)}) collective-permute-start(bf16[800,128]{1,0:T(8,128)(2,1)S(1)} %pass_first.1.packed), channel_id=1, source_target_pairs={{0,1},{1,0},{2,3},{3,2},{4,5},{5,4},{6,7},{7,6},{8,9},{9,8},{10,11... | collective-permute-start | bytes 614408 | tf_op jit(solution)/shard_map/ppermute | solution.py:457
  10.8 0.5 %project_own.1 = (f32[784,128]{1,0:T(8,128)S(1)}, f32[784,128]{1,0:T(8,128)S(1)}) custom-call(bf16[784,128]{1,0:T(8,128)(2,1)S(1)} %get-tuple-element.46.zm_ref, bf16[1024,128]{1,0:T(8,128)(2,1)S(1)} %weights.1), custom_call_target="tpu_custom_call" | custom-call | flops 720000000 | tf_op jit(solution)/shard_map/project_own/pallas_call | solution.py:390
  11.4 0.5 %lift_first.1 = (f32[784,128]{1,0:T(8,128)S(1)}, f32[784,128]{1,0:T(8,128)S(1)}, f32[784,128]{1,0:T(8,128)S(1)}, bf16[784,128]{1,0:T(8,128)(2,1)S(1)}) custom-call(bf16[800,128]{1,0:T(8,128)(2,1)S(1)} %pass_first.1.packed, f32[56,128]{1,0:T(8,128)S(1)} %get-tuple-element.41.chains, f32[2,128]{1,0:T(2,128)S(1)} %get-tuple-element.42.embed, ...), custom_call_target="tpu_custom_call" | custom-call | flops 960000000 | tf_op jit(solution)/shard_map/lift_first/pallas_call | solution.py:390
  11.9 0.4 %project_first.1 = (f32[784,128]{1,0:T(8,128)S(1)}, f32[784,128]{1,0:T(8,128)S(1)}) custom-call(bf16[784,128]{1,0:T(8,128)(2,1)S(1)} %get-tuple-element.50.zm_ref, bf16[1024,128]{1,0:T(8,128)(2,1)S(1)} %weights.1), custom_call_target="tpu_custom_call" | custom-call | flops 720000000 | tf_op jit(solution)/shard_map/project_first/pallas_call | solution.py:390
  12.3 0.4 %lift_second.1 = (f32[784,128]{1,0:T(8,128)S(1)}, f32[784,128]{1,0:T(8,128)S(1)}, f32[784,128]{1,0:T(8,128)S(1)}, bf16[784,128]{1,0:T(8,128)(2,1)S(1)}) custom-call(bf16[800,128]{1,0:T(8,128)(2,1)S(1)} %collective-permute-done.5.packed, f32[56,128]{1,0:T(8,128)S(1)} %get-tuple-element.41.chains, f32[2,128]{1,0:T(2,128)S(1)} %get-tuple-element.42.embed, ...), custom_call_target="tpu_custom_call" | custom-call | flops 960000000 | tf_op jit(solution)/shard_map/lift_second/pallas_call | solution.py:390
  12.7 0.3 %project_second.1 = (f32[784,128]{1,0:T(8,128)S(1)}, f32[784,128]{1,0:T(8,128)S(1)}) custom-call(bf16[784,128]{1,0:T(8,128)(2,1)S(1)} %get-tuple-element.52.zm_ref, bf16[1024,128]{1,0:T(8,128)(2,1)S(1)} %weights.1), custom_call_target="tpu_custom_call" | custom-call | flops 720000000 | tf_op jit(solution)/shard_map/project_second/pallas_call | solution.py:390
  13.1 0.3 %order.1 = (f32[3136,128]{1,0:T(8,128)S(1)}, f32[1176,128]{1,0:T(8,128)S(1)}) custom-call(f32[784,128]{1,0:T(8,128)S(1)} %get-tuple-element.48.left_o, f32[784,128]{1,0:T(8,128)S(1)} %get-tuple-element.51.left_a, f32[784,128]{1,0:T(8,128)S(1)} %get-tuple-element.53.left_e, f32[784,128]{1,0:T(8,128)S(1)} %get-tuple-element.54.right_o, ...), custom_call_target="tpu_custom_call" | custom-call | flops 360000000 | tf_op jit(solution)/shard_map/order/pallas_call | solution.py:390
  13.4 0.6 %collective-permute-done.value = bf16[416,128]{1,0:T(8,128)(2,1)S(1)} collective-permute-done((bf16[416,128]{1,0:T(8,128)(2,1)S(1)}, bf16[416,128]{1,0:T(8,128)(2,1)S(1)}, u32[]{:S(2)}, u32[]{:S(2)}) %collective-permute-start) | collective-permute-done | bytes 106528 | tf_op jit(solution)/shard_map/ppermute | solution.py:433
  14.1 1.7 %early.1.x_in = f32[1176,128]{1,0:T(8,128)S(1)} custom-call(f32[1176,128]{1,0:T(8,128)S(1)} %get-tuple-element.61.left_ref.left_in, f32[3136,128]{1,0:T(8,128)S(1)} %get-tuple-element.57.after.right_ref.right_in), custom_call_target="tpu_custom_call" | custom-call | flops 2400000000 | tf_op jit(solution)/shard_map/early/pallas_call | solution.py:390
  15.8 2.9 %late.1 = (f32[1568,128]{1,0:T(8,128)S(1)}, bf16[784,128]{1,0:T(8,128)(2,1)S(1)}, f32[392,128]{1,0:T(8,128)S(1)}) custom-call(bf16[416,128]{1,0:T(8,128)(2,1)S(1)} %pass_on.1.half_b, bf16[416,128]{1,0:T(8,128)(2,1)S(1)} %collective-permute-done.6.half_f, bf16[1024,128]{1,0:T(8,128)(2,1)S(1)} %weights.1, f32[56,128]{1,0:T(8,128)S(1)} %get-tuple-element.41.chains, ...), custom_call_target="tpu_custom_call" | custom-call | flops 4800000000 | tf_op jit(solution)/shard_map/late/pallas_call | solution.py:390
  18.7 0.6 %collective-permute-start.8 = (bf16[784,128]{1,0:T(8,128)(2,1)S(1)}, bf16[784,128]{1,0:T(8,128)(2,1)S(1)}, u32[]{:S(2)}, u32[]{:S(2)}) collective-permute-start(bf16[784,128]{1,0:T(8,128)(2,1)S(1)} %get-tuple-element.72.own), channel_id=1, source_target_pairs={{0,1},{1,0},{2,3},{3,2},{4,5},{5,4},{6,7},{7,6},{8,9},{9,8},{10,11... | collective-permute-start | bytes 602120 | tf_op jit(solution)/shard_map/ppermute | solution.py:483
  19.3 1.7 %incoming.1.part = bf16[784,128]{1,0:T(8,128)(2,1)S(1)} custom-call(f32[1568,128]{1,0:T(8,128)S(1)} %get-tuple-element.67.z1, f32[784,128]{1,0:T(8,128)S(1)} %get-tuple-element.68.m_o, f32[784,128]{1,0:T(8,128)S(1)} %get-tuple-element.69.m_a, f32[784,128]{1,0:T(8,128)S(1)} %get-tuple-element.70.m_e, f32[392,128]{1,0:T(8,128)S(1)} %get-tuple-element.71.m_f, ...), custom_call_target="tpu_custom_call" | custom-call | flops 3600000000 | tf_op jit(solution)/shard_map/incoming/pallas_call | solution.py:390
  21.0 0.5 %gate.1 = (f32[784,128]{1,0:T(8,128)S(1)}, f32[784,128]{1,0:T(8,128)S(1)}) custom-call(bf16[784,128]{1,0:T(8,128)(2,1)S(1)} %get-tuple-element.72.own, bf16[784,128]{1,0:T(8,128)(2,1)S(1)} %collective-permute-done.8.received, f32[2,128]{1,0:T(2,128)S(1)} %get-tuple-element.43.in_gain, f32[2,128]{1,0:T(2,128)S(1)} %get-tuple-element.44.in_bias, ...), custom_call_target="tpu_custom_call" | custom-call | flops 1200000000 | tf_op jit(solution)/shard_map/gate/pallas_call | solution.py:390
  21.6 0.9 %collective-permute-done.7.received = bf16[784,128]{1,0:T(8,128)(2,1)S(1)} collective-permute-done((bf16[784,128]{1,0:T(8,128)(2,1)S(1)}, bf16[784,128]{1,0:T(8,128)(2,1)S(1)}, u32[]{:S(2)}, u32[]{:S(2)}) %collective-permute-start.7) | collective-permute-done | bytes 200736 | tf_op jit(solution)/shard_map/ppermute | solution.py:492
  22.5 1.1 %last.1 = bf16[784,128]{1,0:T(8,128)(2,1)} custom-call(bf16[784,128]{1,0:T(8,128)(2,1)S(1)} %incoming.1.part, bf16[784,128]{1,0:T(8,128)(2,1)S(1)} %collective-permute-done.7.received, f32[784,128]{1,0:T(8,128)S(1)} %get-tuple-element.73.z_ref, f32[784,128]{1,0:T(8,128)S(1)} %get-tuple-element.74.g_ref, f32[2,128]{1,0:T(2,128)S(1)} %get-tuple-element.58.out_gain, ...), custom_call_target="tpu_custom_call" | custom-call | flops 1000000000 | tf_op jit(solution)/shard_map/last/pallas_call | solution.py:494
  (11 shorter events, 0.3 us)
Async XLA Ops:
  1.0 9.5 %collective-permute-start.4 = (bf16[800,128]{1,0:T(8,128)(2,1)S(1)}, bf16[800,128]{1,0:T(8,128)(2,1)S(1)}, u32[]{:S(2)}, u32[]{:S(2)}) collective-permute-start(bf16[800,128]{1,0:T(8,128)(2,1)S(1)} %pack.1.packed), channel_id=1, source_target_pairs={{4,0},{9,1},{6,2},{11,3},{0,4},{13,5},{2,6},{15,7},{12,8},{1,9},{1... | collective-permute-start | bytes 614408 | tf_op jit(solution)/shard_map/ppermute | solution.py:432
  4.1 5.1 %collective-permute-start.2 = (bf16[256,128]{1,0:T(8,128)(2,1)}, bf16[256,128]{1,0:T(8,128)(2,1)S(1)}, u32[]{:S(2)}, u32[]{:S(2)}) collective-permute-start(bf16[256,128]{1,0:T(8,128)(2,1)} %bitcast.7), channel_id=1, source_target_pairs={{0,2},{1,3},{2,0},{3,1},{4,6},{5,7},{6,4},{7,5},{8,10},{9,11},{10,... | collective-permute-start | bytes 196616 | tf_op jit(solution)/shard_map/ppermute | solution.py:435
  5.6 4.4 %collective-permute-start.1 = (bf16[256,128]{1,0:T(8,128)(2,1)}, bf16[256,128]{1,0:T(8,128)(2,1)S(1)}, u32[]{:S(2)}, u32[]{:S(2)}) collective-permute-start(bf16[256,128]{1,0:T(8,128)(2,1)} %bitcast.8), channel_id=1, source_target_pairs={{0,1},{1,0},{2,3},{3,2},{4,5},{5,4},{6,7},{7,6},{8,9},{9,8},{10,11... | collective-permute-start | bytes 196616 | tf_op jit(solution)/shard_map/ppermute | solution.py:434
  6.9 7.1 %collective-permute-start = (bf16[416,128]{1,0:T(8,128)(2,1)S(1)}, bf16[416,128]{1,0:T(8,128)(2,1)S(1)}, u32[]{:S(2)}, u32[]{:S(2)}) collective-permute-start(bf16[416,128]{1,0:T(8,128)(2,1)S(1)} %get-tuple-element.40), channel_id=1, source_target_pairs={{12,0},{13,1},{14,2},{15,3},{8,4},{9,5},{10,6},{11,7},{4,8},{5,9},... | collective-permute-start | bytes 319496 | tf_op jit(solution)/shard_map/ppermute | solution.py:433
  9.2 1.3 %collective-permute-start.3 = (bf16[256,128]{1,0:T(8,128)(2,1)S(1)}, bf16[256,128]{1,0:T(8,128)(2,1)S(1)}, u32[]{:S(2)}, u32[]{:S(2)}) collective-permute-start(bf16[256,128]{1,0:T(8,128)(2,1)S(1)} %collective-permute-done.2.w_a), channel_id=1, source_target_pairs={{0,1},{1,0},{2,3},{3,2},{4,5},{5,4},{6,7},{7,6},{8,9},{9,8},{10,11... | collective-permute-start | bytes 196616 | tf_op jit(solution)/shard_map/ppermute | solution.py:436
  10.5 1.7 %collective-permute-start.5 = (bf16[800,128]{1,0:T(8,128)(2,1)S(1)}, bf16[800,128]{1,0:T(8,128)(2,1)S(1)}, u32[]{:S(2)}, u32[]{:S(2)}) collective-permute-start(bf16[800,128]{1,0:T(8,128)(2,1)S(1)} %pass_first.1.packed), channel_id=1, source_target_pairs={{0,1},{1,0},{2,3},{3,2},{4,5},{5,4},{6,7},{7,6},{8,9},{9,8},{10,11... | collective-permute-start | bytes 614408 | tf_op jit(solution)/shard_map/ppermute | solution.py:457
  14.0 1.8 %collective-permute-start.6 = (bf16[416,128]{1,0:T(8,128)(2,1)S(1)}, bf16[416,128]{1,0:T(8,128)(2,1)S(1)}, u32[]{:S(2)}, u32[]{:S(2)}) collective-permute-start(bf16[416,128]{1,0:T(8,128)(2,1)S(1)} %pass_on.1.half_b), channel_id=1, source_target_pairs={{0,1},{1,0},{2,3},{3,2},{4,5},{5,4},{6,7},{7,6},{8,9},{9,8},{10,11... | collective-permute-start | bytes 319496 | tf_op jit(solution)/shard_map/ppermute | solution.py:469
  18.7 2.3 %collective-permute-start.8 = (bf16[784,128]{1,0:T(8,128)(2,1)S(1)}, bf16[784,128]{1,0:T(8,128)(2,1)S(1)}, u32[]{:S(2)}, u32[]{:S(2)}) collective-permute-start(bf16[784,128]{1,0:T(8,128)(2,1)S(1)} %get-tuple-element.72.own), channel_id=1, source_target_pairs={{0,1},{1,0},{2,3},{3,2},{4,5},{5,4},{6,7},{7,6},{8,9},{9,8},{10,11... | collective-permute-start | bytes 602120 | tf_op jit(solution)/shard_map/ppermute | solution.py:483
  21.0 1.5 %collective-permute-start.7 = (bf16[784,128]{1,0:T(8,128)(2,1)S(1)}, bf16[784,128]{1,0:T(8,128)(2,1)S(1)}, u32[]{:S(2)}, u32[]{:S(2)}) collective-permute-start(bf16[784,128]{1,0:T(8,128)(2,1)S(1)} %incoming.1.part), channel_id=1, source_target_pairs={{0,1},{1,0},{2,3},{3,2},{4,5},{5,4},{6,7},{7,6},{8,9},{9,8},{10,11... | collective-permute-start | bytes 602120 | tf_op jit(solution)/shard_map/ppermute | solution.py:492
